TPU v7x, 512 devices: a whole 4x4x16 slice. The times are simulated.
512 devices in a mesh: sx: 32 (over z, core), sy: 16 (over y, x).
Axes of the slice: x: 4, y: 4, z: 16, core: 2. Of those that a mesh axis runs over, the one named last changes fastest.
Arguments:
- queries: bfloat16 [512, 4096], P(('sx', 'sy')), may hold values from -6 to 6
- keys: bfloat16 [262144, 1024], P(('sx', 'sy')), may hold values from -6 to 6
- values: bfloat16 [262144, 1024], P(('sx', 'sy')), may hold values from -6 to 6
- block_ids: int32 [512, 16], replicated, may hold values from 0 to 63, as said below
Outputs:
- attended: bfloat16 [512, 4096], P(('sx', 'sy'))
Inputs may be any that keep to these rules, and one draw needn't show every extreme that they name: `block_ids`: each row names 16 different blocks. Among the 32 rows stored on the devices of one sy index, every block is named by exactly 8 rows.
All inputs are finite; a program needn't handle non-finite values.
Results may differ from a plain program's by a relative error of at most 0.0046.
Values may be sent and summed in bfloat16 or wider, within the bound.
No kernel may reach another device: no remote copies, remote signals or barrier semaphores. Data moves between devices by JAX's collectives and lax.ppermute only.
A program may use at most 64 MiB of HBM per device.

v0:
```python
import jax
import jax.numpy as jnp
from jax import lax
from jax.sharding import PartitionSpec as P

QUERY_HEADS = 32
KEY_HEADS = 8
HEAD_WIDTH = 128
BLOCK = 4096
QUERY_PER_KEY = 4


def column_rows(block_ids, block_list, column, count_x, count_second, rows_dev, column_scores):
    named_rows = jnp.any(block_ids[None, :, :] == block_list[:, None, None], axis=2)
    named_rows = named_rows.reshape(block_list.shape[0], count_x, count_second, rows_dev)
    own_column = jnp.take(named_rows, column, axis=2).reshape(
        block_list.shape[0], count_x * rows_dev
    )
    col_width = count_x * rows_dev
    ranked = jnp.where(own_column, 0, col_width).astype(jnp.int32) + jnp.arange(
        col_width, dtype=jnp.int32
    )
    return jnp.argsort(ranked, axis=1)[:, :column_scores]


def every_column(block_ids, my_block, count_x, count_second, rows_dev, column_scores):
    named_rows = jnp.any(block_ids == my_block, axis=1)
    named_rows = named_rows.reshape(count_x, count_second, rows_dev).transpose(1, 0, 2)
    col_width = count_x * rows_dev
    named_rows = named_rows.reshape(count_second, col_width)
    ranked = jnp.where(named_rows, 0, col_width).astype(jnp.int32) + jnp.arange(
        col_width, dtype=jnp.int32
    )
    return jnp.argsort(ranked, axis=1)[:, :column_scores]


def head_parts(asked_rows, keys, values, kv_head):
    score_scale = HEAD_WIDTH ** (-0.5)
    query_part = lax.dynamic_slice_in_dim(
        asked_rows, kv_head * QUERY_PER_KEY * HEAD_WIDTH, QUERY_PER_KEY * HEAD_WIDTH, 1
    )
    query_part = query_part.reshape(asked_rows.shape[0] * QUERY_PER_KEY, HEAD_WIDTH)
    key_part = lax.dynamic_slice_in_dim(keys, kv_head * HEAD_WIDTH, HEAD_WIDTH, 1)
    value_part = lax.dynamic_slice_in_dim(values, kv_head * HEAD_WIDTH, HEAD_WIDTH, 1)
    score = (
        jnp.einsum("qd,sd->qs", query_part, key_part, preferred_element_type=jnp.float32)
        * score_scale
    )
    highest_score = jnp.max(score, axis=1)
    weights = jnp.exp(score - highest_score[:, None])
    device_total = jnp.sum(weights, axis=1)
    weighted_numer = jnp.dot(
        weights.astype(jnp.bfloat16), value_part, preferred_element_type=jnp.float32
    )
    return (highest_score, device_total, weighted_numer)


def per_device(queries, keys, values, block_ids):
    count_x = lax.axis_size("sx")
    count_second = lax.axis_size("sy")
    index_x = lax.axis_index("sx")
    index_y = lax.axis_index("sy")
    rows_dev = queries.shape[0]
    feature = queries.shape[1]
    slab_len = keys.shape[0]
    picks = block_ids.shape[1]
    col_width = count_x * rows_dev
    block_count = count_x * count_second * slab_len // BLOCK
    column_scores = col_width * picks // block_count
    block_slots = count_second * column_scores
    neighbours = (
        (index_x * count_second + jnp.arange(count_second, dtype=jnp.int32)) * slab_len // BLOCK
    )
    incoming = column_rows(
        block_ids, neighbours, index_y, count_x, count_second, rows_dev, column_scores
    )
    my_block = (index_x * count_second + index_y) * slab_len // BLOCK
    everyone = lax.all_gather(queries, ("sx", "sy"), axis=0, tiled=True)
    mine_rows = every_column(block_ids, my_block, count_x, count_second, rows_dev, column_scores)
    column_ids = jnp.arange(count_second, dtype=jnp.int32)[:, None]
    row_ids = (
        mine_rows // rows_dev * (count_second * rows_dev)
        + column_ids * rows_dev
        + mine_rows % rows_dev
    )
    asked_rows = everyone[row_ids.reshape(-1)]

    def single_head(kv_head):
        return head_parts(asked_rows, keys, values, kv_head)

    highest_score, device_total, weighted_numer = lax.map(
        single_head, jnp.arange(KEY_HEADS, dtype=jnp.int32)
    )
    highest_score = (
        highest_score.reshape(KEY_HEADS, block_slots, QUERY_PER_KEY)
        .transpose(1, 0, 2)
        .reshape(count_second, column_scores, QUERY_HEADS)
    )
    device_total = (
        device_total.reshape(KEY_HEADS, block_slots, QUERY_PER_KEY)
        .transpose(1, 0, 2)
        .reshape(count_second, column_scores, QUERY_HEADS)
    )
    weighted_numer = (
        weighted_numer.reshape(KEY_HEADS, block_slots, QUERY_PER_KEY, HEAD_WIDTH)
        .transpose(1, 0, 2, 3)
        .reshape(count_second, column_scores, feature)
    )
    got_numer, got_max, got_total = (
        lax.all_to_all(weighted_numer, "sy", split_axis=0, concat_axis=0, tiled=True),
        lax.all_to_all(highest_score, "sy", split_axis=0, concat_axis=0, tiled=True),
        lax.all_to_all(device_total, "sy", split_axis=0, concat_axis=0, tiled=True),
    )
    got_numer = got_numer.reshape(block_slots, QUERY_HEADS, HEAD_WIDTH)
    got_max = got_max.reshape(block_slots, QUERY_HEADS)
    got_total = got_total.reshape(block_slots, QUERY_HEADS)
    slot_rows = incoming.reshape(-1)
    held_slots = slot_rows.shape[0]
    onehot = (slot_rows[:, None] == jnp.arange(col_width, dtype=jnp.int32)[None, :]).astype(
        jnp.float32
    )
    col_max = jnp.max(jnp.where(onehot[:, :, None] > 0.0, got_max[:, None, :], -1e30), axis=0)
    row_max = lax.pmax(col_max, "sx")
    factor = jnp.exp(got_max - row_max[slot_rows])
    scaled = (got_numer * factor[..., None]).reshape(held_slots, feature)
    numer_col = jnp.einsum("sk,sf->kf", onehot, scaled, precision=lax.Precision.HIGHEST)
    total_col = jnp.einsum("sk,sf->kf", onehot, got_total * factor, precision=lax.Precision.HIGHEST)
    numer_mine, total_mine = (
        lax.psum_scatter(numer_col, "sx", scatter_dimension=0, tiled=True),
        lax.psum_scatter(total_col, "sx", scatter_dimension=0, tiled=True),
    )
    attended = numer_mine.reshape(rows_dev, QUERY_HEADS, HEAD_WIDTH) / total_mine[..., None]
    return attended.reshape(rows_dev, feature).astype(jnp.bfloat16)


def solution(mesh):
    return jax.shard_map(
        per_device,
        mesh=mesh,
        in_specs=(P(("sx", "sy"), None), P(("sx", "sy"), None), P(("sx", "sy"), None), P()),
        out_specs=P(("sx", "sy"), None),
        check_vma=False,
    )
```

profile of v0, /device:TPU:1, one launch (start us, length us, event | category | flops | bytes accessed | tf_op | source)
XLA Modules:
  0.0 632.7 jit_solution(4014194738744815740)
XLA Ops:
  9.2 220.2 %all-gather.3.cloned.1.call-done = bf16[512,1,4096]{2,1,0:T(2,128)(2,1)} async-done(((bf16[1,1,4096]{2,1,0:T(2,128)(2,1)}), bf16[512,1,4096]{2,1,0:T(2,128)(2,1)}) %all-gather.3.cloned.1.call-update) | async-done | bytes 4194320 | tf_op jit(solution)/shard_map/all_gather | solution.py:78
  229.4 10.1 %copy.74 = bf16[512,1,4096]{2,0,1:T(8,128)(2,1)} copy(bf16[512,1,4096]{2,1,0:T(2,128)(2,1)} %all-gather.3.cloned.1.call-done) | data formatting | bytes 8388608
  239.5 4.9 gather_fusion
  244.5 44.1 %while.17 = (s32[]{:T(128)}, f32[8,512]{1,0:T(8,128)S(1)}, f32[8,512]{1,0:T(8,128)S(1)}, f32[8,512,128]{2,1,0:T(8,128)}, s32[8]{0:T(128)S(1)}, /*index=5*/bf16[1...) while((s32[]{:T(128)}, f32[8,512]{1,0:T(8,128)S(1)}, ...), condition=%wide.region_7.8_spmd, body=%wide.region_4.7_spmd.sunk | while | flops 135789568 | bytes 4342029 | solution.py:91
  246.5 1.2 fusion.30
  248.1 2.0 fusion.32
  252.0 1.2 fusion.30
  253.6 2.0 fusion.32
  257.6 1.2 fusion.30
  259.1 2.0 fusion.32
  263.1 1.2 fusion.30
  264.6 2.0 fusion.32
  270.2 1.9 fusion.32
  274.1 1.2 fusion.30
  275.7 1.9 fusion.32
  279.6 1.2 fusion.30
  281.2 1.9 fusion.32
  285.1 1.2 fusion.30
  286.7 2.0 fusion.32
  289.9 5.1 all-to-all-start.1
  296.3 5.2 all-to-all-done.1
  301.4 3.5 all-to-all-start.2
  304.9 2.2 copy.75
  307.1 1.9 reshape.205
  309.0 2.3 all-to-all-done.2
  311.3 4.5 all-to-all-start
  317.9 1.3 dynamic-slice.4
  321.6 90.0 %pmax.7 = f32[32,32]{1,0:T(8,128)S(1)} all-reduce(f32[32,32]{1,0:T(8,128)S(1)} %select_reduce_fusion), channel_id=1, replica_groups=mesh['sx'=32,'sy'=16] {'sx'}, use_global_device_ids=true, to_apply=%region_9.10 | all-reduce | flops 1024 | bytes 8192 | tf_op jit(solution)/shard_map/pmax | solution.py:123
  412.9 2.9 fusion.9
  416.0 90.1 %all-reduce.1 = f32[32,32]{1,0:T(8,128)S(1)} all-reduce(f32[32,32]{1,0:T(8,128)S(1)} %fusion.12), channel_id=3, replica_groups=mesh['sx'=32,'sy'=16] {'sx'}, use_global_device_ids=true, to_apply=%region_11.12.clone | all-reduce | flops 1024 | bytes 8192
  506.7 116.9 %all-reduce.4.cloned.1.call-done = f32[32,4096]{1,0:T(8,128)} async-done(((f32[32,4096]{1,0:T(8,128)}), f32[32,4096]{1,0:T(8,128)}) %all-reduce.4.cloned.1.call-update) | async-done | bytes 524304
  623.7 2.2 fusion.13
  (109 shorter events, 20.8 us)
Async XLA Ops:
  6.5 222.9 %all-gather.3.cloned.1.call-start = ((), (), s32[]{:S(2)}) async-start(), calls=%async_computation.3 | async-start | bytes 8404992 | tf_op jit(solution)/shard_map/all_gather | solution.py:78
  289.9 11.5 %all-to-all-start.1 = ((f32[16,1,256]{2,1,0:T(1,128)}), f32[16,1,256]{2,1,0:T(1,128)S(1)}, u32[]{:S(2)}, u32[]{:S(2)}) async-start(f32[16,1,256]{2,1,0:T(1,128)} %reshape.280), calls=%async_computation.1 | async-start | bytes 32768 | tf_op jit(solution)/shard_map/all_to_all | solution.py:111
  301.4 9.9 %all-to-all-start.2 = ((f32[16,1,256]{2,1,0:T(1,128)}), f32[16,1,256]{2,1,0:T(1,128)S(1)}, u32[]{:S(2)}, u32[]{:S(2)}) async-start(f32[16,1,256]{2,1,0:T(1,128)} %reshape.282), calls=%async_computation.2 | async-start | bytes 32768 | tf_op jit(solution)/shard_map/all_to_all | solution.py:112
  309.0 7.0 %copy-start = (s32[512,16]{0,1:T(8,128)S(1)}, s32[512,16]{0,1:T(8,128)}, u32[]{:S(2)}) copy-start(s32[512,16]{0,1:T(8,128)} %param.9) | copy-start | bytes 98308
  311.3 101.0 %all-to-all-start = ((f32[16,8,4096]{2,1,0:T(8,128)}), f32[16,8,4096]{2,1,0:T(8,128)S(1)}, u32[]{:S(2)}, u32[]{:S(2)}) async-start(f32[16,8,4096]{2,1,0:T(8,128)} %reshape.205), calls=%async_computation | async-start | bytes 4194304 | tf_op jit(solution)/shard_map/all_to_all | solution.py:110
  315.8 307.8 %all-reduce.4.cloned.1.call-start = ((), (), s32[]{:S(2)}) async-start(), calls=%async_computation.4 | async-start | bytes 1048576
Sparse Core Ops, SparseCore 0:
  11.9 217.4 all-gather.2
  415.9 207.6 all-reduce.3
where the time goes:
time: 634 us; the launch traced here: 633 us
  waiting for transfers between devices  345 us (54%)
  blocking collectives  180 us (28%)
  local copies, waits for them, and re-layouts  33 us (5%)
  matrix products  28.5 us (4%)
  between operations  13.7 us (2%)
  starting transfers between devices  13.2 us (2%)
  loops' own time  10.7 us (2%)
  other arithmetic  8.12 us (1%)
    all_gather x1, waiting for transfers between devices, per_device(): everyone = lax.all_gather(queries, ('sx', 'sy'), axis=0, tiled=True)  220 us
    unnamed x3, waiting for transfers between devices  118 us
    unnamed x1, blocking collectives  90.1 us
    pmax x1, blocking collectives, per_device(): row_max = lax.pmax(col_max, 'sx')  90 us
    dot_general x8, matrix products, head_parts(): jnp.dot(weights.astype(jnp.bfloat16), value_part, preferred_element_type=...  15.6 us
    unnamed x8, local copies, waits for them, and re-layouts  12.9 us
  transfers between devices with their start and end apart: 5, of which 4 were waited for; matrix products, arithmetic and copies ran while one was open for 2% of the time, Pallas kernels for 0%

commit v1 on v0

v1 whole, which is shorter than its diff:
```python
import functools

import jax
import jax.numpy as jnp
from jax import lax
from jax.experimental import pallas as pl
from jax.experimental.pallas import tpu as pltpu
from jax.sharding import PartitionSpec as P

QUERY_HEADS = 32
KEY_HEADS = 8
HEAD_WIDTH = 128
BLOCK = 4096
QUERY_PER_KEY = 4
LOG2E = 1.4426950408889634
NEVER = -1e30

HG = 16
FEAT = 256
SLOTS = 8
STAT = 128


def pieces(x):
    hi = x.astype(jnp.bfloat16)
    rest = x - hi.astype(jnp.float32)
    mid = rest.astype(jnp.bfloat16)
    lo = (rest - mid.astype(jnp.float32)).astype(jnp.bfloat16)
    return hi, mid, lo


def slot_onehot(pos, rows, dtype):
    shape = (HG * SLOTS, rows * HG)
    r = lax.broadcasted_iota(jnp.int32, shape, 0)
    c = lax.broadcasted_iota(jnp.int32, shape, 1)
    hit = (pos == r % SLOTS) & (r // SLOTS == c % HG)
    return jnp.where(hit, 1.0, 0.0).astype(dtype)


def select_kernel(pos_ref, q_ref, out_ref):
    rows = q_ref.shape[0] // HG
    q = q_ref[...]
    for p in range(2):
        hot = slot_onehot(pos_ref[p : p + 1, :], rows, jnp.bfloat16)
        picked = jnp.dot(hot, q, preferred_element_type=jnp.float32).astype(jnp.bfloat16)
        for s in range(8):
            out_ref[p * 8 + s] = picked


def attend_kernel(x_ref, k_ref, v_ref, y_ref):
    scale = HEAD_WIDTH ** (-0.5) * LOG2E
    cols = x_ref.shape[0]
    rows = cols * HG
    lane = lax.broadcasted_iota(jnp.int32, (rows, HEAD_WIDTH), 1)
    stats = jnp.zeros((rows, HEAD_WIDTH), jnp.float32)
    for h in range(KEY_HEADS):
        k = k_ref[:, h * HEAD_WIDTH : (h + 1) * HEAD_WIDTH]
        v = v_ref[:, h * HEAD_WIDTH : (h + 1) * HEAD_WIDTH]
        for gl in range(2):
            q = x_ref[:, h * HG : (h + 1) * HG, gl * HEAD_WIDTH : (gl + 1) * HEAD_WIDTH]
            q = q.reshape(rows, HEAD_WIDTH)
            s = lax.dot_general(q, k, (((1,), (1,)), ((), ())), preferred_element_type=jnp.float32)
            m = jnp.max(s, axis=1, keepdims=True)
            w = jnp.exp2((s - m) * scale)
            total = jnp.sum(w, axis=1, keepdims=True)
            o = jnp.dot(w.astype(jnp.bfloat16), v, preferred_element_type=jnp.float32)
            o = (o / total).astype(jnp.bfloat16).reshape(cols, HG, HEAD_WIDTH)
            y_ref[:, h * HG : (h + 1) * HG, gl * HEAD_WIDTH : (gl + 1) * HEAD_WIDTH] = o
            stats = jnp.where(lane == h * 2 + gl, m * scale + jnp.log2(total), stats)
    hi, mid, lo = pieces(stats)
    base = KEY_HEADS * HG
    both = hi.astype(jnp.float32) + pltpu.roll(mid.astype(jnp.float32), 16, 1)
    y_ref[:, base : base + HG, :HEAD_WIDTH] = both.astype(jnp.bfloat16).reshape(cols, HG, HEAD_WIDTH)
    y_ref[:, base : base + HG, HEAD_WIDTH:] = lo.reshape(cols, HG, HEAD_WIDTH)


def merge_kernel(pos_ref, y_ref, out_ref):
    rows = pos_ref.shape[1] // HG
    base = KEY_HEADS * HG
    lane = lax.broadcasted_iota(jnp.int32, (HG, HEAD_WIDTH), 1)
    dense, lse = [], []
    for p in range(2):
        stat = []
        for s in range(8):
            first = y_ref[p * 8 + s, base : base + HG, :HEAD_WIDTH].astype(jnp.float32)
            lo = y_ref[p * 8 + s, base : base + HG, HEAD_WIDTH:].astype(jnp.float32)
            mid = pltpu.roll(first, HEAD_WIDTH - 16, 1)
            stat.append(jnp.where(lane < 16, first + (mid + lo), 0.0))
        top = functools.reduce(jnp.maximum, stat)
        weight = [jnp.exp2(x - top) for x in stat]
        total = functools.reduce(jnp.add, weight)
        inverse = 1.0 / total
        weight = [w * inverse for w in weight]
        block_lse = top + jnp.log2(total)
        heads = []
        for h in range(KEY_HEADS):
            halves = []
            for gl in range(2):
                at = h * 2 + gl
                acc = None
                for s in range(8):
                    x = y_ref[p * 8 + s, h * HG : (h + 1) * HG, gl * HEAD_WIDTH : (gl + 1) * HEAD_WIDTH]
                    x = x.astype(jnp.float32) * weight[s][:, at : at + 1]
                    acc = x if acc is None else acc + x
                halves.append(acc)
            heads.append(jnp.concatenate(halves, axis=1))
        block_out = jnp.concatenate(heads, axis=0)
        hot = slot_onehot(pos_ref[p : p + 1, :], rows, jnp.float32)
        flip = (((0,), (0,)), ((), ()))
        dense.append(
            lax.dot_general(hot, block_out, flip, precision=lax.Precision.HIGHEST, preferred_element_type=jnp.float32)
        )
        tall = jnp.concatenate([block_lse] * KEY_HEADS, axis=0)
        r = lax.broadcasted_iota(jnp.int32, tall.shape, 0)
        c = lax.broadcasted_iota(jnp.int32, tall.shape, 1)
        tall = jnp.where(c == 16, 1.0, jnp.where(c // 2 == r // HG, tall, 0.0))
        moved = lax.dot_general(
            hot, tall, flip, precision=lax.Precision.HIGHEST, preferred_element_type=jnp.float32
        )
        wide = lax.broadcasted_iota(jnp.int32, moved.shape, 1)
        named = moved[:, 16:17] > 0.5
        lse.append(
            [
                jnp.where(
                    named,
                    jnp.sum(jnp.where((wide < 16) & (wide % 2 == gl), moved, 0.0), axis=1, keepdims=True),
                    NEVER,
                )
                for gl in range(2)
            ]
        )
    combine_two(dense, lse, out_ref, rows)


def combine_two(data, lse, out_ref, rows):
    shape = out_ref.shape[:-1]
    ends = []
    for gl in range(2):
        a, b = lse[0][gl], lse[1][gl]
        top = jnp.maximum(a, b)
        wa, wb = jnp.exp2(a - top), jnp.exp2(b - top)
        total = wa + wb
        inverse = 1.0 / total
        lanes = slice(gl * HEAD_WIDTH, (gl + 1) * HEAD_WIDTH)
        mixed = data[0][:, lanes] * (wa * inverse) + data[1][:, lanes] * (wb * inverse)
        out_ref[..., lanes] = mixed.reshape(*shape, HEAD_WIDTH).astype(out_ref.dtype)
        ends.append(top + jnp.log2(total))
    lane = lax.broadcasted_iota(jnp.int32, (mixed.shape[0], STAT), 1)
    if out_ref.dtype == jnp.float32:
        stat = jnp.where(lane == 0, ends[0], jnp.where(lane == 1, ends[1], 0.0))
    else:
        stat = jnp.zeros(lane.shape, jnp.float32)
        for gl in range(2):
            for k, piece in enumerate(pieces(ends[gl])):
                stat = jnp.where(lane == gl * 3 + k, piece.astype(jnp.float32), stat)
    out_ref[..., FEAT:] = stat.reshape(*shape, STAT).astype(out_ref.dtype)


def pair_kernel(a_ref, out_ref):
    rows = a_ref.shape[1]
    data = [a_ref[c, :, :FEAT] for c in range(2)]
    lse = [[a_ref[c, :, FEAT + gl : FEAT + gl + 1] for gl in range(2)] for c in range(2)]
    combine_two(data, lse, out_ref, rows)


def last_kernel(a_ref, out_ref):
    for gl in range(2):
        lse = functools.reduce(
            jnp.add, [a_ref[:, :, FEAT + gl * 3 + k : FEAT + gl * 3 + k + 1].astype(jnp.float32) for k in range(3)]
        )
        weight = jnp.exp2(lse - jnp.max(lse, axis=0, keepdims=True))
        total = jnp.sum(weight, axis=0)
        lanes = slice(gl * HEAD_WIDTH, (gl + 1) * HEAD_WIDTH)
        mixed = jnp.sum(a_ref[:, :, lanes].astype(jnp.float32) * weight, axis=0) / total
        out_ref[:, lanes] = mixed.astype(jnp.bfloat16)


def call(kernel, shape, dtype, name, *args):
    return pl.pallas_call(
        kernel,
        out_shape=jax.ShapeDtypeStruct(shape, dtype),
        in_specs=[pl.BlockSpec(memory_space=pltpu.VMEM)] * len(args),
        out_specs=pl.BlockSpec(memory_space=pltpu.VMEM),
        compiler_params=pltpu.CompilerParams(vmem_limit_bytes=32 * 1024 * 1024),
        name=name,
    )(*args)


def per_device(queries, keys, values, block_ids):
    count_x = lax.axis_size("sx")
    count_y = lax.axis_size("sy")
    index_x = lax.axis_index("sx")
    index_y = lax.axis_index("sy")
    count_z = count_x // 2
    cores = [[2 * z, 2 * z + 1] for z in range(count_z)]
    along_z = [[2 * z + c for z in range(count_z)] for c in range(2)]

    def exchange(x, axis, groups=None):
        return lax.all_to_all(x, axis, split_axis=0, concat_axis=0, tiled=True, axis_index_groups=groups)

    column = lax.dynamic_index_in_dim(block_ids.reshape(count_x, count_y, -1), index_y, 1, keepdims=False)
    wanted = index_x * 2 + jnp.arange(2, dtype=jnp.int32)
    named = jnp.any(column[None] == wanted[:, None, None], axis=2)
    before = jnp.arange(count_x)[None, :] < jnp.arange(count_x)[:, None]
    rank = jnp.sum((named[:, None, :] & before[None]).astype(jnp.int32), axis=2)
    pos = jnp.where(named, rank, -1)
    pos = pos.reshape(2, count_z, 2).transpose(0, 2, 1)
    pos = jnp.repeat(pos.reshape(2, count_x), HG, axis=1)

    own = queries.reshape(1, HG, FEAT)
    got = exchange(jnp.broadcast_to(own, (count_z, HG, FEAT)), "sx", along_z)
    got = got.reshape(1, count_z * HG, FEAT)
    got = exchange(jnp.broadcast_to(got, (2, count_z * HG, FEAT)), "sx", cores)
    q_column = got.reshape(count_x * HG, FEAT)
    asked = call(select_kernel, (count_y, HG * SLOTS, FEAT), jnp.bfloat16, "select", pos, q_column)
    asked = exchange(asked, "sy")
    slab = call(attend_kernel, (count_y, HG * SLOTS + HG, FEAT), jnp.bfloat16, "attend", asked, keys, values)
    slab = exchange(slab, "sy")
    dense = call(merge_kernel, (2, count_z * HG, FEAT + STAT), jnp.float32, "merge", pos, slab)
    dense = exchange(dense, "sx", cores)
    chip = call(pair_kernel, (count_z, HG, FEAT + STAT), jnp.bfloat16, "pair", dense)
    chip = exchange(chip, "sx", along_z)
    out = call(last_kernel, (HG, FEAT), jnp.bfloat16, "last", chip)
    return out.reshape(1, HG * FEAT)


def solution(mesh):
    return jax.shard_map(
        per_device,
        mesh=mesh,
        in_specs=(P(("sx", "sy"), None), P(("sx", "sy"), None), P(("sx", "sy"), None), P()),
        out_specs=P(("sx", "sy"), None),
        check_vma=False,
    )
```

time: 634 us -> 115 us (0.18)
  the two profiles are of different devices: /device:TPU:1 before, /device:TPU:32 now
where the time goes in v1:
time: 115 us; the launch traced here: 114 us
  blocking collectives  74.1 us (64%)
  starting transfers between devices  15.2 us (13%)
  waiting for transfers between devices  12.2 us (11%)
  Pallas kernels  8.79 us (8%)
  local copies, waits for them, and re-layouts  3.08 us (3%)
    all_to_all x5, blocking collectives, exchange(): lax.all_to_all(x, axis, split_axis=0, concat_axis=0, tiled=True, axis_ind...  74.1 us
    all_to_all x1, starting transfers between devices, exchange(): lax.all_to_all(x, axis, split_axis=0, concat_axis=0, tiled=True, axis_ind...  15.2 us
    all_to_all x1, waiting for transfers between devices, exchange(): lax.all_to_all(x, axis, split_axis=0, concat_axis=0, tiled=True, axis_ind...  12.2 us
    pallas_call x5, Pallas kernels, call(): pl.pallas_call(kernel, out_shape=jax.ShapeDtypeStruct(shape, dtype), in_s...  8.79 us
  transfers between devices with their start and end apart: 1, of which 1 were waited for; matrix products, arithmetic and copies ran while one was open for 2% of the time, Pallas kernels for 0%

profile of v1, /device:TPU:32, one launch (start us, length us, event | category | flops | bytes accessed | tf_op | source)
XLA Modules:
  0.0 114.5 jit_solution(15196410935738656906)
XLA Ops:
  0.0 0.8 reduce.1
  0.8 0.6 broadcast_in_dim.30
  1.4 15.2 %all-to-all-start = ((bf16[16,16,256]{2,1,0:T(8,128)(2,1)}), bf16[16,16,256]{2,1,0:T(8,128)(2,1)S(1)}, u32[]{:S(2)}, u32[]{:S(2)}) async-start(bf16[16,16,256]{2,1,0:T(8,128)(2,1)} %broadcast_in_dim.30), calls=%async_computation | async-start | bytes 262144 | tf_op jit(solution)/shard_map/all_to_all | solution.py:199
  16.7 0.9 reshape.43
  17.6 0.5 dynamic-slice_reduce_fusion
  18.0 0.1 compare_reduce_fusion
  18.1 0.1 convert_reduce_fusion
  18.2 0.1 select_n.14
  18.3 0.1 copy.8
  18.4 0.1 reshape.44
  18.5 0.1 broadcast_in_dim.28
  18.6 0.1 reshape.45.pos_ref
  18.7 12.2 %all-to-all-done = bf16[16,16,256]{2,1,0:T(8,128)(2,1)S(1)} async-done(((bf16[16,16,256]{2,1,0:T(8,128)(2,1)}), bf16[16,16,256]{2,1,0:T(8,128)(2,1)S(1)}, u32[]{:S(2)}, u32[]{:S(2)}) %all-to-all-start) | async-done | bytes 131104 | tf_op jit(solution)/shard_map/all_to_all | solution.py:199
  30.9 3.9 %all_to_all.30 = bf16[2,256,256]{2,1,0:T(8,128)(2,1)S(1)} all-to-all(bf16[2,256,256]{2,1,0:T(8,128)(2,1)S(1)} %broadcast_in_dim.32), channel_id=1, replica_groups={{0,16},{32,48},{64,80},{96,112},{128,144},{160,176},{192,208},{224,240}..., dimensions={0} | all-to-all | bytes 524288 | tf_op jit(solution)/shard_map/all_to_all | solution.py:199
  34.8 0.3 select.1
  35.1 0.0 copy-start
  35.2 0.0 copy-start.1
  35.2 24.4 %all_to_all.31.x_ref = bf16[16,128,256]{2,1,0:T(8,128)(2,1)S(1)} all-to-all(bf16[16,128,256]{2,1,0:T(8,128)(2,1)S(1)} %select.1), channel_id=1, replica_groups=mesh['sx'=32,'sy'=16] {'sy'}, dimensions={0} | all-to-all | bytes 2097152 | tf_op jit(solution)/shard_map/all_to_all | solution.py:199
  59.6 0.0 copy-done
  59.6 0.0 copy-done.1
  59.6 5.2 %attend.1 = bf16[16,144,256]{2,1,0:T(8,128)(2,1)S(1)} custom-call(bf16[16,128,256]{2,1,0:T(8,128)(2,1)S(1)} %all_to_all.31.x_ref, bf16[512,1024]{1,0:T(8,128)(2,1)S(1)} %copy-done, bf16[512,1024]{1,0:T(8,128)(2,1)S(1)} %copy-done.1), custom_call_target="tpu_custom_call" | custom-call | tf_op jit(solution)/shard_map/attend/pallas_call | solution.py:179
  64.8 21.0 %all_to_all.32.y_ref = bf16[16,144,256]{2,1,0:T(8,128)(2,1)S(1)} all-to-all(bf16[16,144,256]{2,1,0:T(8,128)(2,1)S(1)} %attend.1), channel_id=1, replica_groups=mesh['sx'=32,'sy'=16] {'sy'}, dimensions={0} | all-to-all | bytes 2359296 | tf_op jit(solution)/shard_map/all_to_all | solution.py:199
  85.8 2.6 %merge.1 = f32[2,256,384]{2,1,0:T(8,128)S(1)} custom-call(s32[2,512]{1,0:T(2,128)S(1)} %reshape.45.pos_ref, bf16[16,144,256]{2,1,0:T(8,128)(2,1)S(1)} %all_to_all.32.y_ref), custom_call_target="tpu_custom_call" | custom-call | tf_op jit(solution)/shard_map/merge/pallas_call | solution.py:179
  88.4 4.4 %all_to_all.33.a_ref = f32[2,256,384]{2,1,0:T(8,128)S(1)} all-to-all(f32[2,256,384]{2,1,0:T(8,128)S(1)} %merge.1), channel_id=1, replica_groups={{0,16},{32,48},{64,80},{96,112},{128,144},{160,176},{192,208},{224,240}..., dimensions={0} | all-to-all | bytes 1572864 | tf_op jit(solution)/shard_map/all_to_all | solution.py:199
  92.8 0.4 pair.1
  93.2 20.3 %all_to_all.34.a_ref = bf16[16,16,384]{2,1,0:T(8,128)(2,1)S(1)} all-to-all(bf16[16,16,384]{2,1,0:T(8,128)(2,1)S(1)} %pair.1), channel_id=1, replica_groups={{0,32,64,96,128,160,192,224,256,288,320,352,384,416,448,480},{16,48,80,..., dimensions={0} | all-to-all | bytes 393216 | tf_op jit(solution)/shard_map/all_to_all | solution.py:199
  113.5 0.4 last.1
  113.9 0.6 copy.9
  (5 shorter events, 0.0 us)
Async XLA Ops:
  1.4 29.4 %all-to-all-start = ((bf16[16,16,256]{2,1,0:T(8,128)(2,1)}), bf16[16,16,256]{2,1,0:T(8,128)(2,1)S(1)}, u32[]{:S(2)}, u32[]{:S(2)}) async-start(bf16[16,16,256]{2,1,0:T(8,128)(2,1)} %broadcast_in_dim.30), calls=%async_computation | async-start | bytes 262144 | tf_op jit(solution)/shard_map/all_to_all | solution.py:199
  35.1 24.5 %copy-start = (bf16[512,1024]{1,0:T(8,128)(2,1)S(1)}, bf16[512,1024]{1,0:T(8,128)(2,1)}, u32[]{:S(2)}) copy-start(bf16[512,1024]{1,0:T(8,128)(2,1)} %k_ref.1) | copy-start | bytes 3145732
  35.2 24.4 %copy-start.1 = (bf16[512,1024]{1,0:T(8,128)(2,1)S(1)}, bf16[512,1024]{1,0:T(8,128)(2,1)}, u32[]{:S(2)}) copy-start(bf16[512,1024]{1,0:T(8,128)(2,1)} %v_ref.1) | copy-start | bytes 3145732

commit v2 on v1

v2 whole, which is shorter than its diff:
```python
import functools

import jax
import jax.numpy as jnp
from jax import lax
from jax.experimental import pallas as pl
from jax.experimental.pallas import tpu as pltpu
from jax.sharding import PartitionSpec as P

QUERY_HEADS = 32
KEY_HEADS = 8
HEAD_WIDTH = 128
BLOCK = 4096
QUERY_PER_KEY = 4
LOG2E = 1.4426950408889634
NEVER = -1e30

FEAT = QUERY_PER_KEY * HEAD_WIDTH
STAT = 128
ONE_LANE = 12
SLOTS = 8


def pieces(x):
    hi = x.astype(jnp.bfloat16).astype(jnp.float32)
    rest = x - hi
    mid = rest.astype(jnp.bfloat16).astype(jnp.float32)
    return hi, mid, rest - mid


def stat_lanes(lse):
    lane = lax.broadcasted_iota(jnp.int32, (lse[0].shape[0], STAT), 1)
    stat = jnp.where(lane == ONE_LANE, 1.0, 0.0)
    for g in range(QUERY_PER_KEY):
        for k, piece in enumerate(pieces(lse[g])):
            stat = jnp.where(lane == g * 3 + k, piece, stat)
    return stat


def slot_onehot(pos):
    shape = (KEY_HEADS * SLOTS, pos.shape[1])
    r = lax.broadcasted_iota(jnp.int32, shape, 0)
    c = lax.broadcasted_iota(jnp.int32, shape, 1)
    hit = (pos == r % SLOTS) & (r // SLOTS == c % KEY_HEADS)
    return jnp.where(hit, 1.0, 0.0).astype(jnp.bfloat16)


def relay_kernel(k_ref, v_ref, out_ref):
    tokens = k_ref.shape[0]
    for h in range(KEY_HEADS):
        lanes = slice(h * HEAD_WIDTH, (h + 1) * HEAD_WIDTH)
        out_ref[h, :tokens] = k_ref[:, lanes]
        out_ref[h, tokens:] = v_ref[:, lanes]


def select_kernel(pos_ref, q_ref, out_ref):
    q = q_ref[...].astype(jnp.float32).reshape(-1, FEAT).astype(jnp.bfloat16)
    for b in range(4):
        hot = slot_onehot(pos_ref[b : b + 1, :])
        picked = jnp.dot(hot, q, preferred_element_type=jnp.float32)
        picked = picked.reshape(KEY_HEADS, SLOTS, FEAT).astype(jnp.bfloat16)
        out_ref[b * KEY_HEADS : (b + 1) * KEY_HEADS] = picked


def attend_kernel(x_ref, kv_ref, y_ref):
    scale = HEAD_WIDTH ** (-0.5) * LOG2E
    columns = x_ref.shape[0] // 2
    tokens = kv_ref.shape[1] // 2
    rows = columns * SLOTS
    lse = []
    for g in range(QUERY_PER_KEY):
        lanes = slice(g * HEAD_WIDTH, (g + 1) * HEAD_WIDTH)
        q = x_ref[:columns, :, lanes].astype(jnp.float32) + x_ref[columns:, :, lanes].astype(jnp.float32)
        q = q.reshape(rows, HEAD_WIDTH).astype(jnp.bfloat16)
        tops, totals, sums = [], [], []
        for slab in range(kv_ref.shape[0]):
            k = kv_ref[slab, :tokens]
            v = kv_ref[slab, tokens:]
            s = lax.dot_general(q, k, (((1,), (1,)), ((), ())), preferred_element_type=jnp.float32)
            m = jnp.max(s, axis=1, keepdims=True)
            w = jnp.exp2((s - m) * scale)
            tops.append(m)
            totals.append(jnp.sum(w, axis=1, keepdims=True))
            sums.append(jnp.dot(w.astype(jnp.bfloat16), v, preferred_element_type=jnp.float32))
        top = functools.reduce(jnp.maximum, tops)
        weights = [jnp.exp2((m - top) * scale) for m in tops]
        total = functools.reduce(jnp.add, [w * t for w, t in zip(weights, totals)])
        out = functools.reduce(jnp.add, [w * o for w, o in zip(weights, sums)]) / total
        out = out.reshape(columns, SLOTS, HEAD_WIDTH).astype(jnp.bfloat16)
        y_ref[:columns, :, lanes] = out
        y_ref[columns:, :, lanes] = out
        lse.append(top * scale + jnp.log2(total))
    stat = stat_lanes(lse).reshape(columns, SLOTS, STAT).astype(jnp.bfloat16)
    y_ref[:columns, :, FEAT:] = stat
    y_ref[columns:, :, FEAT:] = stat


def merge_kernel(pos_ref, y_ref, out_ref):
    flip = (((0,), (0,)), ((), ()))
    parts = []
    for b in range(4):
        y = y_ref[b * KEY_HEADS : (b + 1) * KEY_HEADS].astype(jnp.float32)
        y = y.reshape(KEY_HEADS * SLOTS, FEAT + STAT).astype(jnp.bfloat16)
        hot = slot_onehot(pos_ref[b : b + 1, :])
        parts.append(lax.dot_general(hot, y, flip, preferred_element_type=jnp.float32))
    named = [x[:, FEAT + ONE_LANE : FEAT + ONE_LANE + 1] > 0.5 for x in parts]
    shape = out_ref.shape[:-1]
    ends = []
    for g in range(QUERY_PER_KEY):
        lanes = slice(g * HEAD_WIDTH, (g + 1) * HEAD_WIDTH)
        at = FEAT + 3 * g
        lse = [
            jnp.where(n, x[:, at : at + 1] + (x[:, at + 1 : at + 2] + x[:, at + 2 : at + 3]), NEVER)
            for n, x in zip(named, parts)
        ]
        top = functools.reduce(jnp.maximum, lse)
        weights = [jnp.exp2(x - top) for x in lse]
        total = functools.reduce(jnp.add, weights)
        out = functools.reduce(jnp.add, [w * x[:, lanes] for w, x in zip(weights, parts)]) / total
        out_ref[:, :, lanes] = out.reshape(*shape, HEAD_WIDTH).astype(jnp.bfloat16)
        ends.append(top + jnp.log2(total))
    out_ref[:, :, FEAT:] = stat_lanes(ends).reshape(*shape, STAT).astype(jnp.bfloat16)


def last_kernel(a_ref, out_ref):
    for g in range(QUERY_PER_KEY):
        at = FEAT + 3 * g
        lse = [a_ref[:, :, at + k : at + k + 1].astype(jnp.float32) for k in range(3)]
        lse = lse[0] + (lse[1] + lse[2])
        weight = jnp.exp2(lse - jnp.max(lse, axis=0, keepdims=True))
        total = jnp.sum(weight, axis=0)
        lanes = slice(g * HEAD_WIDTH, (g + 1) * HEAD_WIDTH)
        mixed = jnp.sum(a_ref[:, :, lanes].astype(jnp.float32) * weight, axis=0) / total
        out_ref[:, lanes] = mixed.astype(jnp.bfloat16)


def call(kernel, shape, dtype, name, *args):
    return pl.pallas_call(
        kernel,
        out_shape=jax.ShapeDtypeStruct(shape, dtype),
        in_specs=[pl.BlockSpec(memory_space=pltpu.VMEM)] * len(args),
        out_specs=pl.BlockSpec(memory_space=pltpu.VMEM),
        compiler_params=pltpu.CompilerParams(vmem_limit_bytes=40 * 1024 * 1024),
        name=name,
    )(*args)


def per_device(queries, keys, values, block_ids):
    count_x = lax.axis_size("sx")
    count_y = lax.axis_size("sy")
    index_x = lax.axis_index("sx")
    index_y = lax.axis_index("sy")
    count_z = count_x // 2
    index_z, core = index_x // 2, index_x % 2
    tokens = keys.shape[0]
    slabs = BLOCK // tokens
    along_z = [[2 * z + c for z in range(count_z)] for c in range(2)]
    block_devices = [list(range(start, start + slabs)) for start in range(0, count_y, slabs)]
    plane = 2 * count_y
    planes = [list(range(z * plane, (z + 1) * plane)) for z in range(count_z)]

    def exchange(x, axis, groups):
        return lax.all_to_all(x, axis, split_axis=0, concat_axis=0, tiled=True, axis_index_groups=groups)

    column = lax.dynamic_index_in_dim(block_ids.reshape(count_x, count_y, -1), index_y, 1, keepdims=False)
    wanted = index_z * 4 + jnp.arange(4, dtype=jnp.int32)
    named = jnp.any(column[None] == wanted[:, None, None], axis=2)
    before = jnp.arange(count_x)[None, :] < jnp.arange(count_x)[:, None]
    rank = jnp.sum((named[:, None, :] & before[None]).astype(jnp.int32), axis=2)
    pos = jnp.where(named, rank, -1).reshape(4, count_z, 2)
    pos = lax.dynamic_index_in_dim(pos, core, 2, keepdims=False)
    pos = jnp.repeat(pos, KEY_HEADS, axis=1)

    rows = lax.all_gather(queries.reshape(KEY_HEADS, FEAT), "sx", axis=0, axis_index_groups=along_z)
    kv = call(relay_kernel, (KEY_HEADS, 2 * tokens, HEAD_WIDTH), jnp.bfloat16, "relay", keys, values)
    kv = exchange(kv, "sy", block_devices)
    asked = call(select_kernel, (plane, SLOTS, FEAT), jnp.bfloat16, "select", pos, rows)
    asked = exchange(asked, ("sx", "sy"), planes)
    part = call(attend_kernel, (plane, SLOTS, FEAT + STAT), jnp.bfloat16, "attend", asked, kv)
    part = exchange(part, ("sx", "sy"), planes)
    part = call(merge_kernel, (count_z, KEY_HEADS, FEAT + STAT), jnp.bfloat16, "merge", pos, part)
    part = exchange(part, "sx", along_z)
    out = call(last_kernel, (KEY_HEADS, FEAT), jnp.bfloat16, "last", part)
    return out.reshape(1, KEY_HEADS * FEAT)


def solution(mesh):
    return jax.shard_map(
        per_device,
        mesh=mesh,
        in_specs=(P(("sx", "sy"), None), P(("sx", "sy"), None), P(("sx", "sy"), None), P()),
        out_specs=P(("sx", "sy"), None),
        check_vma=False,
    )
```

time: 115 us -> 132 us (1.15)
  blocking collectives: 74.1 us -> 101 us
  starting transfers between devices: 15.2 us -> 7.32 us
  waiting for transfers between devices: 12.2 us -> 7.49 us
  Pallas kernels: 8.79 us -> 11.6 us
    all_gather x0 -> x1, blocking collectives: none -> 34 us  [per_device(): lax.all_gather(queries.reshape(KEY_HEADS, FEAT), 'sx', axis=0, axis_index...]
    all_to_all x1, starting transfers between devices: 15.2 us -> 7.32 us  [exchange(): lax.all_to_all(x, axis, split_axis=0, concat_axis=0, tiled=True, axis_ind...]
    all_to_all x5 -> x3, blocking collectives: 74.1 us -> 66.8 us  [exchange(): lax.all_to_all(x, axis, split_axis=0, concat_axis=0, tiled=True, axis_ind...]
    all_to_all x1, waiting for transfers between devices: 12.2 us -> 7.49 us  [exchange(): lax.all_to_all(x, axis, split_axis=0, concat_axis=0, tiled=True, axis_ind...]
    pallas_call x5, Pallas kernels: 8.79 us -> 11.6 us  [call(): pl.pallas_call(kernel, out_shape=jax.ShapeDtypeStruct(shape, dtype), in_s...]
  transfers between devices with their start and end apart: 1 -> 1, of which waited for: 1 -> 1; matrix products, arithmetic and copies ran while one was open for 2% -> 0% of each run, Pallas kernels for 0% -> 0%
where the time goes in v2:
time: 132 us
  blocking collectives  101 us (77%)
  Pallas kernels  11.6 us (9%)
  waiting for transfers between devices  7.49 us (6%)
  starting transfers between devices  7.32 us (6%)
  local copies, waits for them, and re-layouts  3.55 us (3%)
    all_to_all x3, blocking collectives, exchange(): lax.all_to_all(x, axis, split_axis=0, concat_axis=0, tiled=True, axis_ind...  66.8 us
    all_gather x1, blocking collectives, per_device(): lax.all_gather(queries.reshape(KEY_HEADS, FEAT), 'sx', axis=0, axis_index...  34 us
    pallas_call x5, Pallas kernels, call(): pl.pallas_call(kernel, out_shape=jax.ShapeDtypeStruct(shape, dtype), in_s...  11.6 us
    all_to_all x1, waiting for transfers between devices, exchange(): lax.all_to_all(x, axis, split_axis=0, concat_axis=0, tiled=True, axis_ind...  7.49 us
    all_to_all x1, starting transfers between devices, exchange(): lax.all_to_all(x, axis, split_axis=0, concat_axis=0, tiled=True, axis_ind...  7.32 us
  transfers between devices with their start and end apart: 1, of which 1 were waited for; matrix products, arithmetic and copies ran while one was open for 0% of the time, Pallas kernels for 0%

profile of v2, /device:TPU:32, one launch (start us, length us, event | category | flops | bytes accessed | tf_op | source)
XLA Modules:
  0.0 131.9 jit_solution(1995353881163802633)
XLA Ops:
  0.0 0.0 copy-start
  0.0 0.9 reduce.1
  0.9 34.0 %all_gather.3.q_ref = bf16[16,8,512]{2,1,0:T(8,128)(2,1)S(1)} all-gather(bf16[1,8,512]{2,1,0:T(8,128)(2,1)S(1)} %all_gather_reshape.3), channel_id=1, replica_groups={{0,32,64,96,128,160,192,224,256,288,320,352,384,416,448,480},{16,48,80,..., dimensions={0}, use_global_device_ids=true | all-gather | bytes 139264 | tf_op jit(solution)/shard_map/all_gather | solution.py:174
  34.9 0.9 reshape.33
  35.8 0.5 dynamic-slice_reduce_fusion
  36.2 0.1 compare_reduce_fusion
  36.3 0.2 convert_reduce_fusion
  36.5 0.1 copy.13
  36.6 0.1 copy.14
  36.7 0.1 broadcast_in_dim.6
  36.8 0.1 reshape.34.pos_ref
  36.9 0.9 select.7
  37.8 7.3 %all-to-all-start = ((bf16[32,8,512]{2,1,0:T(8,128)(2,1)}), bf16[32,8,512]{2,1,0:T(8,128)(2,1)S(1)}, u32[]{:S(2)}, u32[]{:S(2)}) async-start(bf16[32,8,512]{2,1,0:T(8,128)(2,1)} %select.7), calls=%async_computation | async-start | bytes 524288 | tf_op jit(solution)/shard_map/all_to_all | solution.py:163
  45.1 0.0 copy-done
  45.1 0.0 copy-start.1
  45.1 1.2 copy-done.1
  46.3 0.4 relay.1
  46.8 7.5 %all-to-all-done.x_ref = bf16[32,8,512]{2,1,0:T(8,128)(2,1)S(1)} async-done(((bf16[32,8,512]{2,1,0:T(8,128)(2,1)}), bf16[32,8,512]{2,1,0:T(8,128)(2,1)S(1)}, u32[]{:S(2)}, u32[]{:S(2)}) %all-to-all-start) | async-done | bytes 262176 | tf_op jit(solution)/shard_map/all_to_all | solution.py:163
  54.2 29.6 %all_to_all.20.kv_ref = bf16[8,1024,128]{2,1,0:T(8,128)(2,1)S(1)} all-to-all(bf16[8,1024,128]{2,1,0:T(8,128)(2,1)S(1)} %relay.1), channel_id=1, replica_groups={{0,1,2,3,4,5,6,7},{8,9,10,11,12,13,14,15},{16,17,18,19,20,21,22,23},{24..., dimensions={0} | all-to-all | bytes 4194304 | tf_op jit(solution)/shard_map/all_to_all | solution.py:163
  83.8 8.7 %attend.1 = bf16[32,8,640]{2,1,0:T(8,128)(2,1)S(1)} custom-call(bf16[32,8,512]{2,1,0:T(8,128)(2,1)S(1)} %all-to-all-done.x_ref, bf16[8,1024,128]{2,1,0:T(8,128)(2,1)S(1)} %all_to_all.20.kv_ref), custom_call_target="tpu_custom_call" | custom-call | tf_op jit(solution)/shard_map/attend/pallas_call | solution.py:138
  92.5 13.9 %all_to_all.21.y_ref = bf16[32,8,640]{2,1,0:T(8,128)(2,1)S(1)} all-to-all(bf16[32,8,640]{2,1,0:T(8,128)(2,1)S(1)} %attend.1), channel_id=1, replica_groups={{0,1,2,3,4,5,6,7,8,9,10,11,12,13,14,15,16,17,18,19,20,21,22,23,24,25,26..., dimensions={0} | all-to-all | bytes 655360 | tf_op jit(solution)/shard_map/all_to_all | solution.py:163
  106.4 1.3 merge.1
  107.7 23.3 %all_to_all.22.a_ref = bf16[16,8,640]{2,1,0:T(8,128)(2,1)S(1)} all-to-all(bf16[16,8,640]{2,1,0:T(8,128)(2,1)S(1)} %merge.1), channel_id=1, replica_groups={{0,32,64,96,128,160,192,224,256,288,320,352,384,416,448,480},{16,48,80,..., dimensions={0} | all-to-all | bytes 327680 | tf_op jit(solution)/shard_map/all_to_all | solution.py:163
  131.0 0.3 last.1
  131.3 0.6 copy.15
  (5 shorter events, 0.0 us)
Async XLA Ops:
  0.0 45.1 %copy-start = (bf16[512,1024]{1,0:T(8,128)(2,1)S(1)}, bf16[512,1024]{1,0:T(8,128)(2,1)}, u32[]{:S(2)}) copy-start(bf16[512,1024]{1,0:T(8,128)(2,1)} %k_ref.1) | copy-start | bytes 3145732
  37.8 16.5 %all-to-all-start = ((bf16[32,8,512]{2,1,0:T(8,128)(2,1)}), bf16[32,8,512]{2,1,0:T(8,128)(2,1)S(1)}, u32[]{:S(2)}, u32[]{:S(2)}) async-start(bf16[32,8,512]{2,1,0:T(8,128)(2,1)} %select.7), calls=%async_computation | async-start | bytes 524288 | tf_op jit(solution)/shard_map/all_to_all | solution.py:163
  45.1 1.2 copy-start.1

commit v3 on v2

--- a/solution.py
+++ b/solution.py
@@ -174,6 +174,7 @@
     rows = lax.all_gather(queries.reshape(KEY_HEADS, FEAT), "sx", axis=0, axis_index_groups=along_z)
     kv = call(relay_kernel, (KEY_HEADS, 2 * tokens, HEAD_WIDTH), jnp.bfloat16, "relay", keys, values)
     kv = exchange(kv, "sy", block_devices)
+    rows, pos, kv = lax.optimization_barrier((rows, pos, kv))
     asked = call(select_kernel, (plane, SLOTS, FEAT), jnp.bfloat16, "select", pos, rows)
     asked = exchange(asked, ("sx", "sy"), planes)
     part = call(attend_kernel, (plane, SLOTS, FEAT + STAT), jnp.bfloat16, "attend", asked, kv)

time: 132 us -> 109 us (0.83)
  blocking collectives: 101 us -> 86.9 us
  waiting for transfers between devices: 7.49 us -> 0.01 us
  starting transfers between devices: 7.32 us -> 5.44 us
  local copies, waits for them, and re-layouts: 3.55 us -> 5.37 us
    all_to_all x3, blocking collectives: 66.8 us -> 52.9 us  [exchange(): lax.all_to_all(x, axis, split_axis=0, concat_axis=0, tiled=True, axis_ind...]
    all_to_all x1, waiting for transfers between devices: 7.49 us -> 0.01 us  [exchange(): lax.all_to_all(x, axis, split_axis=0, concat_axis=0, tiled=True, axis_ind...]
    unnamed x5 -> x11, local copies, waits for them, and re-layouts: 1.84 us -> 4.42 us
    all_to_all x1, starting transfers between devices: 7.32 us -> 5.44 us  [exchange(): lax.all_to_all(x, axis, split_axis=0, concat_axis=0, tiled=True, axis_ind...]
  transfers between devices with their start and end apart: 1 -> 1, of which waited for: 1 -> 0; matrix products, arithmetic and copies ran while one was open for 0% -> 1% of each run, Pallas kernels for 0% -> 0%
where the time goes in v3:
time: 109 us
  blocking collectives  86.9 us (80%)
  Pallas kernels  10.9 us (10%)
  starting transfers between devices  5.44 us (5%)
  local copies, waits for them, and re-layouts  5.37 us (5%)
    all_to_all x3, blocking collectives, exchange(): lax.all_to_all(x, axis, split_axis=0, concat_axis=0, tiled=True, axis_ind...  52.9 us
    all_gather x1, blocking collectives, per_device(): lax.all_gather(queries.reshape(KEY_HEADS, FEAT), 'sx', axis=0, axis_index...  34 us
    pallas_call x5, Pallas kernels, call(): pl.pallas_call(kernel, out_shape=jax.ShapeDtypeStruct(shape, dtype), in_s...  10.9 us
    all_to_all x1, starting transfers between devices, exchange(): lax.all_to_all(x, axis, split_axis=0, concat_axis=0, tiled=True, axis_ind...  5.44 us
    unnamed x11, local copies, waits for them, and re-layouts  4.42 us
  transfers between devices with their start and end apart: 1, of which 0 were waited for; matrix products, arithmetic and copies ran while one was open for 1% of the time, Pallas kernels for 0%

profile of v3, /device:TPU:32, one launch (start us, length us, event | category | flops | bytes accessed | tf_op | source)
XLA Modules:
  0.0 109.0 jit_solution(4148235720565896466)
XLA Ops:
  0.0 0.0 copy-start.1
  0.0 1.2 %copy-done.1 = bf16[512,1024]{1,0:T(8,128)(2,1)S(1)} copy-done((bf16[512,1024]{1,0:T(8,128)(2,1)S(1)}, bf16[512,1024]{1,0:T(8,128)(2,1)}, u32[]{:S(2)}) %copy-start.1) | copy-done | bytes 1048600
  1.2 0.0 copy-start.2
  1.2 1.2 %copy-done.2 = bf16[512,1024]{1,0:T(8,128)(2,1)S(1)} copy-done((bf16[512,1024]{1,0:T(8,128)(2,1)S(1)}, bf16[512,1024]{1,0:T(8,128)(2,1)}, u32[]{:S(2)}) %copy-start.2) | copy-done | bytes 1048600
  2.5 0.4 relay.1
  2.9 0.0 copy-start
  2.9 1.3 %copy-done = bf16[8,1024,128]{2,1,0:T(8,128)(2,1)} copy-done((bf16[8,1024,128]{2,1,0:T(8,128)(2,1)}, bf16[8,1024,128]{2,1,0:T(8,128)(2,1)S(1)}, u32[]{:S(2)}) %copy-start) | copy-done | bytes 2097176
  4.2 0.0 copy-start.3
  4.2 0.0 copy-start.4
  4.2 5.4 %all-to-all-start = ((bf16[8,1024,128]{2,1,0:T(8,128)(2,1)}), bf16[8,1024,128]{2,1,0:T(8,128)(2,1)S(1)}, u32[]{:S(2)}, u32[]{:S(2)}) async-start(bf16[8,1024,128]{2,1,0:T(8,128)(2,1)} %copy-done), calls=%async_computation | async-start | bytes 4194304 | tf_op jit(solution)/shard_map/all_to_all | solution.py:163
  9.7 0.0 copy-done.3
  9.7 0.1 reshape.33
  9.8 0.5 dynamic-slice_reduce_fusion
  10.3 0.1 compare_reduce_fusion
  10.4 0.2 convert_reduce_fusion
  10.6 0.1 copy.13
  10.7 0.1 copy.14
  10.8 0.1 broadcast_in_dim.6
  10.8 0.1 reshape.34.pos_ref
  10.9 0.0 copy-done.4
  10.9 0.1 reduce
  11.0 34.0 %all_gather.3.q_ref = bf16[16,8,512]{2,1,0:T(8,128)(2,1)S(1)} all-gather(bf16[1,8,512]{2,1,0:T(8,128)(2,1)S(1)} %all_gather_reshape.3), channel_id=1, replica_groups={{0,32,64,96,128,160,192,224,256,288,320,352,384,416,448,480},{16,48,80,..., dimensions={0}, use_global_device_ids=true | all-gather | bytes 139264 | tf_op jit(solution)/shard_map/all_gather | solution.py:174
  45.0 0.0 all-to-all-done.kv_ref
  45.0 0.2 select.7
  45.2 16.5 %all_to_all.20.x_ref = bf16[32,8,512]{2,1,0:T(8,128)(2,1)S(1)} all-to-all(bf16[32,8,512]{2,1,0:T(8,128)(2,1)S(1)} %select.7), channel_id=1, replica_groups={{0,1,2,3,4,5,6,7,8,9,10,11,12,13,14,15,16,17,18,19,20,21,22,23,24,25,26..., dimensions={0} | all-to-all | bytes 524288 | tf_op jit(solution)/shard_map/all_to_all | solution.py:163
  61.7 8.7 %attend.1 = bf16[32,8,640]{2,1,0:T(8,128)(2,1)S(1)} custom-call(bf16[32,8,512]{2,1,0:T(8,128)(2,1)S(1)} %all_to_all.20.x_ref, bf16[8,1024,128]{2,1,0:T(8,128)(2,1)S(1)} %all-to-all-done.kv_ref), custom_call_target="tpu_custom_call" | custom-call | tf_op jit(solution)/shard_map/attend/pallas_call | solution.py:138
  70.4 13.1 %all_to_all.21.y_ref = bf16[32,8,640]{2,1,0:T(8,128)(2,1)S(1)} all-to-all(bf16[32,8,640]{2,1,0:T(8,128)(2,1)S(1)} %attend.1), channel_id=1, replica_groups={{0,1,2,3,4,5,6,7,8,9,10,11,12,13,14,15,16,17,18,19,20,21,22,23,24,25,26..., dimensions={0} | all-to-all | bytes 655360 | tf_op jit(solution)/shard_map/all_to_all | solution.py:163
  83.4 1.3 %merge.1 = bf16[16,8,640]{2,1,0:T(8,128)(2,1)S(1)} custom-call(s32[4,128]{1,0:T(4,128)S(1)} %reshape.34.pos_ref, bf16[32,8,640]{2,1,0:T(8,128)(2,1)S(1)} %all_to_all.21.y_ref), custom_call_target="tpu_custom_call" | custom-call | tf_op jit(solution)/shard_map/merge/pallas_call | solution.py:138
  84.7 23.3 %all_to_all.22.a_ref = bf16[16,8,640]{2,1,0:T(8,128)(2,1)S(1)} all-to-all(bf16[16,8,640]{2,1,0:T(8,128)(2,1)S(1)} %merge.1), channel_id=1, replica_groups={{0,32,64,96,128,160,192,224,256,288,320,352,384,416,448,480},{16,48,80,..., dimensions={0} | all-to-all | bytes 327680 | tf_op jit(solution)/shard_map/all_to_all | solution.py:163
  108.1 0.3 last.1
  108.4 0.6 copy.15
  (5 shorter events, 0.1 us)
Async XLA Ops:
  0.0 1.2 %copy-start.1 = (bf16[512,1024]{1,0:T(8,128)(2,1)S(1)}, bf16[512,1024]{1,0:T(8,128)(2,1)}, u32[]{:S(2)}) copy-start(bf16[512,1024]{1,0:T(8,128)(2,1)} %k_ref.1) | copy-start | bytes 3145732
  1.2 1.2 %copy-start.2 = (bf16[512,1024]{1,0:T(8,128)(2,1)S(1)}, bf16[512,1024]{1,0:T(8,128)(2,1)}, u32[]{:S(2)}) copy-start(bf16[512,1024]{1,0:T(8,128)(2,1)} %v_ref.1) | copy-start | bytes 3145732
  2.9 1.4 %copy-start = (bf16[8,1024,128]{2,1,0:T(8,128)(2,1)}, bf16[8,1024,128]{2,1,0:T(8,128)(2,1)S(1)}, u32[]{:S(2)}) copy-start(bf16[8,1024,128]{2,1,0:T(8,128)(2,1)S(1)} %relay.1) | copy-start | bytes 6291460
  4.2 5.5 %copy-start.3 = (s32[512,16]{0,1:T(8,128)S(1)}, s32[512,16]{0,1:T(8,128)}, u32[]{:S(2)}) copy-start(s32[512,16]{0,1:T(8,128)} %param.7) | copy-start | bytes 98308
  4.2 6.7 %copy-start.4 = (bf16[1,4096]{1,0:T(2,128)(2,1)S(1)}, bf16[1,4096]{1,0:T(2,128)(2,1)}, u32[]{:S(2)}) copy-start(bf16[1,4096]{1,0:T(2,128)(2,1)} %param.4) | copy-start | bytes 24580
  4.2 40.8 %all-to-all-start = ((bf16[8,1024,128]{2,1,0:T(8,128)(2,1)}), bf16[8,1024,128]{2,1,0:T(8,128)(2,1)S(1)}, u32[]{:S(2)}, u32[]{:S(2)}) async-start(bf16[8,1024,128]{2,1,0:T(8,128)(2,1)} %copy-done), calls=%async_computation | async-start | bytes 4194304 | tf_op jit(solution)/shard_map/all_to_all | solution.py:163

commit v4 on v2

--- a/solution.py
+++ b/solution.py
@@ -53,44 +53,54 @@
         out_ref[h, tokens:] = v_ref[:, lanes]
 
 
-def select_kernel(pos_ref, q_ref, out_ref):
-    q = q_ref[...].astype(jnp.float32).reshape(-1, FEAT).astype(jnp.bfloat16)
-    for b in range(4):
-        hot = slot_onehot(pos_ref[b : b + 1, :])
-        picked = jnp.dot(hot, q, preferred_element_type=jnp.float32)
-        picked = picked.reshape(KEY_HEADS, SLOTS, FEAT).astype(jnp.bfloat16)
-        out_ref[b * KEY_HEADS : (b + 1) * KEY_HEADS] = picked
-
-
-def attend_kernel(x_ref, kv_ref, y_ref):
+def by_head_kernel(x_ref, out_ref):
+    n = x_ref.shape[0]
+    rows = n // QUERY_PER_KEY
+    r = lax.broadcasted_iota(jnp.int32, (n, n), 0)
+    c = lax.broadcasted_iota(jnp.int32, (n, n), 1)
+    hot = jnp.where((c % QUERY_PER_KEY == r // rows) & (c // QUERY_PER_KEY == r % rows), 1.0, 0.0)
+    x = jnp.dot(hot.astype(jnp.bfloat16), x_ref[...], preferred_element_type=jnp.float32)
+    out_ref[...] = x.astype(jnp.bfloat16)
+
+
+def attend_kernel(pos_ref, x_ref, kv_ref, y_ref):
     scale = HEAD_WIDTH ** (-0.5) * LOG2E
-    columns = x_ref.shape[0] // 2
+    columns = y_ref.shape[0] // 2
     tokens = kv_ref.shape[1] // 2
     rows = columns * SLOTS
-    lse = []
-    for g in range(QUERY_PER_KEY):
+    everyone = pos_ref.shape[1]
+    r = lax.broadcasted_iota(jnp.int32, (rows, everyone), 0)
+    c = lax.broadcasted_iota(jnp.int32, (rows, everyone), 1)
+    hit = (pos_ref[...] == r % SLOTS) & (r // SLOTS == c % columns)
+    hot = jnp.where(hit, 1.0, 0.0).astype(jnp.bfloat16)
+    q = [
+        jnp.dot(hot, x_ref[:, g].reshape(everyone, HEAD_WIDTH), preferred_element_type=jnp.float32)
+        for g in range(QUERY_PER_KEY)
+    ]
+    q = jnp.concatenate([x.astype(jnp.bfloat16) for x in q], axis=0)
+    ones = jnp.ones((tokens, HEAD_WIDTH), jnp.bfloat16)
+    tops, sums = [], []
+    for slab in range(kv_ref.shape[0]):
+        k = kv_ref[slab, :tokens]
+        v = jnp.concatenate([kv_ref[slab, tokens:], ones], axis=1)
+        s = lax.dot_general(q, k, (((1,), (1,)), ((), ())), preferred_element_type=jnp.float32)
+        m = jnp.max(s, axis=1, keepdims=True)
+        w = jnp.exp2((s - m) * scale).astype(jnp.bfloat16)
+        tops.append(m)
+        sums.append(jnp.dot(w, v, preferred_element_type=jnp.float32))
+    top = functools.reduce(jnp.maximum, tops)
+    both = functools.reduce(jnp.add, [jnp.exp2((m - top) * scale) * x for m, x in zip(tops, sums)])
+    total = both[:, HEAD_WIDTH:]
+    out = both[:, :HEAD_WIDTH] / total
+    lse = top * scale + jnp.log2(total[:, :1])
+    ends = []
+    for g in range(QUERY_PER_KEY):
+        part = out[g * rows : (g + 1) * rows].reshape(columns, SLOTS, HEAD_WIDTH).astype(jnp.bfloat16)
         lanes = slice(g * HEAD_WIDTH, (g + 1) * HEAD_WIDTH)
-        q = x_ref[:columns, :, lanes].astype(jnp.float32) + x_ref[columns:, :, lanes].astype(jnp.float32)
-        q = q.reshape(rows, HEAD_WIDTH).astype(jnp.bfloat16)
-        tops, totals, sums = [], [], []
-        for slab in range(kv_ref.shape[0]):
-            k = kv_ref[slab, :tokens]
-            v = kv_ref[slab, tokens:]
-            s = lax.dot_general(q, k, (((1,), (1,)), ((), ())), preferred_element_type=jnp.float32)
-            m = jnp.max(s, axis=1, keepdims=True)
-            w = jnp.exp2((s - m) * scale)
-            tops.append(m)
-            totals.append(jnp.sum(w, axis=1, keepdims=True))
-            sums.append(jnp.dot(w.astype(jnp.bfloat16), v, preferred_element_type=jnp.float32))
-        top = functools.reduce(jnp.maximum, tops)
-        weights = [jnp.exp2((m - top) * scale) for m in tops]
-        total = functools.reduce(jnp.add, [w * t for w, t in zip(weights, totals)])
-        out = functools.reduce(jnp.add, [w * o for w, o in zip(weights, sums)]) / total
-        out = out.reshape(columns, SLOTS, HEAD_WIDTH).astype(jnp.bfloat16)
-        y_ref[:columns, :, lanes] = out
-        y_ref[columns:, :, lanes] = out
-        lse.append(top * scale + jnp.log2(total))
-    stat = stat_lanes(lse).reshape(columns, SLOTS, STAT).astype(jnp.bfloat16)
+        y_ref[:columns, :, lanes] = part
+        y_ref[columns:, :, lanes] = part
+        ends.append(lse[g * rows : (g + 1) * rows])
+    stat = stat_lanes(ends).reshape(columns, SLOTS, STAT).astype(jnp.bfloat16)
     y_ref[:columns, :, FEAT:] = stat
     y_ref[columns:, :, FEAT:] = stat
 
@@ -162,23 +172,33 @@
     def exchange(x, axis, groups):
         return lax.all_to_all(x, axis, split_axis=0, concat_axis=0, tiled=True, axis_index_groups=groups)
 
-    column = lax.dynamic_index_in_dim(block_ids.reshape(count_x, count_y, -1), index_y, 1, keepdims=False)
-    wanted = index_z * 4 + jnp.arange(4, dtype=jnp.int32)
-    named = jnp.any(column[None] == wanted[:, None, None], axis=2)
-    before = jnp.arange(count_x)[None, :] < jnp.arange(count_x)[:, None]
-    rank = jnp.sum((named[:, None, :] & before[None]).astype(jnp.int32), axis=2)
-    pos = jnp.where(named, rank, -1).reshape(4, count_z, 2)
-    pos = lax.dynamic_index_in_dim(pos, core, 2, keepdims=False)
-    pos = jnp.repeat(pos, KEY_HEADS, axis=1)
-
-    rows = lax.all_gather(queries.reshape(KEY_HEADS, FEAT), "sx", axis=0, axis_index_groups=along_z)
+    def ranks(block_named):
+        before = jnp.arange(count_x)[None, :] < jnp.arange(count_x)[:, None]
+        rank = jnp.sum((block_named[:, None] & before[None, :, :, None]).astype(jnp.int32), axis=2)
+        return jnp.where(block_named, rank, -1)
+
+    ids = block_ids.reshape(1, count_x, count_y, -1)
+    my_block = index_x * 2 + index_y // slabs
+    pos_in = ranks(jnp.any(ids == my_block, axis=3)).reshape(1, count_x * count_y)
+    column = lax.dynamic_slice_in_dim(ids, index_y, 1, 2)
+    wanted = (index_z * 4 + jnp.arange(4, dtype=jnp.int32)).reshape(4, 1, 1, 1)
+    pos_out = ranks(jnp.any(column == wanted, axis=3)).reshape(4, count_z, 2)
+    pos_out = lax.dynamic_index_in_dim(pos_out, core, 2, keepdims=False)
+    pos_out = jnp.repeat(pos_out, KEY_HEADS, axis=1)
+
+    own = queries.reshape(1, KEY_HEADS, QUERY_PER_KEY, HEAD_WIDTH)
+    own = jnp.broadcast_to(own, (4, KEY_HEADS, QUERY_PER_KEY, HEAD_WIDTH))
+    slices = exchange(own.reshape(plane, QUERY_PER_KEY, HEAD_WIDTH), ("sx", "sy"), planes)
     kv = call(relay_kernel, (KEY_HEADS, 2 * tokens, HEAD_WIDTH), jnp.bfloat16, "relay", keys, values)
+    slices, kv, pos_in, pos_out = lax.optimization_barrier((slices, kv, pos_in, pos_out))
     kv = exchange(kv, "sy", block_devices)
-    asked = call(select_kernel, (plane, SLOTS, FEAT), jnp.bfloat16, "select", pos, rows)
-    asked = exchange(asked, ("sx", "sy"), planes)
-    part = call(attend_kernel, (plane, SLOTS, FEAT + STAT), jnp.bfloat16, "attend", asked, kv)
+    slices = slices.reshape(plane * QUERY_PER_KEY, HEAD_WIDTH)
+    slices = call(by_head_kernel, slices.shape, jnp.bfloat16, "by_head", slices)
+    slices = slices.reshape(QUERY_PER_KEY, plane, HEAD_WIDTH)
+    rows = lax.all_gather(slices, "sx", axis=0, axis_index_groups=along_z)
+    part = call(attend_kernel, (plane, SLOTS, FEAT + STAT), jnp.bfloat16, "attend", pos_in, rows, kv)
     part = exchange(part, ("sx", "sy"), planes)
-    part = call(merge_kernel, (count_z, KEY_HEADS, FEAT + STAT), jnp.bfloat16, "merge", pos, part)
+    part = call(merge_kernel, (count_z, KEY_HEADS, FEAT + STAT), jnp.bfloat16, "merge", pos_out, part)
     part = exchange(part, "sx", along_z)
     out = call(last_kernel, (KEY_HEADS, FEAT), jnp.bfloat16, "last", part)
     return out.reshape(1, KEY_HEADS * FEAT)

time: 132 us -> 105 us (0.80)
  blocking collectives: 101 us -> 76.7 us
  waiting for transfers between devices: 7.49 us -> 0.01 us
  Pallas kernels: 11.6 us -> 5.52 us
  starting transfers between devices: 7.32 us -> 12.8 us
  local copies, waits for them, and re-layouts: 3.55 us -> 6.96 us
  other arithmetic: 1.12 us -> 2.45 us
    all_to_all x3 -> x2, blocking collectives: 66.8 us -> 40.4 us  [exchange(): lax.all_to_all(x, axis, split_axis=0, concat_axis=0, tiled=True, axis_ind...]
    all_to_all x1 -> x2, waiting for transfers between devices: 7.49 us -> 0.01 us  [exchange(): lax.all_to_all(x, axis, split_axis=0, concat_axis=0, tiled=True, axis_ind...]
    pallas_call x5, Pallas kernels: 11.6 us -> 5.52 us  [call(): pl.pallas_call(kernel, out_shape=jax.ShapeDtypeStruct(shape, dtype), in_s...]
    all_to_all x1 -> x2, starting transfers between devices: 7.32 us -> 12.8 us  [exchange(): lax.all_to_all(x, axis, split_axis=0, concat_axis=0, tiled=True, axis_ind...]
    unnamed x5 -> x7, local copies, waits for them, and re-layouts: 1.84 us -> 4.41 us
    all_gather x1, blocking collectives: 34 us -> 36.3 us  [per_device(): rows = lax.all_gather(slices, 'sx', axis=0, axis_index_groups=along_z)]
  transfers between devices with their start and end apart: 1 -> 2, of which waited for: 1 -> 0; matrix products, arithmetic and copies ran while one was open for 0% -> 3% of each run, Pallas kernels for 0% -> 1%
where the time goes in v4:
time: 105 us
  blocking collectives  76.7 us (73%)
  starting transfers between devices  12.8 us (12%)
  local copies, waits for them, and re-layouts  6.96 us (7%)
  Pallas kernels  5.52 us (5%)
  other arithmetic  2.45 us (2%)
    all_to_all x2, blocking collectives, exchange(): lax.all_to_all(x, axis, split_axis=0, concat_axis=0, tiled=True, axis_ind...  40.4 us
    all_gather x1, blocking collectives, per_device(): rows = lax.all_gather(slices, 'sx', axis=0, axis_index_groups=along_z)  36.3 us
    all_to_all x2, starting transfers between devices, exchange(): lax.all_to_all(x, axis, split_axis=0, concat_axis=0, tiled=True, axis_ind...  12.8 us
    pallas_call x5, Pallas kernels, call(): pl.pallas_call(kernel, out_shape=jax.ShapeDtypeStruct(shape, dtype), in_s...  5.52 us
    unnamed x7, local copies, waits for them, and re-layouts  4.41 us
  transfers between devices with their start and end apart: 2, of which 0 were waited for; matrix products, arithmetic and copies ran while one was open for 3% of the time, Pallas kernels for 1%

profile of v4, /device:TPU:32, one launch (start us, length us, event | category | flops | bytes accessed | tf_op | source)
XLA Modules:
  0.0 104.6 jit_solution(17780263558444730621)
XLA Ops:
  0.0 0.8 reduce.4
  0.8 0.6 broadcast_in_dim.15
  1.4 7.3 %all-to-all-start = ((bf16[32,4,128]{2,1,0:T(4,128)(2,1)}), bf16[32,4,128]{2,1,0:T(4,128)(2,1)S(1)}, u32[]{:S(2)}, u32[]{:S(2)}) async-start(bf16[32,4,128]{2,1,0:T(4,128)(2,1)} %bitcast), calls=%async_computation | async-start | bytes 65536 | tf_op jit(solution)/shard_map/all_to_all | solution.py:173
  8.8 0.9 reshape.106
  9.7 0.8 compare_reduce_fusion.1
  10.5 0.1 and.61
  10.6 0.1 copy.13
  10.6 0.6 convert_reduce_fusion
  11.3 0.1 reduce_sum.21
  11.4 0.5 dynamic-slice_reduce_fusion
  11.8 0.1 compare_reduce_fusion
  11.9 0.2 convert_reduce_fusion.1
  12.1 0.1 copy.14
  12.2 0.1 copy.15
  12.3 0.1 broadcast_in_dim.30
  12.4 0.1 reshape.107.pos_ref
  12.5 0.0 copy-start.1
  12.5 1.2 %copy-done.1 = bf16[512,1024]{1,0:T(8,128)(2,1)S(1)} copy-done((bf16[512,1024]{1,0:T(8,128)(2,1)S(1)}, bf16[512,1024]{1,0:T(8,128)(2,1)}, u32[]{:S(2)}) %copy-start.1) | copy-done | bytes 1048600
  13.7 1.2 %copy-done.2 = bf16[512,1024]{1,0:T(8,128)(2,1)S(1)} copy-done((bf16[512,1024]{1,0:T(8,128)(2,1)S(1)}, bf16[512,1024]{1,0:T(8,128)(2,1)}, u32[]{:S(2)}) %copy-start.2) | copy-done | bytes 1048600
  14.9 0.4 relay.1
  15.3 1.3 %copy-done = bf16[8,1024,128]{2,1,0:T(8,128)(2,1)} copy-done((bf16[8,1024,128]{2,1,0:T(8,128)(2,1)}, bf16[8,1024,128]{2,1,0:T(8,128)(2,1)S(1)}, u32[]{:S(2)}) %copy-start) | copy-done | bytes 2097176
  16.7 0.0 all-to-all-done
  16.7 5.5 %all-to-all-start.1 = ((bf16[8,1024,128]{2,1,0:T(8,128)(2,1)}), bf16[8,1024,128]{2,1,0:T(8,128)(2,1)S(1)}, u32[]{:S(2)}, u32[]{:S(2)}) async-start(bf16[8,1024,128]{2,1,0:T(8,128)(2,1)} %copy-done), calls=%async_computation.1 | async-start | bytes 4194304 | tf_op jit(solution)/shard_map/all_to_all | solution.py:173
  22.2 0.1 by_head.1
  22.3 36.3 %all_gather.3.x_ref = bf16[16,4,32,128]{3,2,1,0:T(8,128)(2,1)S(1)} all-gather(bf16[1,4,32,128]{3,2,1,0:T(8,128)(2,1)S(1)} %bitcast.11), channel_id=1, replica_groups={{0,32,64,96,128,160,192,224,256,288,320,352,384,416,448,480},{16,48,80,..., dimensions={0}, use_global_device_ids=true | all-gather | bytes 557056 | tf_op jit(solution)/shard_map/all_gather | solution.py:198
  58.6 0.0 all-to-all-done.1.kv_ref
  58.6 3.3 %attend.1 = bf16[32,8,640]{2,1,0:T(8,128)(2,1)S(1)} custom-call(s32[1,512]{1,0:T(1,128)S(1)} %reshape_select_fusion.pos_ref, bf16[16,4,32,128]{3,2,1,0:T(8,128)(2,1)S(1)} %all_gather.3.x_ref, bf16[8,1024,128]{2,1,0:T(8,128)(2,1)S(1)} %all-to-all-done.1.kv_ref), custom_call_target="tpu_custom_call" | custom-call | tf_op jit(solution)/shard_map/attend/pallas_call | solution.py:148
  61.9 17.1 %all_to_all.20.y_ref = bf16[32,8,640]{2,1,0:T(8,128)(2,1)S(1)} all-to-all(bf16[32,8,640]{2,1,0:T(8,128)(2,1)S(1)} %attend.1), channel_id=1, replica_groups={{0,1,2,3,4,5,6,7,8,9,10,11,12,13,14,15,16,17,18,19,20,21,22,23,24,25,26..., dimensions={0} | all-to-all | bytes 655360 | tf_op jit(solution)/shard_map/all_to_all | solution.py:173
  79.0 1.3 %merge.1 = bf16[16,8,640]{2,1,0:T(8,128)(2,1)S(1)} custom-call(s32[4,128]{1,0:T(4,128)S(1)} %reshape.107.pos_ref, bf16[32,8,640]{2,1,0:T(8,128)(2,1)S(1)} %all_to_all.20.y_ref), custom_call_target="tpu_custom_call" | custom-call | tf_op jit(solution)/shard_map/merge/pallas_call | solution.py:148
  80.3 23.3 %all_to_all.21.a_ref = bf16[16,8,640]{2,1,0:T(8,128)(2,1)S(1)} all-to-all(bf16[16,8,640]{2,1,0:T(8,128)(2,1)S(1)} %merge.1), channel_id=1, replica_groups={{0,32,64,96,128,160,192,224,256,288,320,352,384,416,448,480},{16,48,80,..., dimensions={0} | all-to-all | bytes 327680 | tf_op jit(solution)/shard_map/all_to_all | solution.py:173
  103.6 0.3 last.1
  104.0 0.6 copy.16
  (7 shorter events, 0.0 us)
Async XLA Ops:
  1.4 15.3 %all-to-all-start = ((bf16[32,4,128]{2,1,0:T(4,128)(2,1)}), bf16[32,4,128]{2,1,0:T(4,128)(2,1)S(1)}, u32[]{:S(2)}, u32[]{:S(2)}) async-start(bf16[32,4,128]{2,1,0:T(4,128)(2,1)} %bitcast), calls=%async_computation | async-start | bytes 65536 | tf_op jit(solution)/shard_map/all_to_all | solution.py:173
  12.5 1.2 %copy-start.1 = (bf16[512,1024]{1,0:T(8,128)(2,1)S(1)}, bf16[512,1024]{1,0:T(8,128)(2,1)}, u32[]{:S(2)}) copy-start(bf16[512,1024]{1,0:T(8,128)(2,1)} %k_ref.1) | copy-start | bytes 3145732
  13.7 1.2 %copy-start.2 = (bf16[512,1024]{1,0:T(8,128)(2,1)S(1)}, bf16[512,1024]{1,0:T(8,128)(2,1)}, u32[]{:S(2)}) copy-start(bf16[512,1024]{1,0:T(8,128)(2,1)} %v_ref.1) | copy-start | bytes 3145732
  15.3 1.4 %copy-start = (bf16[8,1024,128]{2,1,0:T(8,128)(2,1)}, bf16[8,1024,128]{2,1,0:T(8,128)(2,1)S(1)}, u32[]{:S(2)}) copy-start(bf16[8,1024,128]{2,1,0:T(8,128)(2,1)S(1)} %relay.1) | copy-start | bytes 6291460
  16.7 41.9 %all-to-all-start.1 = ((bf16[8,1024,128]{2,1,0:T(8,128)(2,1)}), bf16[8,1024,128]{2,1,0:T(8,128)(2,1)S(1)}, u32[]{:S(2)}, u32[]{:S(2)}) async-start(bf16[8,1024,128]{2,1,0:T(8,128)(2,1)} %copy-done), calls=%async_computation.1 | async-start | bytes 4194304 | tf_op jit(solution)/shard_map/all_to_all | solution.py:173

commit v5 on v2

--- a/solution.py
+++ b/solution.py
@@ -45,12 +45,13 @@
     return jnp.where(hit, 1.0, 0.0).astype(jnp.bfloat16)
 
 
-def relay_kernel(k_ref, v_ref, out_ref):
+def relay_kernel(me_ref, k_ref, v_ref, *out_refs):
     tokens = k_ref.shape[0]
-    for h in range(KEY_HEADS):
-        lanes = slice(h * HEAD_WIDTH, (h + 1) * HEAD_WIDTH)
-        out_ref[h, :tokens] = k_ref[:, lanes]
-        out_ref[h, tokens:] = v_ref[:, lanes]
+    for i, out_ref in enumerate(out_refs):
+        head = jnp.bitwise_xor(me_ref[0], i)
+        lanes = pl.ds(pl.multiple_of(head * HEAD_WIDTH, HEAD_WIDTH), HEAD_WIDTH)
+        out_ref[:tokens] = k_ref[:, lanes]
+        out_ref[tokens:] = v_ref[:, lanes]
 
 
 def select_kernel(pos_ref, q_ref, out_ref):
@@ -62,35 +63,39 @@
         out_ref[b * KEY_HEADS : (b + 1) * KEY_HEADS] = picked
 
 
-def attend_kernel(x_ref, kv_ref, y_ref):
+def attend_kernel(x_ref, *refs):
+    kv_refs, y_ref = refs[:-1], refs[-1]
     scale = HEAD_WIDTH ** (-0.5) * LOG2E
-    columns = x_ref.shape[0] // 2
-    tokens = kv_ref.shape[1] // 2
+    columns = y_ref.shape[0] // 2
+    tokens = kv_refs[0].shape[0] // 2
     rows = columns * SLOTS
-    lse = []
-    for g in range(QUERY_PER_KEY):
+    x = x_ref[:columns].astype(jnp.float32) + x_ref[columns:].astype(jnp.float32)
+    x = x.reshape(rows, FEAT).astype(jnp.bfloat16)
+    q = [x[:, g * HEAD_WIDTH : (g + 1) * HEAD_WIDTH] for g in range(QUERY_PER_KEY)]
+    q = jnp.concatenate(q, axis=0)
+    ones = jnp.ones((tokens, HEAD_WIDTH), jnp.bfloat16)
+    tops, sums = [], []
+    for kv_ref in kv_refs:
+        k = kv_ref[:tokens]
+        v = jnp.concatenate([kv_ref[tokens:], ones], axis=1)
+        s = lax.dot_general(q, k, (((1,), (1,)), ((), ())), preferred_element_type=jnp.float32)
+        m = jnp.max(s, axis=1, keepdims=True)
+        w = jnp.exp2((s - m) * scale).astype(jnp.bfloat16)
+        tops.append(m)
+        sums.append(jnp.dot(w, v, preferred_element_type=jnp.float32))
+    top = functools.reduce(jnp.maximum, tops)
+    both = functools.reduce(jnp.add, [jnp.exp2((m - top) * scale) * x for m, x in zip(tops, sums)])
+    total = both[:, HEAD_WIDTH:]
+    out = both[:, :HEAD_WIDTH] / total
+    lse = top * scale + jnp.log2(total[:, :1])
+    ends = []
+    for g in range(QUERY_PER_KEY):
+        part = out[g * rows : (g + 1) * rows].reshape(columns, SLOTS, HEAD_WIDTH).astype(jnp.bfloat16)
         lanes = slice(g * HEAD_WIDTH, (g + 1) * HEAD_WIDTH)
-        q = x_ref[:columns, :, lanes].astype(jnp.float32) + x_ref[columns:, :, lanes].astype(jnp.float32)
-        q = q.reshape(rows, HEAD_WIDTH).astype(jnp.bfloat16)
-        tops, totals, sums = [], [], []
-        for slab in range(kv_ref.shape[0]):
-            k = kv_ref[slab, :tokens]
-            v = kv_ref[slab, tokens:]
-            s = lax.dot_general(q, k, (((1,), (1,)), ((), ())), preferred_element_type=jnp.float32)
-            m = jnp.max(s, axis=1, keepdims=True)
-            w = jnp.exp2((s - m) * scale)
-            tops.append(m)
-            totals.append(jnp.sum(w, axis=1, keepdims=True))
-            sums.append(jnp.dot(w.astype(jnp.bfloat16), v, preferred_element_type=jnp.float32))
-        top = functools.reduce(jnp.maximum, tops)
-        weights = [jnp.exp2((m - top) * scale) for m in tops]
-        total = functools.reduce(jnp.add, [w * t for w, t in zip(weights, totals)])
-        out = functools.reduce(jnp.add, [w * o for w, o in zip(weights, sums)]) / total
-        out = out.reshape(columns, SLOTS, HEAD_WIDTH).astype(jnp.bfloat16)
-        y_ref[:columns, :, lanes] = out
-        y_ref[columns:, :, lanes] = out
-        lse.append(top * scale + jnp.log2(total))
-    stat = stat_lanes(lse).reshape(columns, SLOTS, STAT).astype(jnp.bfloat16)
+        y_ref[:columns, :, lanes] = part
+        y_ref[columns:, :, lanes] = part
+        ends.append(lse[g * rows : (g + 1) * rows])
+    stat = stat_lanes(ends).reshape(columns, SLOTS, STAT).astype(jnp.bfloat16)
     y_ref[:columns, :, FEAT:] = stat
     y_ref[columns:, :, FEAT:] = stat
 
@@ -155,7 +160,6 @@
     tokens = keys.shape[0]
     slabs = BLOCK // tokens
     along_z = [[2 * z + c for z in range(count_z)] for c in range(2)]
-    block_devices = [list(range(start, start + slabs)) for start in range(0, count_y, slabs)]
     plane = 2 * count_y
     planes = [list(range(z * plane, (z + 1) * plane)) for z in range(count_z)]
 
@@ -171,12 +175,22 @@
     pos = lax.dynamic_index_in_dim(pos, core, 2, keepdims=False)
     pos = jnp.repeat(pos, KEY_HEADS, axis=1)
 
-    rows = lax.all_gather(queries.reshape(KEY_HEADS, FEAT), "sx", axis=0, axis_index_groups=along_z)
-    kv = call(relay_kernel, (KEY_HEADS, 2 * tokens, HEAD_WIDTH), jnp.bfloat16, "relay", keys, values)
-    kv = exchange(kv, "sy", block_devices)
+    own = jnp.broadcast_to(queries.reshape(1, KEY_HEADS, FEAT), (count_z, KEY_HEADS, FEAT))
+    rows = exchange(own, "sx", along_z)
+    me = (index_y % slabs).astype(jnp.int32).reshape(1)
+    vmem = pl.BlockSpec(memory_space=pltpu.VMEM)
+    kv = pl.pallas_call(
+        relay_kernel,
+        out_shape=[jax.ShapeDtypeStruct((2 * tokens, HEAD_WIDTH), jnp.bfloat16)] * slabs,
+        in_specs=[pl.BlockSpec(memory_space=pltpu.SMEM), vmem, vmem],
+        out_specs=[vmem] * slabs,
+        compiler_params=pltpu.CompilerParams(vmem_limit_bytes=40 * 1024 * 1024),
+        name="relay",
+    )(me, keys, values)
+    kv = [kv[0]] + [lax.ppermute(kv[i], "sy", [(d, d ^ i) for d in range(count_y)]) for i in range(1, slabs)]
     asked = call(select_kernel, (plane, SLOTS, FEAT), jnp.bfloat16, "select", pos, rows)
     asked = exchange(asked, ("sx", "sy"), planes)
-    part = call(attend_kernel, (plane, SLOTS, FEAT + STAT), jnp.bfloat16, "attend", asked, kv)
+    part = call(attend_kernel, (plane, SLOTS, FEAT + STAT), jnp.bfloat16, "attend", asked, *kv)
     part = exchange(part, ("sx", "sy"), planes)
     part = call(merge_kernel, (count_z, KEY_HEADS, FEAT + STAT), jnp.bfloat16, "merge", pos, part)
     part = exchange(part, "sx", along_z)

time: 132 us -> 110 us (0.83)
  blocking collectives: 101 us -> 39.6 us
  starting transfers between devices: 7.32 us -> 47.4 us
  Pallas kernels: 11.6 us -> 6.98 us
  local copies, waits for them, and re-layouts: 3.55 us -> 5.45 us
  waiting for transfers between devices: 7.49 us -> 9.13 us
    all_gather x1 -> x0, blocking collectives: 34 us -> none  [per_device(): lax.all_gather(queries.reshape(KEY_HEADS, FEAT), 'sx', axis=0, axis_index...]
    all_to_all x3 -> x2, blocking collectives: 66.8 us -> 39.6 us  [exchange(): lax.all_to_all(x, axis, split_axis=0, concat_axis=0, tiled=True, axis_ind...]
    ppermute x0 -> x7, starting transfers between devices: none -> 25.1 us  [per_device(): lax.ppermute(kv[i], 'sy', [(d, d ^ i) for d in range(count_y)])]
    all_to_all x1 -> x2, starting transfers between devices: 7.32 us -> 22.3 us  [exchange(): lax.all_to_all(x, axis, split_axis=0, concat_axis=0, tiled=True, axis_ind...]
    pallas_call x5 -> x4, Pallas kernels: 11.6 us -> 5.75 us  [call(): pl.pallas_call(kernel, out_shape=jax.ShapeDtypeStruct(shape, dtype), in_s...]
    ppermute x0 -> x7, waiting for transfers between devices: none -> 1.35 us  [per_device(): lax.ppermute(kv[i], 'sy', [(d, d ^ i) for d in range(count_y)])]
    all_to_all x1 -> x2, waiting for transfers between devices: 7.49 us -> 7.78 us  [exchange(): lax.all_to_all(x, axis, split_axis=0, concat_axis=0, tiled=True, axis_ind...]
  transfers between devices with their start and end apart: 1 -> 9, of which waited for: 1 -> 2; matrix products, arithmetic and copies ran while one was open for 0% -> 2% of each run, Pallas kernels for 0% -> 2%
where the time goes in v5:
time: 110 us
  starting transfers between devices  47.4 us (43%)
  blocking collectives  39.6 us (36%)
  waiting for transfers between devices  9.13 us (8%)
  Pallas kernels  6.98 us (6%)
  local copies, waits for them, and re-layouts  5.45 us (5%)
    all_to_all x2, blocking collectives, exchange(): lax.all_to_all(x, axis, split_axis=0, concat_axis=0, tiled=True, axis_ind...  39.6 us
    ppermute x7, starting transfers between devices, per_device(): lax.ppermute(kv[i], 'sy', [(d, d ^ i) for d in range(count_y)])  25.1 us
    all_to_all x2, starting transfers between devices, exchange(): lax.all_to_all(x, axis, split_axis=0, concat_axis=0, tiled=True, axis_ind...  22.3 us
    all_to_all x2, waiting for transfers between devices, exchange(): lax.all_to_all(x, axis, split_axis=0, concat_axis=0, tiled=True, axis_ind...  7.78 us
    pallas_call x4, Pallas kernels, call(): pl.pallas_call(kernel, out_shape=jax.ShapeDtypeStruct(shape, dtype), in_s...  5.75 us
    unnamed x5, local copies, waits for them, and re-layouts  3.06 us
  transfers between devices with their start and end apart: 9, of which 2 were waited for; matrix products, arithmetic and copies ran while one was open for 2% of the time, Pallas kernels for 2%

profile of v5, /device:TPU:32, one launch (start us, length us, event | category | flops | bytes accessed | tf_op | source)
XLA Modules:
  0.0 109.8 jit_solution(2896348625902011054)
XLA Ops:
  0.0 0.8 reduce.1
  0.8 0.7 broadcast_in_dim.23
  1.5 15.2 %all-to-all-start = ((bf16[16,8,512]{2,1,0:T(8,128)(2,1)}), bf16[16,8,512]{2,1,0:T(8,128)(2,1)S(1)}, u32[]{:S(2)}, u32[]{:S(2)}) async-start(bf16[16,8,512]{2,1,0:T(8,128)(2,1)} %broadcast_in_dim.23), calls=%async_computation | async-start | bytes 262144 | tf_op jit(solution)/shard_map/all_to_all | solution.py:167
  16.7 1.2 %copy-done = bf16[512,1024]{1,0:T(8,128)(2,1)S(1)} copy-done((bf16[512,1024]{1,0:T(8,128)(2,1)S(1)}, bf16[512,1024]{1,0:T(8,128)(2,1)}, u32[]{:S(2)}) %copy-start) | copy-done | bytes 1048600
  17.9 1.2 %copy-done.1 = bf16[512,1024]{1,0:T(8,128)(2,1)S(1)} copy-done((bf16[512,1024]{1,0:T(8,128)(2,1)S(1)}, bf16[512,1024]{1,0:T(8,128)(2,1)}, u32[]{:S(2)}) %copy-start.1) | copy-done | bytes 1048600
  19.1 1.2 %relay.1 = (bf16[1024,128]{1,0:T(8,128)(2,1)S(1)}, bf16[1024,128]{1,0:T(8,128)(2,1)S(1)}, bf16[1024,128]{1,0:T(8,128)(2,1)S(1)}, bf16[1024,128]{1,0:T(8,128)(2,1...) custom-call(s32[1]{0:T(128)} %bitcast.2.me_ref, ...), custom_call_target="tpu_custom_call" | custom-call | tf_op jit(solution)/shard_map/relay/pallas_call | solution.py:182
  20.4 3.4 %collective-permute-start = (bf16[1024,128]{1,0:T(8,128)(2,1)S(1)}, bf16[1024,128]{1,0:T(8,128)(2,1)S(1)}, u32[]{:S(2)}, u32[]{:S(2)}) collective-permute-start(bf16[1024,128]{1,0:T(8,128)(2,1)S(1)} %get-tuple-element.14), channel_id=1, source_target_pairs={{0,1},{1,0},{2,3},{3,2},{4,5},{5,4},{6,7},{7,6},{8,9},{9,8},{10,11... | collective-permute-start | bytes 786440 | tf_op jit(solution)/shard_map/ppermute | solution.py:190
  23.8 4.6 %collective-permute-start.1 = (bf16[1024,128]{1,0:T(8,128)(2,1)S(1)}, bf16[1024,128]{1,0:T(8,128)(2,1)S(1)}, u32[]{:S(2)}, u32[]{:S(2)}) collective-permute-start(bf16[1024,128]{1,0:T(8,128)(2,1)S(1)} %get-tuple-element.15), channel_id=1, source_target_pairs={{0,2},{1,3},{2,0},{3,1},{4,6},{5,7},{6,4},{7,5},{8,10},{9,11},{10,... | collective-permute-start | bytes 786440 | tf_op jit(solution)/shard_map/ppermute | solution.py:190
  28.4 2.4 %collective-permute-start.2 = (bf16[1024,128]{1,0:T(8,128)(2,1)}, bf16[1024,128]{1,0:T(8,128)(2,1)S(1)}, u32[]{:S(2)}, u32[]{:S(2)}) collective-permute-start(bf16[1024,128]{1,0:T(8,128)(2,1)} %get-tuple-element.16), channel_id=1, source_target_pairs={{0,3},{1,2},{2,1},{3,0},{4,7},{5,6},{6,5},{7,4},{8,11},{9,10},{10,... | collective-permute-start | bytes 786440 | tf_op jit(solution)/shard_map/ppermute | solution.py:190
  30.8 3.5 %collective-permute-start.3 = (bf16[1024,128]{1,0:T(8,128)(2,1)S(1)}, bf16[1024,128]{1,0:T(8,128)(2,1)S(1)}, u32[]{:S(2)}, u32[]{:S(2)}) collective-permute-start(bf16[1024,128]{1,0:T(8,128)(2,1)S(1)} %get-tuple-element.17), channel_id=1, source_target_pairs={{0,4},{1,5},{2,6},{3,7},{4,0},{5,1},{6,2},{7,3},{8,12},{9,13},{10,... | collective-permute-start | bytes 786440 | tf_op jit(solution)/shard_map/ppermute | solution.py:190
  34.3 2.1 %collective-permute-start.4 = (bf16[1024,128]{1,0:T(8,128)(2,1)S(1)}, bf16[1024,128]{1,0:T(8,128)(2,1)S(1)}, u32[]{:S(2)}, u32[]{:S(2)}) collective-permute-start(bf16[1024,128]{1,0:T(8,128)(2,1)S(1)} %get-tuple-element.18), channel_id=1, source_target_pairs={{0,5},{1,4},{2,7},{3,6},{4,1},{5,0},{6,3},{7,2},{8,13},{9,12},{10,... | collective-permute-start | bytes 786440 | tf_op jit(solution)/shard_map/ppermute | solution.py:190
  36.4 0.9 reshape.38
  37.3 0.5 dynamic-slice_reduce_fusion
  37.7 0.1 compare_reduce_fusion
  37.9 0.2 convert_reduce_fusion
  38.0 0.1 copy.10
  38.1 6.9 %collective-permute-start.5 = (bf16[1024,128]{1,0:T(8,128)(2,1)S(1)}, bf16[1024,128]{1,0:T(8,128)(2,1)S(1)}, u32[]{:S(2)}, u32[]{:S(2)}) collective-permute-start(bf16[1024,128]{1,0:T(8,128)(2,1)S(1)} %get-tuple-element.19), channel_id=1, source_target_pairs={{0,6},{1,7},{2,4},{3,5},{4,2},{5,3},{6,0},{7,1},{8,14},{9,15},{10,... | collective-permute-start | bytes 786440 | tf_op jit(solution)/shard_map/ppermute | solution.py:190
  45.0 0.0 collective-permute-done.1.refs_2_
  45.0 2.3 %collective-permute-start.6 = (bf16[1024,128]{1,0:T(8,128)(2,1)S(1)}, bf16[1024,128]{1,0:T(8,128)(2,1)S(1)}, u32[]{:S(2)}, u32[]{:S(2)}) collective-permute-start(bf16[1024,128]{1,0:T(8,128)(2,1)S(1)} %get-tuple-element.20), channel_id=1, source_target_pairs={{0,7},{1,6},{2,5},{3,4},{4,3},{5,2},{6,1},{7,0},{8,15},{9,14},{10,... | collective-permute-start | bytes 786440 | tf_op jit(solution)/shard_map/ppermute | solution.py:190
  47.3 0.1 copy.11
  47.4 0.1 broadcast_in_dim.11
  47.5 0.1 reshape.39.pos_ref
  47.6 0.9 select.9
  48.5 7.1 %all-to-all-start.1 = ((bf16[32,8,512]{2,1,0:T(8,128)(2,1)}), bf16[32,8,512]{2,1,0:T(8,128)(2,1)S(1)}, u32[]{:S(2)}, u32[]{:S(2)}) async-start(bf16[32,8,512]{2,1,0:T(8,128)(2,1)} %select.9), calls=%async_computation.1 | async-start | bytes 524288 | tf_op jit(solution)/shard_map/all_to_all | solution.py:167
  55.6 1.3 %collective-permute-done.6.refs_7_ = bf16[1024,128]{1,0:T(8,128)(2,1)S(1)} collective-permute-done((bf16[1024,128]{1,0:T(8,128)(2,1)S(1)}, bf16[1024,128]{1,0:T(8,128)(2,1)S(1)}, u32[]{:S(2)}, u32[]{:S(2)}) %collective-permute-start.6) | collective-permute-done | bytes 262176 | tf_op jit(solution)/shard_map/ppermute | solution.py:190
  56.9 7.8 %all-to-all-done.1.x_ref = bf16[32,8,512]{2,1,0:T(8,128)(2,1)S(1)} async-done(((bf16[32,8,512]{2,1,0:T(8,128)(2,1)}), bf16[32,8,512]{2,1,0:T(8,128)(2,1)S(1)}, u32[]{:S(2)}, u32[]{:S(2)}) %all-to-all-start.1) | async-done | bytes 262176 | tf_op jit(solution)/shard_map/all_to_all | solution.py:167
  64.7 3.2 %attend.1 = bf16[32,8,640]{2,1,0:T(8,128)(2,1)S(1)} custom-call(bf16[32,8,512]{2,1,0:T(8,128)(2,1)S(1)} %all-to-all-done.1.x_ref, bf16[1024,128]{1,0:T(8,128)(2,1)S(1)} %get-tuple-element.13.refs_0_, bf16[1024,128]{1,0:T(8,128)(2,1)S(1)} %collective-permute-done.refs_1_, bf16[1024,128]{1,0:T(8,128)(2,1)S(1)} %collective-permute-done.1.refs_2_, ...), custom_call_target="tpu_custom_call" | custom-call | tf_op jit(solution)/shard_map/attend/pallas_call | solution.py:143
  67.9 13.1 %all_to_all.20.y_ref = bf16[32,8,640]{2,1,0:T(8,128)(2,1)S(1)} all-to-all(bf16[32,8,640]{2,1,0:T(8,128)(2,1)S(1)} %attend.1), channel_id=1, replica_groups={{0,1,2,3,4,5,6,7,8,9,10,11,12,13,14,15,16,17,18,19,20,21,22,23,24,25,26..., dimensions={0} | all-to-all | bytes 655360 | tf_op jit(solution)/shard_map/all_to_all | solution.py:167
  81.0 1.3 %merge.1 = bf16[16,8,640]{2,1,0:T(8,128)(2,1)S(1)} custom-call(s32[4,128]{1,0:T(4,128)S(1)} %reshape.39.pos_ref, bf16[32,8,640]{2,1,0:T(8,128)(2,1)S(1)} %all_to_all.20.y_ref), custom_call_target="tpu_custom_call" | custom-call | tf_op jit(solution)/shard_map/merge/pallas_call | solution.py:143
  82.3 26.5 %all_to_all.21.a_ref = bf16[16,8,640]{2,1,0:T(8,128)(2,1)S(1)} all-to-all(bf16[16,8,640]{2,1,0:T(8,128)(2,1)S(1)} %merge.1), channel_id=1, replica_groups={{0,32,64,96,128,160,192,224,256,288,320,352,384,416,448,480},{16,48,80,..., dimensions={0} | all-to-all | bytes 327680 | tf_op jit(solution)/shard_map/all_to_all | solution.py:167
  108.8 0.3 last.1
  109.1 0.6 copy.12
  (13 shorter events, 0.1 us)
Async XLA Ops:
  1.5 46.1 %all-to-all-start = ((bf16[16,8,512]{2,1,0:T(8,128)(2,1)}), bf16[16,8,512]{2,1,0:T(8,128)(2,1)S(1)}, u32[]{:S(2)}, u32[]{:S(2)}) async-start(bf16[16,8,512]{2,1,0:T(8,128)(2,1)} %broadcast_in_dim.23), calls=%async_computation | async-start | bytes 262144 | tf_op jit(solution)/shard_map/all_to_all | solution.py:167
  16.7 1.2 %copy-start = (bf16[512,1024]{1,0:T(8,128)(2,1)S(1)}, bf16[512,1024]{1,0:T(8,128)(2,1)}, u32[]{:S(2)}) copy-start(bf16[512,1024]{1,0:T(8,128)(2,1)} %k_ref.1) | copy-start | bytes 3145732
  17.9 1.2 %copy-start.1 = (bf16[512,1024]{1,0:T(8,128)(2,1)S(1)}, bf16[512,1024]{1,0:T(8,128)(2,1)}, u32[]{:S(2)}) copy-start(bf16[512,1024]{1,0:T(8,128)(2,1)} %v_ref.1) | copy-start | bytes 3145732
  20.4 17.8 %collective-permute-start = (bf16[1024,128]{1,0:T(8,128)(2,1)S(1)}, bf16[1024,128]{1,0:T(8,128)(2,1)S(1)}, u32[]{:S(2)}, u32[]{:S(2)}) collective-permute-start(bf16[1024,128]{1,0:T(8,128)(2,1)S(1)} %get-tuple-element.14), channel_id=1, source_target_pairs={{0,1},{1,0},{2,3},{3,2},{4,5},{5,4},{6,7},{7,6},{8,9},{9,8},{10,11... | collective-permute-start | bytes 786440 | tf_op jit(solution)/shard_map/ppermute | solution.py:190
  23.8 21.2 %collective-permute-start.1 = (bf16[1024,128]{1,0:T(8,128)(2,1)S(1)}, bf16[1024,128]{1,0:T(8,128)(2,1)S(1)}, u32[]{:S(2)}, u32[]{:S(2)}) collective-permute-start(bf16[1024,128]{1,0:T(8,128)(2,1)S(1)} %get-tuple-element.15), channel_id=1, source_target_pairs={{0,2},{1,3},{2,0},{3,1},{4,6},{5,7},{6,4},{7,5},{8,10},{9,11},{10,... | collective-permute-start | bytes 786440 | tf_op jit(solution)/shard_map/ppermute | solution.py:190
  28.4 27.1 %collective-permute-start.2 = (bf16[1024,128]{1,0:T(8,128)(2,1)}, bf16[1024,128]{1,0:T(8,128)(2,1)S(1)}, u32[]{:S(2)}, u32[]{:S(2)}) collective-permute-start(bf16[1024,128]{1,0:T(8,128)(2,1)} %get-tuple-element.16), channel_id=1, source_target_pairs={{0,3},{1,2},{2,1},{3,0},{4,7},{5,6},{6,5},{7,4},{8,11},{9,10},{10,... | collective-permute-start | bytes 786440 | tf_op jit(solution)/shard_map/ppermute | solution.py:190
  30.8 24.8 %collective-permute-start.3 = (bf16[1024,128]{1,0:T(8,128)(2,1)S(1)}, bf16[1024,128]{1,0:T(8,128)(2,1)S(1)}, u32[]{:S(2)}, u32[]{:S(2)}) collective-permute-start(bf16[1024,128]{1,0:T(8,128)(2,1)S(1)} %get-tuple-element.17), channel_id=1, source_target_pairs={{0,4},{1,5},{2,6},{3,7},{4,0},{5,1},{6,2},{7,3},{8,12},{9,13},{10,... | collective-permute-start | bytes 786440 | tf_op jit(solution)/shard_map/ppermute | solution.py:190
  34.3 21.3 %collective-permute-start.4 = (bf16[1024,128]{1,0:T(8,128)(2,1)S(1)}, bf16[1024,128]{1,0:T(8,128)(2,1)S(1)}, u32[]{:S(2)}, u32[]{:S(2)}) collective-permute-start(bf16[1024,128]{1,0:T(8,128)(2,1)S(1)} %get-tuple-element.18), channel_id=1, source_target_pairs={{0,5},{1,4},{2,7},{3,6},{4,1},{5,0},{6,3},{7,2},{8,13},{9,12},{10,... | collective-permute-start | bytes 786440 | tf_op jit(solution)/shard_map/ppermute | solution.py:190
  38.1 17.5 %collective-permute-start.5 = (bf16[1024,128]{1,0:T(8,128)(2,1)S(1)}, bf16[1024,128]{1,0:T(8,128)(2,1)S(1)}, u32[]{:S(2)}, u32[]{:S(2)}) collective-permute-start(bf16[1024,128]{1,0:T(8,128)(2,1)S(1)} %get-tuple-element.19), channel_id=1, source_target_pairs={{0,6},{1,7},{2,4},{3,5},{4,2},{5,3},{6,0},{7,1},{8,14},{9,15},{10,... | collective-permute-start | bytes 786440 | tf_op jit(solution)/shard_map/ppermute | solution.py:190
  45.0 11.9 %collective-permute-start.6 = (bf16[1024,128]{1,0:T(8,128)(2,1)S(1)}, bf16[1024,128]{1,0:T(8,128)(2,1)S(1)}, u32[]{:S(2)}, u32[]{:S(2)}) collective-permute-start(bf16[1024,128]{1,0:T(8,128)(2,1)S(1)} %get-tuple-element.20), channel_id=1, source_target_pairs={{0,7},{1,6},{2,5},{3,4},{4,3},{5,2},{6,1},{7,0},{8,15},{9,14},{10,... | collective-permute-start | bytes 786440 | tf_op jit(solution)/shard_map/ppermute | solution.py:190
  48.5 16.2 %all-to-all-start.1 = ((bf16[32,8,512]{2,1,0:T(8,128)(2,1)}), bf16[32,8,512]{2,1,0:T(8,128)(2,1)S(1)}, u32[]{:S(2)}, u32[]{:S(2)}) async-start(bf16[32,8,512]{2,1,0:T(8,128)(2,1)} %select.9), calls=%async_computation.1 | async-start | bytes 524288 | tf_op jit(solution)/shard_map/all_to_all | solution.py:167

commit v6 on v5

--- a/solution.py
+++ b/solution.py
@@ -20,6 +20,14 @@
 ONE_LANE = 12
 SLOTS = 8
 
+HEADS = 2
+PARTNERS = (0, 1, 4, 5)
+HALVES = ((0, 1, 4, 5), (2, 3, 6, 7))
+
+
+def heads_of(s):
+    return ((s // 4) * 2 + s % 2) * HEADS
+
 
 def pieces(x):
     hi = x.astype(jnp.bfloat16).astype(jnp.float32)
@@ -45,11 +53,11 @@
     return jnp.where(hit, 1.0, 0.0).astype(jnp.bfloat16)
 
 
-def relay_kernel(me_ref, k_ref, v_ref, *out_refs):
+def relay_kernel(at_ref, k_ref, v_ref, *out_refs):
     tokens = k_ref.shape[0]
+    width = out_refs[0].shape[1]
     for i, out_ref in enumerate(out_refs):
-        head = jnp.bitwise_xor(me_ref[0], i)
-        lanes = pl.ds(pl.multiple_of(head * HEAD_WIDTH, HEAD_WIDTH), HEAD_WIDTH)
+        lanes = pl.ds(pl.multiple_of(at_ref[i] * width, width), width)
         out_ref[:tokens] = k_ref[:, lanes]
         out_ref[tokens:] = v_ref[:, lanes]
 
@@ -58,9 +66,10 @@
     q = q_ref[...].astype(jnp.float32).reshape(-1, FEAT).astype(jnp.bfloat16)
     for b in range(4):
         hot = slot_onehot(pos_ref[b : b + 1, :])
-        picked = jnp.dot(hot, q, preferred_element_type=jnp.float32)
-        picked = picked.reshape(KEY_HEADS, SLOTS, FEAT).astype(jnp.bfloat16)
-        out_ref[b * KEY_HEADS : (b + 1) * KEY_HEADS] = picked
+        picked = jnp.dot(hot, q, preferred_element_type=jnp.float32).astype(jnp.bfloat16)
+        for s in range(8):
+            first = heads_of(s) * SLOTS
+            out_ref[b * 8 + s] = picked[first : first + HEADS * SLOTS]
 
 
 def attend_kernel(x_ref, *refs):
@@ -69,45 +78,49 @@
     columns = y_ref.shape[0] // 2
     tokens = kv_refs[0].shape[0] // 2
     rows = columns * SLOTS
+    ones = jnp.ones((tokens, HEAD_WIDTH), jnp.bfloat16)
     x = x_ref[:columns].astype(jnp.float32) + x_ref[columns:].astype(jnp.float32)
-    x = x.reshape(rows, FEAT).astype(jnp.bfloat16)
-    q = [x[:, g * HEAD_WIDTH : (g + 1) * HEAD_WIDTH] for g in range(QUERY_PER_KEY)]
-    q = jnp.concatenate(q, axis=0)
-    ones = jnp.ones((tokens, HEAD_WIDTH), jnp.bfloat16)
-    tops, sums = [], []
-    for kv_ref in kv_refs:
-        k = kv_ref[:tokens]
-        v = jnp.concatenate([kv_ref[tokens:], ones], axis=1)
-        s = lax.dot_general(q, k, (((1,), (1,)), ((), ())), preferred_element_type=jnp.float32)
-        m = jnp.max(s, axis=1, keepdims=True)
-        w = jnp.exp2((s - m) * scale).astype(jnp.bfloat16)
-        tops.append(m)
-        sums.append(jnp.dot(w, v, preferred_element_type=jnp.float32))
-    top = functools.reduce(jnp.maximum, tops)
-    both = functools.reduce(jnp.add, [jnp.exp2((m - top) * scale) * x for m, x in zip(tops, sums)])
-    total = both[:, HEAD_WIDTH:]
-    out = both[:, :HEAD_WIDTH] / total
-    lse = top * scale + jnp.log2(total[:, :1])
-    ends = []
-    for g in range(QUERY_PER_KEY):
-        part = out[g * rows : (g + 1) * rows].reshape(columns, SLOTS, HEAD_WIDTH).astype(jnp.bfloat16)
-        lanes = slice(g * HEAD_WIDTH, (g + 1) * HEAD_WIDTH)
-        y_ref[:columns, :, lanes] = part
-        y_ref[columns:, :, lanes] = part
-        ends.append(lse[g * rows : (g + 1) * rows])
-    stat = stat_lanes(ends).reshape(columns, SLOTS, STAT).astype(jnp.bfloat16)
-    y_ref[:columns, :, FEAT:] = stat
-    y_ref[columns:, :, FEAT:] = stat
+    for h in range(HEADS):
+        q = x[:, h * SLOTS : (h + 1) * SLOTS].reshape(rows, FEAT).astype(jnp.bfloat16)
+        q = [q[:, g * HEAD_WIDTH : (g + 1) * HEAD_WIDTH] for g in range(QUERY_PER_KEY)]
+        q = jnp.concatenate(q, axis=0)
+        own = slice(h * HEAD_WIDTH, (h + 1) * HEAD_WIDTH)
+        tops, sums = [], []
+        for kv_ref in kv_refs:
+            k = kv_ref[:tokens, own]
+            v = jnp.concatenate([kv_ref[tokens:, own], ones], axis=1)
+            s = lax.dot_general(q, k, (((1,), (1,)), ((), ())), preferred_element_type=jnp.float32)
+            m = jnp.max(s, axis=1, keepdims=True)
+            w = jnp.exp2((s - m) * scale).astype(jnp.bfloat16)
+            tops.append(m)
+            sums.append(jnp.dot(w, v, preferred_element_type=jnp.float32))
+        top = functools.reduce(jnp.maximum, tops)
+        both = functools.reduce(jnp.add, [jnp.exp2((m - top) * scale) * x for m, x in zip(tops, sums)])
+        total = both[:, HEAD_WIDTH:]
+        out = both[:, :HEAD_WIDTH] / total
+        lse = top * scale + jnp.log2(total[:, :1])
+        slots = slice(h * SLOTS, (h + 1) * SLOTS)
+        ends = []
+        for g in range(QUERY_PER_KEY):
+            part = out[g * rows : (g + 1) * rows].reshape(columns, SLOTS, HEAD_WIDTH).astype(jnp.bfloat16)
+            lanes = slice(g * HEAD_WIDTH, (g + 1) * HEAD_WIDTH)
+            y_ref[:columns, slots, lanes] = part
+            y_ref[columns:, slots, lanes] = part
+            ends.append(lse[g * rows : (g + 1) * rows])
+        stat = stat_lanes(ends).reshape(columns, SLOTS, STAT).astype(jnp.bfloat16)
+        y_ref[:columns, slots, FEAT:] = stat
+        y_ref[columns:, slots, FEAT:] = stat
 
 
 def merge_kernel(pos_ref, y_ref, out_ref):
     flip = (((0,), (0,)), ((), ()))
     parts = []
     for b in range(4):
-        y = y_ref[b * KEY_HEADS : (b + 1) * KEY_HEADS].astype(jnp.float32)
-        y = y.reshape(KEY_HEADS * SLOTS, FEAT + STAT).astype(jnp.bfloat16)
         hot = slot_onehot(pos_ref[b : b + 1, :])
-        parts.append(lax.dot_general(hot, y, flip, preferred_element_type=jnp.float32))
+        for half in range(2):
+            y = [y_ref[b * 8 + s] for s in HALVES[half]]
+            y = jnp.concatenate(y, axis=0)
+            parts.append(lax.dot_general(hot, y, flip, preferred_element_type=jnp.float32))
     named = [x[:, FEAT + ONE_LANE : FEAT + ONE_LANE + 1] > 0.5 for x in parts]
     shape = out_ref.shape[:-1]
     ends = []
@@ -177,20 +190,21 @@
 
     own = jnp.broadcast_to(queries.reshape(1, KEY_HEADS, FEAT), (count_z, KEY_HEADS, FEAT))
     rows = exchange(own, "sx", along_z)
-    me = (index_y % slabs).astype(jnp.int32).reshape(1)
+    me = (index_y % slabs).astype(jnp.int32)
+    at = jnp.stack([heads_of(jnp.bitwise_xor(me, i)) // HEADS for i in PARTNERS])
     vmem = pl.BlockSpec(memory_space=pltpu.VMEM)
     kv = pl.pallas_call(
         relay_kernel,
-        out_shape=[jax.ShapeDtypeStruct((2 * tokens, HEAD_WIDTH), jnp.bfloat16)] * slabs,
+        out_shape=[jax.ShapeDtypeStruct((2 * tokens, HEADS * HEAD_WIDTH), jnp.bfloat16)] * len(PARTNERS),
         in_specs=[pl.BlockSpec(memory_space=pltpu.SMEM), vmem, vmem],
-        out_specs=[vmem] * slabs,
+        out_specs=[vmem] * len(PARTNERS),
         compiler_params=pltpu.CompilerParams(vmem_limit_bytes=40 * 1024 * 1024),
         name="relay",
-    )(me, keys, values)
-    kv = [kv[0]] + [lax.ppermute(kv[i], "sy", [(d, d ^ i) for d in range(count_y)]) for i in range(1, slabs)]
-    asked = call(select_kernel, (plane, SLOTS, FEAT), jnp.bfloat16, "select", pos, rows)
+    )(at, keys, values)
+    swaps = [lax.ppermute(x, "sy", [(d, d ^ i) for d in range(count_y)]) for i, x in zip(PARTNERS[1:], kv[1:])]
+    asked = call(select_kernel, (plane, HEADS * SLOTS, FEAT), jnp.bfloat16, "select", pos, rows)
     asked = exchange(asked, ("sx", "sy"), planes)
-    part = call(attend_kernel, (plane, SLOTS, FEAT + STAT), jnp.bfloat16, "attend", asked, *kv)
+    part = call(attend_kernel, (plane, HEADS * SLOTS, FEAT + STAT), jnp.bfloat16, "attend", asked, kv[0], *swaps)
     part = exchange(part, ("sx", "sy"), planes)
     part = call(merge_kernel, (count_z, KEY_HEADS, FEAT + STAT), jnp.bfloat16, "merge", pos, part)
     part = exchange(part, "sx", along_z)

time: 110 us -> 110 us (level)
  starting transfers between devices: 47.4 us -> 31.9 us
  waiting for transfers between devices: 9.13 us -> 18.8 us
  blocking collectives: 39.6 us -> 44 us
  Pallas kernels: 6.98 us -> 8.61 us
    ppermute x7 -> x3, starting transfers between devices: 25.1 us -> 9.33 us  [per_device(): lax.ppermute(x, 'sy', [(d, d ^ i) for d in range(count_y)])]
    ppermute x7 -> x3, waiting for transfers between devices: 1.35 us -> 14.9 us  [per_device(): lax.ppermute(x, 'sy', [(d, d ^ i) for d in range(count_y)])]
    all_to_all x2, blocking collectives: 39.6 us -> 44 us  [exchange(): lax.all_to_all(x, axis, split_axis=0, concat_axis=0, tiled=True, axis_ind...]
    all_to_all x2, waiting for transfers between devices: 7.78 us -> 3.85 us  [exchange(): lax.all_to_all(x, axis, split_axis=0, concat_axis=0, tiled=True, axis_ind...]
    unnamed x5 -> x7, local copies, waits for them, and re-layouts: 3.06 us -> 3.07 us
  transfers between devices with their start and end apart: 9 -> 5, of which waited for: 2 -> 2; matrix products, arithmetic and copies ran while one was open for 2% -> 1% of each run, Pallas kernels for 2% -> 3%
where the time goes in v6:
time: 110 us; the launch traced here: 109 us
  blocking collectives  44 us (40%)
  starting transfers between devices  31.9 us (29%)
  waiting for transfers between devices  18.8 us (17%)
  Pallas kernels  8.61 us (8%)
  local copies, waits for them, and re-layouts  4.68 us (4%)
  other arithmetic  1.1 us (1%)
    all_to_all x2, blocking collectives, exchange(): lax.all_to_all(x, axis, split_axis=0, concat_axis=0, tiled=True, axis_ind...  44 us
    all_to_all x2, starting transfers between devices, exchange(): lax.all_to_all(x, axis, split_axis=0, concat_axis=0, tiled=True, axis_ind...  22.5 us
    ppermute x3, waiting for transfers between devices, per_device(): lax.ppermute(x, 'sy', [(d, d ^ i) for d in range(count_y)])  14.9 us
    ppermute x3, starting transfers between devices, per_device(): lax.ppermute(x, 'sy', [(d, d ^ i) for d in range(count_y)])  9.33 us
    pallas_call x4, Pallas kernels, call(): pl.pallas_call(kernel, out_shape=jax.ShapeDtypeStruct(shape, dtype), in_s...  6.81 us
    all_to_all x2, waiting for transfers between devices, exchange(): lax.all_to_all(x, axis, split_axis=0, concat_axis=0, tiled=True, axis_ind...  3.85 us
    unnamed x7, local copies, waits for them, and re-layouts  3.07 us
  transfers between devices with their start and end apart: 5, of which 2 were waited for; matrix products, arithmetic and copies ran while one was open for 1% of the time, Pallas kernels for 3%

profile of v6, /device:TPU:32, one launch (start us, length us, event | category | flops | bytes accessed | tf_op | source)
XLA Modules:
  0.0 109.2 jit_solution(2638158640688666314)
XLA Ops:
  0.0 0.8 reduce.1
  0.8 0.7 broadcast_in_dim.23
  1.4 15.2 %all-to-all-start = ((bf16[16,8,512]{2,1,0:T(8,128)(2,1)}), bf16[16,8,512]{2,1,0:T(8,128)(2,1)S(1)}, u32[]{:S(2)}, u32[]{:S(2)}) async-start(bf16[16,8,512]{2,1,0:T(8,128)(2,1)} %broadcast_in_dim.23), calls=%async_computation | async-start | bytes 262144 | tf_op jit(solution)/shard_map/all_to_all | solution.py:180
  16.7 0.1 pad_add_fusion.at_ref
  16.7 1.2 %copy-done = bf16[512,1024]{1,0:T(8,128)(2,1)S(1)} copy-done((bf16[512,1024]{1,0:T(8,128)(2,1)S(1)}, bf16[512,1024]{1,0:T(8,128)(2,1)}, u32[]{:S(2)}) %copy-start) | copy-done | bytes 1048600
  18.0 1.2 %copy-done.1 = bf16[512,1024]{1,0:T(8,128)(2,1)S(1)} copy-done((bf16[512,1024]{1,0:T(8,128)(2,1)S(1)}, bf16[512,1024]{1,0:T(8,128)(2,1)}, u32[]{:S(2)}) %copy-start.1) | copy-done | bytes 1048600
  19.2 1.8 %relay.1 = (bf16[1024,256]{1,0:T(8,128)(2,1)S(1)}, bf16[1024,256]{1,0:T(8,128)(2,1)}, bf16[1024,256]{1,0:T(8,128)(2,1)}, bf16[1024,256]{1,0:T(8,128)(2,1)S(1)}) custom-call(s32[4]{0:T(128)S(1)} %pad_add_fusion.at_ref, bf16[512,1024]{1,0:T(8,128)(2,1)S(1)} %copy-done, bf16[512,1024]{1,0:T(8,128)(2,1)S(1)} %copy-done.1), custom_call_target="tpu_custom_call" | custom-call | tf_op jit(solution)/shard_map/relay/pallas_call | solution.py:196
  21.0 3.5 %collective-permute-start = (bf16[1024,256]{1,0:T(8,128)(2,1)}, bf16[1024,256]{1,0:T(8,128)(2,1)S(1)}, u32[]{:S(2)}, u32[]{:S(2)}) collective-permute-start(bf16[1024,256]{1,0:T(8,128)(2,1)} %get-tuple-element.10), channel_id=1, source_target_pairs={{0,1},{1,0},{2,3},{3,2},{4,5},{5,4},{6,7},{7,6},{8,9},{9,8},{10,11... | collective-permute-start | bytes 1572872 | tf_op jit(solution)/shard_map/ppermute | solution.py:204
  24.5 3.5 %collective-permute-start.1 = (bf16[1024,256]{1,0:T(8,128)(2,1)}, bf16[1024,256]{1,0:T(8,128)(2,1)S(1)}, u32[]{:S(2)}, u32[]{:S(2)}) collective-permute-start(bf16[1024,256]{1,0:T(8,128)(2,1)} %get-tuple-element.11), channel_id=1, source_target_pairs={{0,4},{1,5},{2,6},{3,7},{4,0},{5,1},{6,2},{7,3},{8,12},{9,13},{10,... | collective-permute-start | bytes 1572872 | tf_op jit(solution)/shard_map/ppermute | solution.py:204
  28.0 2.3 %collective-permute-start.2 = (bf16[1024,256]{1,0:T(8,128)(2,1)S(1)}, bf16[1024,256]{1,0:T(8,128)(2,1)S(1)}, u32[]{:S(2)}, u32[]{:S(2)}) collective-permute-start(bf16[1024,256]{1,0:T(8,128)(2,1)S(1)} %get-tuple-element.12), channel_id=1, source_target_pairs={{0,5},{1,4},{2,7},{3,6},{4,1},{5,0},{6,3},{7,2},{8,13},{9,12},{10,... | collective-permute-start | bytes 1572872 | tf_op jit(solution)/shard_map/ppermute | solution.py:204
  30.4 0.0 copy-done.2
  30.4 0.1 reshape.35
  30.5 0.5 dynamic-slice_reduce_fusion
  31.0 0.1 compare_reduce_fusion
  31.1 0.1 convert_reduce_fusion
  31.3 0.1 copy.10
  31.4 0.1 copy.11
  31.4 0.1 broadcast_in_dim.11
  31.5 0.1 reshape.36.pos_ref
  31.6 0.0 all-to-all-done.q_ref
  31.6 1.0 select.49
  32.7 7.3 %all-to-all-start.1 = ((bf16[32,16,512]{2,1,0:T(8,128)(2,1)}), bf16[32,16,512]{2,1,0:T(8,128)(2,1)S(1)}, u32[]{:S(2)}, u32[]{:S(2)}) async-start(bf16[32,16,512]{2,1,0:T(8,128)(2,1)} %select.49), calls=%async_computation.1 | async-start | bytes 1048576 | tf_op jit(solution)/shard_map/all_to_all | solution.py:180
  40.0 0.0 collective-permute-done.refs_1_
  40.0 14.9 %collective-permute-done.1.refs_2_ = bf16[1024,256]{1,0:T(8,128)(2,1)S(1)} collective-permute-done((bf16[1024,256]{1,0:T(8,128)(2,1)}, bf16[1024,256]{1,0:T(8,128)(2,1)S(1)}, u32[]{:S(2)}, u32[]{:S(2)}) %collective-permute-start.1) | collective-permute-done | bytes 524320 | tf_op jit(solution)/shard_map/ppermute | solution.py:204
  54.9 0.0 collective-permute-done.2.refs_3_
  54.9 3.9 %all-to-all-done.1.x_ref = bf16[32,16,512]{2,1,0:T(8,128)(2,1)S(1)} async-done(((bf16[32,16,512]{2,1,0:T(8,128)(2,1)}), bf16[32,16,512]{2,1,0:T(8,128)(2,1)S(1)}, u32[]{:S(2)}, u32[]{:S(2)}) %all-to-all-start.1) | async-done | bytes 524320 | tf_op jit(solution)/shard_map/all_to_all | solution.py:180
  58.8 3.2 %attend.1 = bf16[32,16,640]{2,1,0:T(8,128)(2,1)S(1)} custom-call(bf16[32,16,512]{2,1,0:T(8,128)(2,1)S(1)} %all-to-all-done.1.x_ref, bf16[1024,256]{1,0:T(8,128)(2,1)S(1)} %get-tuple-element.9.refs_0_, bf16[1024,256]{1,0:T(8,128)(2,1)S(1)} %collective-permute-done.refs_1_, bf16[1024,256]{1,0:T(8,128)(2,1)S(1)} %collective-permute-done.1.refs_2_, ...), custom_call_target="tpu_custom_call" | custom-call | tf_op jit(solution)/shard_map/attend/pallas_call | solution.py:156
  61.9 17.6 %all_to_all.20.y_ref = bf16[32,16,640]{2,1,0:T(8,128)(2,1)S(1)} all-to-all(bf16[32,16,640]{2,1,0:T(8,128)(2,1)S(1)} %attend.1), channel_id=1, replica_groups={{0,1,2,3,4,5,6,7,8,9,10,11,12,13,14,15,16,17,18,19,20,21,22,23,24,25,26..., dimensions={0} | all-to-all | bytes 1310720 | tf_op jit(solution)/shard_map/all_to_all | solution.py:180
  79.5 2.3 %merge.1 = bf16[16,8,640]{2,1,0:T(8,128)(2,1)S(1)} custom-call(s32[4,128]{1,0:T(4,128)S(1)} %reshape.36.pos_ref, bf16[32,16,640]{2,1,0:T(8,128)(2,1)S(1)} %all_to_all.20.y_ref), custom_call_target="tpu_custom_call" | custom-call | tf_op jit(solution)/shard_map/merge/pallas_call | solution.py:156
  81.8 26.4 %all_to_all.21.a_ref = bf16[16,8,640]{2,1,0:T(8,128)(2,1)S(1)} all-to-all(bf16[16,8,640]{2,1,0:T(8,128)(2,1)S(1)} %merge.1), channel_id=1, replica_groups={{0,32,64,96,128,160,192,224,256,288,320,352,384,416,448,480},{16,48,80,..., dimensions={0} | all-to-all | bytes 327680 | tf_op jit(solution)/shard_map/all_to_all | solution.py:180
  108.2 0.3 last.1
  108.6 0.6 copy.12
  (8 shorter events, 0.1 us)
Async XLA Ops:
  1.4 30.2 %all-to-all-start = ((bf16[16,8,512]{2,1,0:T(8,128)(2,1)}), bf16[16,8,512]{2,1,0:T(8,128)(2,1)S(1)}, u32[]{:S(2)}, u32[]{:S(2)}) async-start(bf16[16,8,512]{2,1,0:T(8,128)(2,1)} %broadcast_in_dim.23), calls=%async_computation | async-start | bytes 262144 | tf_op jit(solution)/shard_map/all_to_all | solution.py:180
  16.7 1.2 %copy-start = (bf16[512,1024]{1,0:T(8,128)(2,1)S(1)}, bf16[512,1024]{1,0:T(8,128)(2,1)}, u32[]{:S(2)}) copy-start(bf16[512,1024]{1,0:T(8,128)(2,1)} %k_ref.1) | copy-start | bytes 3145732
  18.0 1.2 %copy-start.1 = (bf16[512,1024]{1,0:T(8,128)(2,1)S(1)}, bf16[512,1024]{1,0:T(8,128)(2,1)}, u32[]{:S(2)}) copy-start(bf16[512,1024]{1,0:T(8,128)(2,1)} %v_ref.1) | copy-start | bytes 3145732
  21.0 9.4 %copy-start.2 = (s32[512,16]{0,1:T(8,128)S(1)}, s32[512,16]{0,1:T(8,128)}, u32[]{:S(2)}) copy-start(s32[512,16]{0,1:T(8,128)} %param.7) | copy-start | bytes 98308
  21.0 19.0 %collective-permute-start = (bf16[1024,256]{1,0:T(8,128)(2,1)}, bf16[1024,256]{1,0:T(8,128)(2,1)S(1)}, u32[]{:S(2)}, u32[]{:S(2)}) collective-permute-start(bf16[1024,256]{1,0:T(8,128)(2,1)} %get-tuple-element.10), channel_id=1, source_target_pairs={{0,1},{1,0},{2,3},{3,2},{4,5},{5,4},{6,7},{7,6},{8,9},{9,8},{10,11... | collective-permute-start | bytes 1572872 | tf_op jit(solution)/shard_map/ppermute | solution.py:204
  24.5 30.4 %collective-permute-start.1 = (bf16[1024,256]{1,0:T(8,128)(2,1)}, bf16[1024,256]{1,0:T(8,128)(2,1)S(1)}, u32[]{:S(2)}, u32[]{:S(2)}) collective-permute-start(bf16[1024,256]{1,0:T(8,128)(2,1)} %get-tuple-element.11), channel_id=1, source_target_pairs={{0,4},{1,5},{2,6},{3,7},{4,0},{5,1},{6,2},{7,3},{8,12},{9,13},{10,... | collective-permute-start | bytes 1572872 | tf_op jit(solution)/shard_map/ppermute | solution.py:204
  28.0 26.9 %collective-permute-start.2 = (bf16[1024,256]{1,0:T(8,128)(2,1)S(1)}, bf16[1024,256]{1,0:T(8,128)(2,1)S(1)}, u32[]{:S(2)}, u32[]{:S(2)}) collective-permute-start(bf16[1024,256]{1,0:T(8,128)(2,1)S(1)} %get-tuple-element.12), channel_id=1, source_target_pairs={{0,5},{1,4},{2,7},{3,6},{4,1},{5,0},{6,3},{7,2},{8,13},{9,12},{10,... | collective-permute-start | bytes 1572872 | tf_op jit(solution)/shard_map/ppermute | solution.py:204
  32.7 26.1 %all-to-all-start.1 = ((bf16[32,16,512]{2,1,0:T(8,128)(2,1)}), bf16[32,16,512]{2,1,0:T(8,128)(2,1)S(1)}, u32[]{:S(2)}, u32[]{:S(2)}) async-start(bf16[32,16,512]{2,1,0:T(8,128)(2,1)} %select.49), calls=%async_computation.1 | async-start | bytes 1048576 | tf_op jit(solution)/shard_map/all_to_all | solution.py:180

commit v7 on v5

v7 whole, which is shorter than its diff:
```python
import functools

import jax
import jax.numpy as jnp
from jax import lax
from jax.experimental import pallas as pl
from jax.experimental.pallas import tpu as pltpu
from jax.sharding import PartitionSpec as P

QUERY_HEADS = 32
KEY_HEADS = 8
HEAD_WIDTH = 128
BLOCK = 4096
QUERY_PER_KEY = 4
LOG2E = 1.4426950408889634
NEVER = -1e30

SIDE = 4
SLOTS = 8
FEAT = QUERY_PER_KEY * HEAD_WIDTH
STAT = 128
ONE_LANE = 12
PART_ROWS = 12
SWAPS = (2, 6, 7, 5, 3, 4, 1)
EARLY = 2


def pieces(x):
    hi = x.astype(jnp.bfloat16).astype(jnp.float32)
    rest = x - hi
    mid = rest.astype(jnp.bfloat16).astype(jnp.float32)
    return hi, mid, rest - mid


def stat_lanes(lse):
    lane = lax.broadcasted_iota(jnp.int32, (lse[0].shape[0], STAT), 1)
    stat = jnp.zeros(lane.shape, jnp.float32)
    for at, x in enumerate(lse):
        for k, piece in enumerate(pieces(x)):
            stat = jnp.where(lane == at * 3 + k, piece, stat)
    return stat


def find_kernel(here_ref, ids_ref, pos_ref):
    z, core, y = here_ref[0], here_ref[1], here_ref[2]
    count = ids_ref.shape[1]
    ids = ids_ref[...]
    b = lax.broadcasted_iota(jnp.int32, (8, count), 0)
    named = jnp.zeros((8, count), jnp.float32)
    for block in range(4):
        hit = jnp.max(jnp.where(ids == z * 4 + block, 1.0, 0.0), axis=0, keepdims=True)
        named = jnp.where(b == block, hit, named)
    columns = count // SIDE
    r = lax.broadcasted_iota(jnp.int32, (count, columns), 0)
    c = lax.broadcasted_iota(jnp.int32, (count, columns), 1)
    own = jnp.where(r == (c // SIDE) * (SIDE * SIDE) + y * SIDE + c % SIDE, 1.0, 0.0)
    named = jnp.dot(named, own, preferred_element_type=jnp.float32)
    r = lax.broadcasted_iota(jnp.int32, (columns, columns), 0)
    c = lax.broadcasted_iota(jnp.int32, (columns, columns), 1)
    before = jnp.where((r % SIDE == c % SIDE) & (r < c), 1.0, 0.0)
    rank = jnp.dot(named, before, preferred_element_type=jnp.float32)
    pos = jnp.where(named > 0.5, rank, -1.0)
    side = jnp.where(r == (c // SIDE) * (2 * SIDE) + core * SIDE + c % SIDE, 1.0, 0.0)
    pos = jnp.dot(pos, side, preferred_element_type=jnp.float32)
    pos_ref[...] = pos[:, : pos_ref.shape[1]]


def slot_onehot(pos):
    shape = (SIDE * SLOTS, pos.shape[1])
    r = lax.broadcasted_iota(jnp.int32, shape, 0)
    c = lax.broadcasted_iota(jnp.int32, shape, 1)
    hit = (pos == (r % SLOTS).astype(jnp.float32)) & (r // SLOTS == c % SIDE)
    return jnp.where(hit, 1.0, 0.0).astype(jnp.bfloat16)


def relay_kernel(me_ref, k_ref, v_ref, *out_refs):
    tokens = k_ref.shape[0]
    for i, out_ref in zip((0,) + SWAPS, out_refs):
        head = jnp.bitwise_xor(me_ref[0], i)
        lanes = pl.ds(pl.multiple_of(head * HEAD_WIDTH, HEAD_WIDTH), HEAD_WIDTH)
        out_ref[:tokens] = k_ref[:, lanes]
        out_ref[tokens:] = v_ref[:, lanes]


def select_kernel(pos_ref, q_ref, out_ref, wide_ref):
    rows = pos_ref.shape[1]
    wide_ref[...] = q_ref[...].astype(jnp.float32)
    for y0 in range(2):
        q = [wide_ref[pl.ds(y0 * SIDE + g, rows, stride=2 * SIDE), :] for g in range(QUERY_PER_KEY)]
        q = jnp.concatenate(q, axis=1).astype(jnp.bfloat16)
        for b in range(4):
            hot = slot_onehot(pos_ref[b : b + 1, :])
            picked = jnp.dot(hot, q, preferred_element_type=jnp.float32)
            out_ref[b * 2 + y0] = picked.astype(jnp.bfloat16)


def attend_kernel(x_ref, *refs):
    kv_refs, y_ref = refs[:-1], refs[-1]
    scale = HEAD_WIDTH ** (-0.5) * LOG2E
    tokens = kv_refs[0].shape[0] // 2
    slots = x_ref.shape[1]
    rows = SIDE * slots
    ones = jnp.ones((tokens, HEAD_WIDTH), jnp.bfloat16)
    x = x_ref[:SIDE].astype(jnp.float32) + x_ref[SIDE:].astype(jnp.float32)
    x = x.reshape(rows, FEAT).astype(jnp.bfloat16)
    q = [x[:, g * HEAD_WIDTH : (g + 1) * HEAD_WIDTH] for g in range(QUERY_PER_KEY)]
    q = jnp.concatenate(q, axis=0)
    tops, sums = [], []
    for kv_ref in kv_refs:
        k = kv_ref[:tokens]
        v = jnp.concatenate([kv_ref[tokens:], ones], axis=1)
        s = lax.dot_general(q, k, (((1,), (1,)), ((), ())), preferred_element_type=jnp.float32)
        m = jnp.max(s, axis=1, keepdims=True)
        w = jnp.exp2((s - m) * scale).astype(jnp.bfloat16)
        tops.append(m)
        sums.append(jnp.dot(w, v, preferred_element_type=jnp.float32))
    top = functools.reduce(jnp.maximum, tops)
    both = functools.reduce(jnp.add, [jnp.exp2((m - top) * scale) * x for m, x in zip(tops, sums)])
    total = both[:, HEAD_WIDTH:]
    out = (both[:, :HEAD_WIDTH] / total).astype(jnp.bfloat16)
    lse = top * scale + jnp.log2(total[:, :1])
    parts = [out[g * rows : (g + 1) * rows].reshape(SIDE, slots, HEAD_WIDTH) for g in range(QUERY_PER_KEY)]
    stat = stat_lanes([lse[g * rows : (g + 1) * rows] for g in range(QUERY_PER_KEY)])
    lane = lax.broadcasted_iota(jnp.int32, stat.shape, 1)
    stat = jnp.where(lane == ONE_LANE, 1.0, stat).astype(jnp.bfloat16).reshape(SIDE, slots, STAT)
    for core in range(2):
        dest = slice(core * SIDE, (core + 1) * SIDE)
        for g in range(QUERY_PER_KEY):
            y_ref[dest, :, g * HEAD_WIDTH : (g + 1) * HEAD_WIDTH] = parts[g]
        y_ref[dest, :, FEAT:] = stat


def merge_kernel(pos_ref, y_ref, out_ref, wide_ref):
    flip = (((0,), (0,)), ((), ()))
    rows = pos_ref.shape[1]
    hots = [slot_onehot(pos_ref[b : b + 1, :]) for b in range(4)]
    ends = []
    for y0 in range(2):
        parts = [
            lax.dot_general(hots[b], y_ref[b * 2 + y0], flip, preferred_element_type=jnp.float32) for b in range(4)
        ]
        named = [x[:, FEAT + ONE_LANE : FEAT + ONE_LANE + 1] > 0.5 for x in parts]
        for g in range(QUERY_PER_KEY):
            lanes = slice(g * HEAD_WIDTH, (g + 1) * HEAD_WIDTH)
            at = FEAT + 3 * g
            lse = [
                jnp.where(n, x[:, at : at + 1] + (x[:, at + 1 : at + 2] + x[:, at + 2 : at + 3]), NEVER)
                for n, x in zip(named, parts)
            ]
            top = functools.reduce(jnp.maximum, lse)
            weights = [jnp.exp2(x - top) for x in lse]
            total = functools.reduce(jnp.add, weights)
            out = functools.reduce(jnp.add, [w * x[:, lanes] for w, x in zip(weights, parts)]) / total
            wide_ref[pl.ds(y0 * SIDE + g, rows, stride=PART_ROWS), :] = out
            ends.append(top + jnp.log2(total))
    wide_ref[pl.ds(2 * SIDE, rows, stride=PART_ROWS), :] = stat_lanes(ends)
    for r in range(2 * SIDE + 1, PART_ROWS):
        wide_ref[pl.ds(r, rows, stride=PART_ROWS), :] = jnp.zeros((rows, HEAD_WIDTH), jnp.float32)
    out_ref[...] = wide_ref[...].astype(jnp.bfloat16)


def last_kernel(a_ref, out_ref, wide_ref):
    count = a_ref.shape[0] // (SIDE * PART_ROWS)
    wide_ref[...] = a_ref[...].astype(jnp.float32)

    def over_z(x, r):
        return wide_ref[pl.ds(x * PART_ROWS + r, count, stride=SIDE * PART_ROWS), :]

    for x in range(SIDE):
        stat = over_z(x, 2 * SIDE)
        for y0 in range(2):
            outs = []
            for g in range(QUERY_PER_KEY):
                r = y0 * SIDE + g
                lse = stat[:, 3 * r : 3 * r + 1] + (stat[:, 3 * r + 1 : 3 * r + 2] + stat[:, 3 * r + 2 : 3 * r + 3])
                weight = jnp.exp2(lse - jnp.max(lse, axis=0, keepdims=True))
                total = jnp.sum(weight, axis=0, keepdims=True)
                outs.append(jnp.sum(over_z(x, r) * weight, axis=0, keepdims=True) / total)
            head = y0 * SIDE + x
            out_ref[:, head * FEAT : (head + 1) * FEAT] = jnp.concatenate(outs, axis=1).astype(jnp.bfloat16)


def call(kernel, shape, dtype, name, *args, scratch=()):
    return pl.pallas_call(
        kernel,
        out_shape=jax.ShapeDtypeStruct(shape, dtype),
        in_specs=[pl.BlockSpec(memory_space=pltpu.VMEM)] * len(args),
        out_specs=pl.BlockSpec(memory_space=pltpu.VMEM),
        scratch_shapes=[pltpu.VMEM(s, jnp.float32) for s in scratch],
        compiler_params=pltpu.CompilerParams(vmem_limit_bytes=40 * 1024 * 1024),
        name=name,
    )(*args)


def per_device(queries, keys, values, block_ids):
    count_x = lax.axis_size("sx")
    count_y = lax.axis_size("sy")
    index_x = lax.axis_index("sx")
    index_y = lax.axis_index("sy")
    count_z = count_x // 2
    tokens = keys.shape[0]
    slabs = BLOCK // tokens
    rows = count_z * SIDE

    def groups(key):
        found = {}
        for sx in range(count_x):
            for sy in range(count_y):
                found.setdefault(key(sx // 2, sx % 2, sy // SIDE, sy % SIDE), []).append(sx * count_y + sy)
        return list(found.values())

    along_zx = groups(lambda z, core, y, x: (core, y))
    along_cy = groups(lambda z, core, y, x: (z, x))

    def exchange(x, members):
        return lax.all_to_all(x, ("sx", "sy"), split_axis=0, concat_axis=0, tiled=True, axis_index_groups=members)

    vmem = pl.BlockSpec(memory_space=pltpu.VMEM)
    smem = pl.BlockSpec(memory_space=pltpu.SMEM)

    own = queries.reshape(2, SIDE, QUERY_PER_KEY, HEAD_WIDTH).transpose(1, 0, 2, 3)
    own = own.reshape(1, SIDE, 2 * SIDE, HEAD_WIDTH)
    own = jnp.broadcast_to(own, (count_z, SIDE, 2 * SIDE, HEAD_WIDTH))
    own = exchange(own.reshape(rows, 2 * SIDE, HEAD_WIDTH), along_zx)

    here = jnp.stack([index_x // 2, index_x % 2, index_y // SIDE]).astype(jnp.int32)
    pos = pl.pallas_call(
        find_kernel,
        out_shape=jax.ShapeDtypeStruct((8, rows), jnp.float32),
        in_specs=[smem, vmem],
        out_specs=vmem,
        name="find",
    )(here, block_ids.T)

    me = (index_y % slabs).astype(jnp.int32).reshape(1)
    kv = pl.pallas_call(
        relay_kernel,
        out_shape=[jax.ShapeDtypeStruct((2 * tokens, HEAD_WIDTH), jnp.bfloat16)] * slabs,
        in_specs=[smem, vmem, vmem],
        out_specs=[vmem] * slabs,
        compiler_params=pltpu.CompilerParams(vmem_limit_bytes=40 * 1024 * 1024),
        name="relay",
    )(me, keys, values)

    def swap(x, i):
        return lax.ppermute(x, "sy", [(d, d ^ i) for d in range(count_y)])

    early = [swap(x, i) for x, i in zip(kv[1 : EARLY + 1], SWAPS)]
    asked = call(
        select_kernel,
        (2 * SIDE, SIDE * SLOTS, FEAT),
        jnp.bfloat16,
        "select",
        pos,
        own.reshape(rows * 2 * SIDE, HEAD_WIDTH),
        scratch=[(rows * 2 * SIDE, HEAD_WIDTH)],
    )
    asked, *late = lax.optimization_barrier((asked, *kv[EARLY + 1 :]))
    asked = exchange(asked, along_cy)
    late = [swap(x, i) for x, i in zip(late, SWAPS[EARLY:])]
    part = call(
        attend_kernel, (2 * SIDE, SIDE * SLOTS, FEAT + STAT), jnp.bfloat16, "attend", asked, kv[0], *early, *late
    )
    part = exchange(part, along_cy)
    shape = (rows * PART_ROWS, HEAD_WIDTH)
    part = call(merge_kernel, shape, jnp.bfloat16, "merge", pos, part, scratch=[shape])
    part = exchange(part.reshape(rows, PART_ROWS // SIDE, SIDE, HEAD_WIDTH), along_zx)
    return call(
        last_kernel, (1, QUERY_HEADS * HEAD_WIDTH), jnp.bfloat16, "last", part.reshape(shape), scratch=[shape]
    )


def solution(mesh):
    return jax.shard_map(
        per_device,
        mesh=mesh,
        in_specs=(P(("sx", "sy"), None), P(("sx", "sy"), None), P(("sx", "sy"), None), P()),
        out_specs=P(("sx", "sy"), None),
        check_vma=False,
    )
```

time: 110 us -> 113 us (1.027)
  the two profiles are of different devices: /device:TPU:32 before, /device:TPU:2 now
where the time goes in v7:
time: 113 us
  blocking collectives  52.2 us (46%)
  starting transfers between devices  43.7 us (39%)
  Pallas kernels  8.45 us (7%)
  local copies, waits for them, and re-layouts  3.8 us (3%)
  waiting for transfers between devices  2.86 us (3%)
  other arithmetic  1.36 us (1%)
    all_to_all x3, blocking collectives, exchange(): lax.all_to_all(x, ('sx', 'sy'), split_axis=0, concat_axis=0, tiled=True,...  52.2 us
    ppermute x7, starting transfers between devices, swap(): return lax.ppermute(x, 'sy', [(d, d ^ i) for d in range(count_y)])  25 us
    all_to_all x1, starting transfers between devices, exchange(): lax.all_to_all(x, ('sx', 'sy'), split_axis=0, concat_axis=0, tiled=True,...  18.6 us
    pallas_call x4, Pallas kernels, call(): pl.pallas_call(kernel, out_shape=jax.ShapeDtypeStruct(shape, dtype), in_s...  6.15 us
    unnamed x6, local copies, waits for them, and re-layouts  3.13 us
    all_to_all x1, waiting for transfers between devices, exchange(): lax.all_to_all(x, ('sx', 'sy'), split_axis=0, concat_axis=0, tiled=True,...  2.84 us
  transfers between devices with their start and end apart: 8, of which 1 were waited for; matrix products, arithmetic and copies ran while one was open for 1% of the time, Pallas kernels for 2%

profile of v7, /device:TPU:2, one launch (start us, length us, event | category | flops | bytes accessed | tf_op | source)
XLA Modules:
  0.0 112.5 jit_solution(2790798737632388699)
XLA Ops:
  0.0 0.8 reduce
  0.8 0.7 broadcast_in_dim.8
  1.4 18.6 %all-to-all-start = ((bf16[64,8,128]{2,1,0:T(8,128)(2,1)}), bf16[64,8,128]{2,1,0:T(8,128)(2,1)S(1)}, u32[]{:S(2)}, u32[]{:S(2)}) async-start(bf16[64,8,128]{2,1,0:T(8,128)(2,1)} %bitcast.6), calls=%async_computation | async-start | bytes 262144 | tf_op jit(solution)/shard_map/all_to_all | solution.py:216
  20.1 0.0 copy-start
  20.1 1.2 %copy-done = bf16[512,1024]{1,0:T(8,128)(2,1)S(1)} copy-done((bf16[512,1024]{1,0:T(8,128)(2,1)S(1)}, bf16[512,1024]{1,0:T(8,128)(2,1)}, u32[]{:S(2)}) %copy-start) | copy-done | bytes 1048600
  21.3 1.2 %copy-done.1 = bf16[512,1024]{1,0:T(8,128)(2,1)S(1)} copy-done((bf16[512,1024]{1,0:T(8,128)(2,1)S(1)}, bf16[512,1024]{1,0:T(8,128)(2,1)}, u32[]{:S(2)}) %copy-start.1) | copy-done | bytes 1048600
  22.6 0.5 relay.1
  23.1 4.0 %collective-permute-start = (bf16[1024,128]{1,0:T(8,128)(2,1)S(1)}, bf16[1024,128]{1,0:T(8,128)(2,1)S(1)}, u32[]{:S(2)}, u32[]{:S(2)}) collective-permute-start(bf16[1024,128]{1,0:T(8,128)(2,1)S(1)} %get-tuple-element.26), channel_id=1, source_target_pairs={{0,2},{1,3},{2,0},{3,1},{4,6},{5,7},{6,4},{7,5},{8,10},{9,11},{10,... | collective-permute-start | bytes 786440 | tf_op jit(solution)/shard_map/ppermute | solution.py:246
  27.1 4.4 %collective-permute-start.1 = (bf16[1024,128]{1,0:T(8,128)(2,1)S(1)}, bf16[1024,128]{1,0:T(8,128)(2,1)S(1)}, u32[]{:S(2)}, u32[]{:S(2)}) collective-permute-start(bf16[1024,128]{1,0:T(8,128)(2,1)S(1)} %get-tuple-element.27), channel_id=1, source_target_pairs={{0,6},{1,7},{2,4},{3,5},{4,2},{5,3},{6,0},{7,1},{8,14},{9,15},{10,... | collective-permute-start | bytes 786440 | tf_op jit(solution)/shard_map/ppermute | solution.py:246
  31.5 0.6 pad_add_fusion.here_ref
  32.1 1.8 %find.1.pos_ref = f32[8,64]{1,0:T(8,128)} custom-call(s32[3]{0:T(128)} %pad_add_fusion.here_ref, s32[16,512]{1,0:T(8,128)} %bitcast.18), custom_call_target="tpu_custom_call" | custom-call | tf_op jit(solution)/shard_map/find/pallas_call | solution.py:227
  33.9 2.8 %all-to-all-done = bf16[64,8,128]{2,1,0:T(8,128)(2,1)S(1)} async-done(((bf16[64,8,128]{2,1,0:T(8,128)(2,1)}), bf16[64,8,128]{2,1,0:T(8,128)(2,1)S(1)}, u32[]{:S(2)}, u32[]{:S(2)}) %all-to-all-start) | async-done | bytes 131104 | tf_op jit(solution)/shard_map/all_to_all | solution.py:216
  36.7 0.7 copy-done.2
  37.4 0.2 select.13
  37.6 3.6 %collective-permute-start.2 = (bf16[1024,128]{1,0:T(8,128)(2,1)S(1)}, bf16[1024,128]{1,0:T(8,128)(2,1)S(1)}, u32[]{:S(2)}, u32[]{:S(2)}) collective-permute-start(bf16[1024,128]{1,0:T(8,128)(2,1)S(1)} %get-tuple-element.28), channel_id=1, source_target_pairs={{0,7},{1,6},{2,5},{3,4},{4,3},{5,2},{6,1},{7,0},{8,15},{9,14},{10,... | collective-permute-start | bytes 786440 | tf_op jit(solution)/shard_map/ppermute | solution.py:246
  41.3 3.5 %collective-permute-start.3 = (bf16[1024,128]{1,0:T(8,128)(2,1)S(1)}, bf16[1024,128]{1,0:T(8,128)(2,1)S(1)}, u32[]{:S(2)}, u32[]{:S(2)}) collective-permute-start(bf16[1024,128]{1,0:T(8,128)(2,1)S(1)} %get-tuple-element.29), channel_id=1, source_target_pairs={{0,5},{1,4},{2,7},{3,6},{4,1},{5,0},{6,3},{7,2},{8,13},{9,12},{10,... | collective-permute-start | bytes 786440 | tf_op jit(solution)/shard_map/ppermute | solution.py:246
  44.7 3.7 %collective-permute-start.4 = (bf16[1024,128]{1,0:T(8,128)(2,1)S(1)}, bf16[1024,128]{1,0:T(8,128)(2,1)S(1)}, u32[]{:S(2)}, u32[]{:S(2)}) collective-permute-start(bf16[1024,128]{1,0:T(8,128)(2,1)S(1)} %get-tuple-element.30), channel_id=1, source_target_pairs={{0,3},{1,2},{2,1},{3,0},{4,7},{5,6},{6,5},{7,4},{8,11},{9,10},{10,... | collective-permute-start | bytes 786440 | tf_op jit(solution)/shard_map/ppermute | solution.py:246
  48.5 0.0 collective-permute-done.refs_1_
  48.5 3.5 %collective-permute-start.5 = (bf16[1024,128]{1,0:T(8,128)(2,1)S(1)}, bf16[1024,128]{1,0:T(8,128)(2,1)S(1)}, u32[]{:S(2)}, u32[]{:S(2)}) collective-permute-start(bf16[1024,128]{1,0:T(8,128)(2,1)S(1)} %get-tuple-element.31), channel_id=1, source_target_pairs={{0,4},{1,5},{2,6},{3,7},{4,0},{5,1},{6,2},{7,3},{8,12},{9,13},{10,... | collective-permute-start | bytes 786440 | tf_op jit(solution)/shard_map/ppermute | solution.py:246
  52.0 0.0 collective-permute-done.1.refs_2_
  52.0 2.4 %collective-permute-start.6 = (bf16[1024,128]{1,0:T(8,128)(2,1)S(1)}, bf16[1024,128]{1,0:T(8,128)(2,1)S(1)}, u32[]{:S(2)}, u32[]{:S(2)}) collective-permute-start(bf16[1024,128]{1,0:T(8,128)(2,1)S(1)} %get-tuple-element.32), channel_id=1, source_target_pairs={{0,1},{1,0},{2,3},{3,2},{4,5},{5,4},{6,7},{7,6},{8,9},{9,8},{10,11... | collective-permute-start | bytes 786440 | tf_op jit(solution)/shard_map/ppermute | solution.py:246
  54.4 10.9 %all_to_all.20.x_ref = bf16[8,32,512]{2,1,0:T(8,128)(2,1)S(1)} all-to-all(bf16[8,32,512]{2,1,0:T(8,128)(2,1)S(1)} %select.13), channel_id=1, replica_groups={{0,4,8,12,16,20,24,28},{1,5,9,13,17,21,25,29},{2,6,10,14,18,22,26,30},{..., dimensions={0} | all-to-all | bytes 524288 | tf_op jit(solution)/shard_map/all_to_all | solution.py:216
  65.3 0.0 collective-permute-done.2.refs_3_
  65.3 0.0 collective-permute-done.3.refs_4_
  65.3 0.0 collective-permute-done.4.refs_5_
  65.3 0.0 collective-permute-done.5.refs_6_
  65.3 0.0 collective-permute-done.6.refs_7_
  65.3 3.2 %attend.1 = bf16[8,32,640]{2,1,0:T(8,128)(2,1)S(1)} custom-call(bf16[8,32,512]{2,1,0:T(8,128)(2,1)S(1)} %all_to_all.20.x_ref, bf16[1024,128]{1,0:T(8,128)(2,1)S(1)} %get-tuple-element.25.refs_0_, bf16[1024,128]{1,0:T(8,128)(2,1)S(1)} %collective-permute-done.refs_1_, bf16[1024,128]{1,0:T(8,128)(2,1)S(1)} %collective-permute-done.1.refs_2_, ...), custom_call_target="tpu_custom_call" | custom-call | tf_op jit(solution)/shard_map/attend/pallas_call | solution.py:184
  68.5 10.8 %all_to_all.21.y_ref = bf16[8,32,640]{2,1,0:T(8,128)(2,1)S(1)} all-to-all(bf16[8,32,640]{2,1,0:T(8,128)(2,1)S(1)} %attend.1), channel_id=1, replica_groups={{0,4,8,12,16,20,24,28},{1,5,9,13,17,21,25,29},{2,6,10,14,18,22,26,30},{..., dimensions={0} | all-to-all | bytes 655360 | tf_op jit(solution)/shard_map/all_to_all | solution.py:216
  79.4 1.7 %merge.1 = bf16[768,128]{1,0:T(8,128)(2,1)S(1)} custom-call(f32[8,64]{1,0:T(8,128)S(1)} %copy-done.2, bf16[8,32,640]{2,1,0:T(8,128)(2,1)S(1)} %all_to_all.21.y_ref), custom_call_target="tpu_custom_call" | custom-call | tf_op jit(solution)/shard_map/merge/pallas_call | solution.py:184
  81.0 30.4 %all_to_all.22 = bf16[64,3,4,128]{3,2,1,0:T(4,128)(2,1)S(1)} all-to-all(bf16[64,3,4,128]{3,2,1,0:T(4,128)(2,1)S(1)} %bitcast.13), channel_id=1, replica_groups={{0,1,2,3,32,33,34,35,64,65,66,67,96,97,98,99,128,129,130,131,160,161,16..., dimensions={0} | all-to-all | bytes 393216 | tf_op jit(solution)/shard_map/all_to_all | solution.py:216
  111.5 1.0 last.1
  (3 shorter events, 0.0 us)
Async XLA Ops:
  1.4 35.3 %all-to-all-start = ((bf16[64,8,128]{2,1,0:T(8,128)(2,1)}), bf16[64,8,128]{2,1,0:T(8,128)(2,1)S(1)}, u32[]{:S(2)}, u32[]{:S(2)}) async-start(bf16[64,8,128]{2,1,0:T(8,128)(2,1)} %bitcast.6), calls=%async_computation | async-start | bytes 262144 | tf_op jit(solution)/shard_map/all_to_all | solution.py:216
  20.1 1.2 %copy-start = (bf16[512,1024]{1,0:T(8,128)(2,1)S(1)}, bf16[512,1024]{1,0:T(8,128)(2,1)}, u32[]{:S(2)}) copy-start(bf16[512,1024]{1,0:T(8,128)(2,1)} %k_ref.1) | copy-start | bytes 3145732
  21.3 1.2 %copy-start.1 = (bf16[512,1024]{1,0:T(8,128)(2,1)S(1)}, bf16[512,1024]{1,0:T(8,128)(2,1)}, u32[]{:S(2)}) copy-start(bf16[512,1024]{1,0:T(8,128)(2,1)} %v_ref.1) | copy-start | bytes 3145732
  23.1 25.4 %collective-permute-start = (bf16[1024,128]{1,0:T(8,128)(2,1)S(1)}, bf16[1024,128]{1,0:T(8,128)(2,1)S(1)}, u32[]{:S(2)}, u32[]{:S(2)}) collective-permute-start(bf16[1024,128]{1,0:T(8,128)(2,1)S(1)} %get-tuple-element.26), channel_id=1, source_target_pairs={{0,2},{1,3},{2,0},{3,1},{4,6},{5,7},{6,4},{7,5},{8,10},{9,11},{10,... | collective-permute-start | bytes 786440 | tf_op jit(solution)/shard_map/ppermute | solution.py:246
  27.1 24.9 %collective-permute-start.1 = (bf16[1024,128]{1,0:T(8,128)(2,1)S(1)}, bf16[1024,128]{1,0:T(8,128)(2,1)S(1)}, u32[]{:S(2)}, u32[]{:S(2)}) collective-permute-start(bf16[1024,128]{1,0:T(8,128)(2,1)S(1)} %get-tuple-element.27), channel_id=1, source_target_pairs={{0,6},{1,7},{2,4},{3,5},{4,2},{5,3},{6,0},{7,1},{8,14},{9,15},{10,... | collective-permute-start | bytes 786440 | tf_op jit(solution)/shard_map/ppermute | solution.py:246
  36.7 0.7 copy-start.2
  37.6 27.6 %collective-permute-start.2 = (bf16[1024,128]{1,0:T(8,128)(2,1)S(1)}, bf16[1024,128]{1,0:T(8,128)(2,1)S(1)}, u32[]{:S(2)}, u32[]{:S(2)}) collective-permute-start(bf16[1024,128]{1,0:T(8,128)(2,1)S(1)} %get-tuple-element.28), channel_id=1, source_target_pairs={{0,7},{1,6},{2,5},{3,4},{4,3},{5,2},{6,1},{7,0},{8,15},{9,14},{10,... | collective-permute-start | bytes 786440 | tf_op jit(solution)/shard_map/ppermute | solution.py:246
  41.3 24.0 %collective-permute-start.3 = (bf16[1024,128]{1,0:T(8,128)(2,1)S(1)}, bf16[1024,128]{1,0:T(8,128)(2,1)S(1)}, u32[]{:S(2)}, u32[]{:S(2)}) collective-permute-start(bf16[1024,128]{1,0:T(8,128)(2,1)S(1)} %get-tuple-element.29), channel_id=1, source_target_pairs={{0,5},{1,4},{2,7},{3,6},{4,1},{5,0},{6,3},{7,2},{8,13},{9,12},{10,... | collective-permute-start | bytes 786440 | tf_op jit(solution)/shard_map/ppermute | solution.py:246
  44.7 20.5 %collective-permute-start.4 = (bf16[1024,128]{1,0:T(8,128)(2,1)S(1)}, bf16[1024,128]{1,0:T(8,128)(2,1)S(1)}, u32[]{:S(2)}, u32[]{:S(2)}) collective-permute-start(bf16[1024,128]{1,0:T(8,128)(2,1)S(1)} %get-tuple-element.30), channel_id=1, source_target_pairs={{0,3},{1,2},{2,1},{3,0},{4,7},{5,6},{6,5},{7,4},{8,11},{9,10},{10,... | collective-permute-start | bytes 786440 | tf_op jit(solution)/shard_map/ppermute | solution.py:246
  48.5 16.8 %collective-permute-start.5 = (bf16[1024,128]{1,0:T(8,128)(2,1)S(1)}, bf16[1024,128]{1,0:T(8,128)(2,1)S(1)}, u32[]{:S(2)}, u32[]{:S(2)}) collective-permute-start(bf16[1024,128]{1,0:T(8,128)(2,1)S(1)} %get-tuple-element.31), channel_id=1, source_target_pairs={{0,4},{1,5},{2,6},{3,7},{4,0},{5,1},{6,2},{7,3},{8,12},{9,13},{10,... | collective-permute-start | bytes 786440 | tf_op jit(solution)/shard_map/ppermute | solution.py:246
  52.0 13.3 %collective-permute-start.6 = (bf16[1024,128]{1,0:T(8,128)(2,1)S(1)}, bf16[1024,128]{1,0:T(8,128)(2,1)S(1)}, u32[]{:S(2)}, u32[]{:S(2)}) collective-permute-start(bf16[1024,128]{1,0:T(8,128)(2,1)S(1)} %get-tuple-element.32), channel_id=1, source_target_pairs={{0,1},{1,0},{2,3},{3,2},{4,5},{5,4},{6,7},{7,6},{8,9},{9,8},{10,11... | collective-permute-start | bytes 786440 | tf_op jit(solution)/shard_map/ppermute | solution.py:246

commit v8 on v5

--- a/solution.py
+++ b/solution.py
@@ -37,21 +37,68 @@
     return stat
 
 
+def find_kernel(ids_ref, in_ref, out_ref):
+    count_x, count_y = lax.axis_size("sx"), lax.axis_size("sy")
+    index_x, index_y = lax.axis_index("sx"), lax.axis_index("sy")
+    z, core = index_x // 2, index_x % 2
+    lanes = 128
+    r = lax.broadcasted_iota(jnp.int32, (count_x * count_y, lanes), 0)
+    c = lax.broadcasted_iota(jnp.int32, (count_x * count_y, lanes), 1)
+    own = jnp.where((r == c * count_y + index_y) & (c < count_x), 1.0, 0.0).astype(jnp.bfloat16)
+    ids = ids_ref[...].astype(jnp.float32).astype(jnp.bfloat16)
+    column = jnp.dot(ids, own, preferred_element_type=jnp.float32)
+    b = lax.broadcasted_iota(jnp.int32, (8, lanes), 0)
+    c = lax.broadcasted_iota(jnp.int32, (8, lanes), 1)
+    named = jnp.zeros((8, lanes), jnp.float32)
+    for block in range(4):
+        wanted = (z * 4 + block).astype(jnp.float32)
+        hit = jnp.max(jnp.where(column == wanted, 1.0, 0.0), axis=0, keepdims=True)
+        named = jnp.where((b == block) & (c < count_x), hit, named)
+    r = lax.broadcasted_iota(jnp.int32, (lanes, lanes), 0)
+    c = lax.broadcasted_iota(jnp.int32, (lanes, lanes), 1)
+    before = jnp.where(r < c, 1.0, 0.0).astype(jnp.bfloat16)
+    rank = jnp.dot(named.astype(jnp.bfloat16), before, preferred_element_type=jnp.float32)
+    pos = jnp.where(named > 0.5, rank, -1.0).astype(jnp.bfloat16)
+    side = jnp.where(r == (c // KEY_HEADS) * 2 + core, 1.0, 0.0).astype(jnp.bfloat16)
+    out_ref[...] = jnp.dot(pos, side, preferred_element_type=jnp.float32)
+    shape = (lanes, in_ref.shape[1])
+    r = lax.broadcasted_iota(jnp.int32, shape, 0)
+    c = lax.broadcasted_iota(jnp.int32, shape, 1)
+    both = jnp.where(r == c // KEY_HEADS, 1.0, 0.0).astype(jnp.bfloat16)
+    in_ref[...] = jnp.dot(pos, both, preferred_element_type=jnp.float32)
+
+
 def slot_onehot(pos):
     shape = (KEY_HEADS * SLOTS, pos.shape[1])
     r = lax.broadcasted_iota(jnp.int32, shape, 0)
     c = lax.broadcasted_iota(jnp.int32, shape, 1)
-    hit = (pos == r % SLOTS) & (r // SLOTS == c % KEY_HEADS)
+    hit = (pos == (r % SLOTS).astype(jnp.float32)) & (r // SLOTS == c % KEY_HEADS)
     return jnp.where(hit, 1.0, 0.0).astype(jnp.bfloat16)
 
 
-def relay_kernel(me_ref, k_ref, v_ref, *out_refs):
+def relay_kernel(k_ref, v_ref, out_ref, k_here, v_here, by_head, in_sems, out_sems):
     tokens = k_ref.shape[0]
-    for i, out_ref in enumerate(out_refs):
-        head = jnp.bitwise_xor(me_ref[0], i)
-        lanes = pl.ds(pl.multiple_of(head * HEAD_WIDTH, HEAD_WIDTH), HEAD_WIDTH)
-        out_ref[:tokens] = k_ref[:, lanes]
-        out_ref[tokens:] = v_ref[:, lanes]
+    chunks = in_sems.shape[1]
+    step = tokens // chunks
+    pairs = [(i, j) for i in range(chunks) for j in range(2)]
+    there, here = (k_ref, v_ref), (k_here, v_here)
+    arriving = {}
+    for i, j in pairs:
+        part = pl.ds(i * step, step)
+        arriving[i, j] = pltpu.make_async_copy(there[j].at[part], here[j].at[part], in_sems.at[j, i])
+        arriving[i, j].start()
+    leaving = []
+    for i, j in pairs:
+        arriving[i, j].wait()
+        start = j * tokens + i * step
+        for h in range(KEY_HEADS):
+            lanes = slice(h * HEAD_WIDTH, (h + 1) * HEAD_WIDTH)
+            by_head[h, start : start + step] = here[j][i * step : (i + 1) * step, lanes]
+        part = pl.ds(start, step)
+        leaving.append(pltpu.make_async_copy(by_head.at[:, part], out_ref.at[:, part], out_sems.at[j, i]))
+        leaving[-1].start()
+    for copy in leaving:
+        copy.wait()
 
 
 def select_kernel(pos_ref, q_ref, out_ref):
@@ -63,21 +110,19 @@
         out_ref[b * KEY_HEADS : (b + 1) * KEY_HEADS] = picked
 
 
-def attend_kernel(x_ref, *refs):
-    kv_refs, y_ref = refs[:-1], refs[-1]
+def attend_kernel(x_ref, kv_ref, y_ref):
     scale = HEAD_WIDTH ** (-0.5) * LOG2E
-    columns = y_ref.shape[0] // 2
-    tokens = kv_refs[0].shape[0] // 2
+    columns = x_ref.shape[0] // 2
+    tokens = kv_ref.shape[1] // 2
     rows = columns * SLOTS
-    x = x_ref[:columns].astype(jnp.float32) + x_ref[columns:].astype(jnp.float32)
-    x = x.reshape(rows, FEAT).astype(jnp.bfloat16)
+    ones = jnp.ones((tokens, HEAD_WIDTH), jnp.bfloat16)
+    x = x_ref[columns:].astype(jnp.float32).reshape(rows, FEAT).astype(jnp.bfloat16)
     q = [x[:, g * HEAD_WIDTH : (g + 1) * HEAD_WIDTH] for g in range(QUERY_PER_KEY)]
     q = jnp.concatenate(q, axis=0)
-    ones = jnp.ones((tokens, HEAD_WIDTH), jnp.bfloat16)
     tops, sums = [], []
-    for kv_ref in kv_refs:
-        k = kv_ref[:tokens]
-        v = jnp.concatenate([kv_ref[tokens:], ones], axis=1)
+    for slab in range(kv_ref.shape[0]):
+        k = kv_ref[slab, :tokens]
+        v = jnp.concatenate([kv_ref[slab, tokens:], ones], axis=1)
         s = lax.dot_general(q, k, (((1,), (1,)), ((), ())), preferred_element_type=jnp.float32)
         m = jnp.max(s, axis=1, keepdims=True)
         w = jnp.exp2((s - m) * scale).astype(jnp.bfloat16)
@@ -136,7 +181,9 @@
         total = jnp.sum(weight, axis=0)
         lanes = slice(g * HEAD_WIDTH, (g + 1) * HEAD_WIDTH)
         mixed = jnp.sum(a_ref[:, :, lanes].astype(jnp.float32) * weight, axis=0) / total
-        out_ref[:, lanes] = mixed.astype(jnp.bfloat16)
+        for h in range(KEY_HEADS):
+            head = h * FEAT + g * HEAD_WIDTH
+            out_ref[:, head : head + HEAD_WIDTH] = mixed[h : h + 1].astype(jnp.bfloat16)
 
 
 def call(kernel, shape, dtype, name, *args):
@@ -153,49 +200,60 @@
 def per_device(queries, keys, values, block_ids):
     count_x = lax.axis_size("sx")
     count_y = lax.axis_size("sy")
-    index_x = lax.axis_index("sx")
-    index_y = lax.axis_index("sy")
     count_z = count_x // 2
-    index_z, core = index_x // 2, index_x % 2
     tokens = keys.shape[0]
     slabs = BLOCK // tokens
+    cores = [[2 * z, 2 * z + 1] for z in range(count_z)]
     along_z = [[2 * z + c for z in range(count_z)] for c in range(2)]
+    block_devices = [list(range(start, start + slabs)) for start in range(0, count_y, slabs)]
     plane = 2 * count_y
     planes = [list(range(z * plane, (z + 1) * plane)) for z in range(count_z)]
+    core_1_along_z = [[(2 * z + 1) * count_y + y for z in range(count_z)] for y in range(count_y)]
+    core_0_planes = [[2 * z * count_y + y for y in range(count_y)] for z in range(count_z)]
 
     def exchange(x, axis, groups):
         return lax.all_to_all(x, axis, split_axis=0, concat_axis=0, tiled=True, axis_index_groups=groups)
 
-    column = lax.dynamic_index_in_dim(block_ids.reshape(count_x, count_y, -1), index_y, 1, keepdims=False)
-    wanted = index_z * 4 + jnp.arange(4, dtype=jnp.int32)
-    named = jnp.any(column[None] == wanted[:, None, None], axis=2)
-    before = jnp.arange(count_x)[None, :] < jnp.arange(count_x)[:, None]
-    rank = jnp.sum((named[:, None, :] & before[None]).astype(jnp.int32), axis=2)
-    pos = jnp.where(named, rank, -1).reshape(4, count_z, 2)
-    pos = lax.dynamic_index_in_dim(pos, core, 2, keepdims=False)
-    pos = jnp.repeat(pos, KEY_HEADS, axis=1)
-
-    own = jnp.broadcast_to(queries.reshape(1, KEY_HEADS, FEAT), (count_z, KEY_HEADS, FEAT))
-    rows = exchange(own, "sx", along_z)
-    me = (index_y % slabs).astype(jnp.int32).reshape(1)
     vmem = pl.BlockSpec(memory_space=pltpu.VMEM)
+    hbm = pl.BlockSpec(memory_space=pltpu.HBM)
     kv = pl.pallas_call(
         relay_kernel,
-        out_shape=[jax.ShapeDtypeStruct((2 * tokens, HEAD_WIDTH), jnp.bfloat16)] * slabs,
-        in_specs=[pl.BlockSpec(memory_space=pltpu.SMEM), vmem, vmem],
-        out_specs=[vmem] * slabs,
-        compiler_params=pltpu.CompilerParams(vmem_limit_bytes=40 * 1024 * 1024),
+        out_shape=jax.ShapeDtypeStruct((KEY_HEADS, 2 * tokens, HEAD_WIDTH), jnp.bfloat16),
+        in_specs=[hbm, hbm],
+        out_specs=hbm,
+        scratch_shapes=[
+            pltpu.VMEM(keys.shape, keys.dtype),
+            pltpu.VMEM(values.shape, values.dtype),
+            pltpu.VMEM((KEY_HEADS, 2 * tokens, HEAD_WIDTH), keys.dtype),
+            pltpu.SemaphoreType.DMA((2, 4)),
+            pltpu.SemaphoreType.DMA((2, 4)),
+        ],
+        compiler_params=pltpu.CompilerParams(vmem_limit_bytes=60 * 1024 * 1024),
         name="relay",
-    )(me, keys, values)
-    kv = [kv[0]] + [lax.ppermute(kv[i], "sy", [(d, d ^ i) for d in range(count_y)]) for i in range(1, slabs)]
-    asked = call(select_kernel, (plane, SLOTS, FEAT), jnp.bfloat16, "select", pos, rows)
+    )(keys, values)
+    kv = exchange(kv, "sy", block_devices)
+
+    pos_in, pos_out = pl.pallas_call(
+        find_kernel,
+        out_shape=[
+            jax.ShapeDtypeStruct((8, count_x * KEY_HEADS), jnp.float32),
+            jax.ShapeDtypeStruct((8, count_z * KEY_HEADS), jnp.float32),
+        ],
+        in_specs=[vmem],
+        out_specs=[vmem, vmem],
+        name="find",
+    )(block_ids.T)
+    rows = lax.all_gather(queries.reshape(KEY_HEADS, FEAT), "sx", axis=0, axis_index_groups=cores)
+    rows = lax.all_gather(rows, ("sx", "sy"), axis=0, axis_index_groups=core_1_along_z + core_0_planes)
+    rows, pos_in, pos_out, kv = lax.optimization_barrier((rows, pos_in, pos_out, kv))
+    rows = rows.reshape(count_x, KEY_HEADS, FEAT)
+    asked = call(select_kernel, (plane, SLOTS, FEAT), jnp.bfloat16, "select", pos_in, rows)
     asked = exchange(asked, ("sx", "sy"), planes)
-    part = call(attend_kernel, (plane, SLOTS, FEAT + STAT), jnp.bfloat16, "attend", asked, *kv)
+    part = call(attend_kernel, (plane, SLOTS, FEAT + STAT), jnp.bfloat16, "attend", asked, kv)
     part = exchange(part, ("sx", "sy"), planes)
-    part = call(merge_kernel, (count_z, KEY_HEADS, FEAT + STAT), jnp.bfloat16, "merge", pos, part)
+    part = call(merge_kernel, (count_z, KEY_HEADS, FEAT + STAT), jnp.bfloat16, "merge", pos_out, part)
     part = exchange(part, "sx", along_z)
-    out = call(last_kernel, (KEY_HEADS, FEAT), jnp.bfloat16, "last", part)
-    return out.reshape(1, KEY_HEADS * FEAT)
+    return call(last_kernel, (1, KEY_HEADS * FEAT), jnp.bfloat16, "last", part)
 
 
 def solution(mesh):

time: 110 us -> 129 us (1.17)
  blocking collectives: 39.6 us -> 112 us
  starting transfers between devices: 47.4 us -> 5.32 us
  waiting for transfers between devices: 9.13 us -> 0.01 us
  local copies, waits for them, and re-layouts: 5.45 us -> 0.73 us
  Pallas kernels: 6.98 us -> 10 us
    all_gather x0 -> x2, blocking collectives: none -> 57.1 us  [the longest x1 55.3 us: per_device(): lax.all_gather(rows, ('sx', 'sy'), axis=0, axis_index_groups=core_1_along...]
    ppermute x7 -> x0, starting transfers between devices: 25.1 us -> none  [per_device(): lax.ppermute(kv[i], 'sy', [(d, d ^ i) for d in range(count_y)])]
    all_to_all x2 -> x1, starting transfers between devices: 22.3 us -> 5.32 us  [exchange(): lax.all_to_all(x, axis, split_axis=0, concat_axis=0, tiled=True, axis_ind...]
    all_to_all x2 -> x3, blocking collectives: 39.6 us -> 54.8 us  [exchange(): lax.all_to_all(x, axis, split_axis=0, concat_axis=0, tiled=True, axis_ind...]
    all_to_all x2 -> x1, waiting for transfers between devices: 7.78 us -> 0.01 us  [exchange(): lax.all_to_all(x, axis, split_axis=0, concat_axis=0, tiled=True, axis_ind...]
    pallas_call x1 -> x2, Pallas kernels: 1.23 us -> 4.22 us  [the longest x1 2.47 us: per_device(): pl.pallas_call(relay_kernel, out_shape=jax.ShapeDtypeStruct((KEY_HEADS, 2...]
    unnamed x5 -> x6, local copies, waits for them, and re-layouts: 3.06 us -> 0.71 us
    ppermute x7 -> x0, waiting for transfers between devices: 1.35 us -> none  [per_device(): lax.ppermute(kv[i], 'sy', [(d, d ^ i) for d in range(count_y)])]
  transfers between devices with their start and end apart: 9 -> 1, of which waited for: 2 -> 0; matrix products, arithmetic and copies ran while one was open for 2% -> 0% of each run, Pallas kernels for 2% -> 1%
where the time goes in v8:
time: 129 us; the launch traced here: 128 us
  blocking collectives  112 us (87%)
  Pallas kernels  10 us (8%)
  starting transfers between devices  5.32 us (4%)
    all_gather x1, blocking collectives, per_device(): lax.all_gather(rows, ('sx', 'sy'), axis=0, axis_index_groups=core_1_along...  55.3 us
    all_to_all x3, blocking collectives, exchange(): lax.all_to_all(x, axis, split_axis=0, concat_axis=0, tiled=True, axis_ind...  54.8 us
    pallas_call x4, Pallas kernels, call(): pl.pallas_call(kernel, out_shape=jax.ShapeDtypeStruct(shape, dtype), in_s...  5.8 us
    all_to_all x1, starting transfers between devices, exchange(): lax.all_to_all(x, axis, split_axis=0, concat_axis=0, tiled=True, axis_ind...  5.32 us
  transfers between devices with their start and end apart: 1, of which 0 were waited for; matrix products, arithmetic and copies ran while one was open for 0% of the time, Pallas kernels for 1%

profile of v8, /device:TPU:32, one launch (start us, length us, event | category | flops | bytes accessed | tf_op | source)
XLA Modules:
  0.0 128.1 jit_solution(17308864359407055112)
XLA Ops:
  0.0 2.5 %relay.1 = bf16[8,1024,128]{2,1,0:T(8,128)(2,1)} custom-call(bf16[512,1024]{1,0:T(8,128)(2,1)} %k_ref.1, bf16[512,1024]{1,0:T(8,128)(2,1)} %v_ref.1), custom_call_target="tpu_custom_call" | custom-call | tf_op jit(solution)/shard_map/relay/pallas_call | solution.py:219
  2.5 0.0 copy-start.2
  2.5 5.3 %all-to-all-start = ((bf16[8,1024,128]{2,1,0:T(8,128)(2,1)}), bf16[8,1024,128]{2,1,0:T(8,128)(2,1)S(1)}, u32[]{:S(2)}, u32[]{:S(2)}) async-start(bf16[8,1024,128]{2,1,0:T(8,128)(2,1)} %relay.1), calls=%async_computation | async-start | bytes 4194304 | tf_op jit(solution)/shard_map/all_to_all | solution.py:215
  7.8 1.7 %find.1 = (f32[8,256]{1,0:T(8,128)}, f32[8,128]{1,0:T(8,128)}) custom-call(s32[16,512]{1,0:T(8,128)} %bitcast.3), custom_call_target="tpu_custom_call" | custom-call | tf_op jit(solution)/shard_map/find/pallas_call | solution.py:236
  9.6 0.0 copy-done.2
  9.6 0.1 reduce
  9.6 1.8 %all_gather.9 = bf16[2,8,512]{2,1,0:T(8,128)(2,1)S(1)} all-gather(bf16[1,8,512]{2,1,0:T(8,128)(2,1)S(1)} %all_gather_reshape.3), channel_id=1, replica_groups={{0,16},{32,48},{64,80},{96,112},{128,144},{160,176},{192,208},{224,240}..., dimensions={0}, use_global_device_ids=true | all-gather | bytes 24576 | tf_op jit(solution)/shard_map/all_gather | solution.py:246
  11.5 55.3 %all-gather = bf16[32,8,512]{2,1,0:T(8,128)(2,1)S(1)} all-gather(bf16[2,8,512]{2,1,0:T(8,128)(2,1)S(1)} %all_gather.9), channel_id=2, replica_groups={{16,48,80,112,144,176,208,240,272,304,336,368,400,432,464,496},{17,49,8..., dimensions={0}, use_global_device_ids=true | all-gather | bytes 278528 | tf_op jit(solution)/shard_map/all_gather | solution.py:247
  66.7 0.0 all-to-all-done.kv_ref
  66.7 0.0 copy-start
  66.7 0.7 copy-done
  67.4 0.0 copy-start.1
  67.4 0.3 select.1
  67.7 12.1 %all_to_all.20.x_ref = bf16[32,8,512]{2,1,0:T(8,128)(2,1)S(1)} all-to-all(bf16[32,8,512]{2,1,0:T(8,128)(2,1)S(1)} %select.1), channel_id=1, replica_groups={{0,1,2,3,4,5,6,7,8,9,10,11,12,13,14,15,16,17,18,19,20,21,22,23,24,25,26..., dimensions={0} | all-to-all | bytes 524288 | tf_op jit(solution)/shard_map/all_to_all | solution.py:215
  79.9 3.3 %attend.1 = bf16[32,8,640]{2,1,0:T(8,128)(2,1)S(1)} custom-call(bf16[32,8,512]{2,1,0:T(8,128)(2,1)S(1)} %all_to_all.20.x_ref, bf16[8,1024,128]{2,1,0:T(8,128)(2,1)S(1)} %all-to-all-done.kv_ref), custom_call_target="tpu_custom_call" | custom-call | tf_op jit(solution)/shard_map/attend/pallas_call | solution.py:190
  83.1 13.0 %all_to_all.21.y_ref = bf16[32,8,640]{2,1,0:T(8,128)(2,1)S(1)} all-to-all(bf16[32,8,640]{2,1,0:T(8,128)(2,1)S(1)} %attend.1), channel_id=1, replica_groups={{0,1,2,3,4,5,6,7,8,9,10,11,12,13,14,15,16,17,18,19,20,21,22,23,24,25,26..., dimensions={0} | all-to-all | bytes 655360 | tf_op jit(solution)/shard_map/all_to_all | solution.py:215
  96.2 0.0 copy-done.1
  96.2 1.3 %merge.1 = bf16[16,8,640]{2,1,0:T(8,128)(2,1)S(1)} custom-call(f32[8,128]{1,0:T(8,128)S(1)} %copy-done.1, bf16[32,8,640]{2,1,0:T(8,128)(2,1)S(1)} %all_to_all.21.y_ref), custom_call_target="tpu_custom_call" | custom-call | tf_op jit(solution)/shard_map/merge/pallas_call | solution.py:190
  97.5 29.7 %all_to_all.22.a_ref = bf16[16,8,640]{2,1,0:T(8,128)(2,1)S(1)} all-to-all(bf16[16,8,640]{2,1,0:T(8,128)(2,1)S(1)} %merge.1), channel_id=1, replica_groups={{0,32,64,96,128,160,192,224,256,288,320,352,384,416,448,480},{16,48,80,..., dimensions={0} | all-to-all | bytes 327680 | tf_op jit(solution)/shard_map/all_to_all | solution.py:215
  127.1 0.9 last.1
  (1 shorter events, 0.0 us)
Async XLA Ops:
  2.5 7.1 %copy-start.2 = (bf16[1,4096]{1,0:T(2,128)(2,1)S(1)}, bf16[1,4096]{1,0:T(2,128)(2,1)}, u32[]{:S(2)}) copy-start(bf16[1,4096]{1,0:T(2,128)(2,1)} %param.4) | copy-start | bytes 24580
  2.5 64.2 %all-to-all-start = ((bf16[8,1024,128]{2,1,0:T(8,128)(2,1)}), bf16[8,1024,128]{2,1,0:T(8,128)(2,1)S(1)}, u32[]{:S(2)}, u32[]{:S(2)}) async-start(bf16[8,1024,128]{2,1,0:T(8,128)(2,1)} %relay.1), calls=%async_computation | async-start | bytes 4194304 | tf_op jit(solution)/shard_map/all_to_all | solution.py:215
  66.7 0.7 copy-start
  67.4 28.7 %copy-start.1 = (f32[8,128]{1,0:T(8,128)S(1)}, f32[8,128]{1,0:T(8,128)}, u32[]{:S(2)}) copy-start(f32[8,128]{1,0:T(8,128)} %get-tuple-element.13.pos_ref) | copy-start | bytes 12292

commit v9 on v8

v9 whole, which is shorter than its diff:
```python
import functools

import jax
import jax.numpy as jnp
from jax import lax
from jax.experimental import pallas as pl
from jax.experimental.pallas import tpu as pltpu
from jax.sharding import PartitionSpec as P

QUERY_HEADS = 32
KEY_HEADS = 8
HEAD_WIDTH = 128
BLOCK = 4096
QUERY_PER_KEY = 4
LOG2E = 1.4426950408889634
NEVER = -1e30

FEAT = QUERY_PER_KEY * HEAD_WIDTH
SLOTS = 8
SLABS = 8
HALF = KEY_HEADS // 2
PARTNER = (1, 4)
STAT = 128
ONE_LANE = 12


def half_of(core, s):
    return jnp.where(core == 0, s % 2, s // 4)


def pieces(x):
    hi = x.astype(jnp.bfloat16).astype(jnp.float32)
    rest = x - hi
    mid = rest.astype(jnp.bfloat16).astype(jnp.float32)
    return hi, mid, rest - mid


def stat_lanes(lse):
    lane = lax.broadcasted_iota(jnp.int32, (lse[0].shape[0], STAT), 1)
    stat = jnp.zeros(lane.shape, jnp.float32)
    for at, x in enumerate(lse):
        for k, piece in enumerate(pieces(x)):
            stat = jnp.where(lane == at * 3 + k, piece, stat)
    return stat


def find_kernel(ids_ref, pos_ref):
    count_x, count_y = lax.axis_size("sx"), lax.axis_size("sy")
    index_x, index_y = lax.axis_index("sx"), lax.axis_index("sy")
    lanes = 128
    r = lax.broadcasted_iota(jnp.int32, (count_x * count_y, lanes), 0)
    c = lax.broadcasted_iota(jnp.int32, (count_x * count_y, lanes), 1)
    row = (c % (count_x // 2)) * 2 + c // (count_x // 2)
    own = jnp.where((r == row * count_y + index_y) & (c < count_x), 1.0, 0.0).astype(jnp.bfloat16)
    ids = ids_ref[...].astype(jnp.float32).astype(jnp.bfloat16)
    column = jnp.dot(ids, own, preferred_element_type=jnp.float32)
    b = lax.broadcasted_iota(jnp.int32, (8, lanes), 0)
    c = lax.broadcasted_iota(jnp.int32, (8, lanes), 1)
    named = jnp.zeros((8, lanes), jnp.float32)
    for block in range(2):
        wanted = (index_x * 2 + block).astype(jnp.float32)
        hit = jnp.max(jnp.where(column == wanted, 1.0, 0.0), axis=0, keepdims=True)
        named = jnp.where((b == block) & (c < count_x), hit, named)
    r = lax.broadcasted_iota(jnp.int32, (lanes, lanes), 0)
    c = lax.broadcasted_iota(jnp.int32, (lanes, lanes), 1)
    before = jnp.where(r < c, 1.0, 0.0).astype(jnp.bfloat16)
    rank = jnp.dot(named.astype(jnp.bfloat16), before, preferred_element_type=jnp.float32)
    pos = jnp.where(named > 0.5, rank, -1.0).astype(jnp.bfloat16)
    shape = (lanes, pos_ref.shape[1])
    r = lax.broadcasted_iota(jnp.int32, shape, 0)
    c = lax.broadcasted_iota(jnp.int32, shape, 1)
    heads = jnp.where(r == c // KEY_HEADS, 1.0, 0.0).astype(jnp.bfloat16)
    pos_ref[...] = jnp.dot(pos, heads, preferred_element_type=jnp.float32)


def slot_onehot(pos, dtype):
    shape = (KEY_HEADS * SLOTS, pos.shape[1])
    r = lax.broadcasted_iota(jnp.int32, shape, 0)
    c = lax.broadcasted_iota(jnp.int32, shape, 1)
    hit = (pos == (r % SLOTS).astype(jnp.float32)) & (r // SLOTS == c % KEY_HEADS)
    return jnp.where(hit, 1.0, 0.0).astype(dtype)


def relay_kernel(k_ref, v_ref, out_ref, here, in_sems, out_sems):
    core = lax.axis_index("sx") % 2
    theirs = 1 - half_of(core, lax.axis_index("sy") % SLABS)
    tokens, width = k_ref.shape[0], out_ref.shape[1]
    lanes = pl.ds(pl.multiple_of(theirs * width, width), width)
    chunks = in_sems.shape[1]
    step = tokens // chunks
    pairs = [(i, j) for i in range(chunks) for j in range(2)]
    there = (k_ref, v_ref)
    arriving, leaving = {}, []
    for i, j in pairs:
        to = pl.ds(j * tokens + i * step, step)
        arriving[i, j] = pltpu.make_async_copy(there[j].at[pl.ds(i * step, step), lanes], here.at[to], in_sems.at[j, i])
        arriving[i, j].start()
    for i, j in pairs:
        arriving[i, j].wait()
        to = pl.ds(j * tokens + i * step, step)
        leaving.append(pltpu.make_async_copy(here.at[to], out_ref.at[to], out_sems.at[j, i]))
        leaving[-1].start()
    for copy in leaving:
        copy.wait()


def select_kernel(pos_ref, q_ref, out_ref, halves):
    core = lax.axis_index("sx") % 2
    q = q_ref[...].astype(jnp.float32).reshape(-1, FEAT).astype(jnp.bfloat16)
    for p in range(2):
        hot = slot_onehot(pos_ref[p : p + 1, :], jnp.bfloat16)
        picked = jnp.dot(hot, q, preferred_element_type=jnp.float32)
        for h in range(KEY_HEADS):
            lanes = slice((h % HALF) * FEAT, (h % HALF + 1) * FEAT)
            halves[p, h // HALF, :, lanes] = picked[h * SLOTS : (h + 1) * SLOTS].astype(jnp.bfloat16)
        for s in range(SLABS):
            out_ref[p * SLABS + s] = halves[p, half_of(core, s)]


def attend_kernel(x_ref, k_ref, v_ref, kv_ref, y_ref):
    scale = HEAD_WIDTH ** (-0.5) * LOG2E
    mine = half_of(lax.axis_index("sx") % 2, lax.axis_index("sy") % SLABS)
    columns, tokens = x_ref.shape[0], k_ref.shape[0]
    rows = columns * SLOTS
    ones = jnp.ones((tokens, HEAD_WIDTH), jnp.bfloat16)
    ends = []
    for h in range(HALF):
        x = x_ref[:, :, h * FEAT : (h + 1) * FEAT].astype(jnp.float32).reshape(rows, FEAT).astype(jnp.bfloat16)
        q = [x[:, g * HEAD_WIDTH : (g + 1) * HEAD_WIDTH] for g in range(QUERY_PER_KEY)]
        q = jnp.concatenate(q, axis=0)
        there = pl.ds(pl.multiple_of((mine * HALF + h) * HEAD_WIDTH, HEAD_WIDTH), HEAD_WIDTH)
        here = slice(h * HEAD_WIDTH, (h + 1) * HEAD_WIDTH)
        slabs = ((k_ref[:, there], v_ref[:, there]), (kv_ref[:tokens, here], kv_ref[tokens:, here]))
        tops, sums = [], []
        for k, v in slabs:
            v = jnp.concatenate([v, ones], axis=1)
            s = lax.dot_general(q, k, (((1,), (1,)), ((), ())), preferred_element_type=jnp.float32)
            m = jnp.max(s, axis=1, keepdims=True)
            w = jnp.exp2((s - m) * scale).astype(jnp.bfloat16)
            tops.append(m)
            sums.append(jnp.dot(w, v, preferred_element_type=jnp.float32))
        top = functools.reduce(jnp.maximum, tops)
        both = functools.reduce(jnp.add, [jnp.exp2((m - top) * scale) * o for m, o in zip(tops, sums)])
        total = both[:, HEAD_WIDTH:]
        out = both[:, :HEAD_WIDTH] / total
        lse = top * scale + jnp.log2(total[:, :1])
        for g in range(QUERY_PER_KEY):
            part = out[g * rows : (g + 1) * rows].reshape(columns, SLOTS, HEAD_WIDTH).astype(jnp.bfloat16)
            at = (h * QUERY_PER_KEY + g) * HEAD_WIDTH
            y_ref[:, :, at : at + HEAD_WIDTH] = part
            ends.append(lse[g * rows : (g + 1) * rows])
    stat = stat_lanes(ends).reshape(columns, SLOTS, STAT).astype(jnp.bfloat16)
    y_ref[:, :, HALF * FEAT :] = stat


def merge_kernel(pos_ref, y_ref, out_ref):
    core = lax.axis_index("sx") % 2
    flip = (((0,), (0,)), ((), ()))
    data, lse = [], []
    for p in range(2):
        tall = []
        for half in range(2):
            froms = [p * SLABS + jnp.where(core == 0, 2 * t + half, HALF * half + t) for t in range(4)]
            ends = []
            for s in froms:
                stat = y_ref[s, :, HALF * FEAT :].astype(jnp.float32)
                ends.append(stat + (pltpu.roll(stat, STAT - 1, 1) + pltpu.roll(stat, STAT - 2, 1)))
            top = functools.reduce(jnp.maximum, ends)
            weights = [jnp.exp2(x - top) for x in ends]
            total = functools.reduce(jnp.add, weights)
            inverse = 1.0 / total
            weights = [w * inverse for w in weights]
            block = top + jnp.log2(total)
            for h in range(HALF):
                pair = []
                for g in range(QUERY_PER_KEY):
                    n = h * QUERY_PER_KEY + g
                    lanes = slice(n * HEAD_WIDTH, (n + 1) * HEAD_WIDTH)
                    terms = [w[:, 3 * n : 3 * n + 1] * y_ref[s, :, lanes].astype(jnp.float32) for w, s in zip(weights, froms)]
                    pair.append(functools.reduce(jnp.add, terms))
                shift = 3 * h * QUERY_PER_KEY
                stat = block if shift == 0 else pltpu.roll(block, STAT - shift, 1)
                lane = lax.broadcasted_iota(jnp.int32, stat.shape, 1)
                stat = jnp.where(lane == ONE_LANE, 1.0, jnp.where(lane < ONE_LANE, stat, 0.0))
                tall.append(jnp.concatenate(pair + [stat], axis=1))
        hot = slot_onehot(pos_ref[p : p + 1, :], jnp.float32)
        dense = lax.dot_general(
            hot,
            jnp.concatenate(tall, axis=0),
            flip,
            precision=lax.Precision.HIGHEST,
            preferred_element_type=jnp.float32,
        )
        named = dense[:, FEAT + ONE_LANE : FEAT + ONE_LANE + 1] > 0.5
        data.append(dense)
        lse.append(
            [jnp.where(named, dense[:, FEAT + 3 * g : FEAT + 3 * g + 1], NEVER) for g in range(QUERY_PER_KEY)]
        )
    combine_two(data, lse, out_ref)


def combine_two(data, lse, out_ref):
    shape = out_ref.shape[:-1]
    ends = []
    for g in range(QUERY_PER_KEY):
        a, b = lse[0][g], lse[1][g]
        top = jnp.maximum(a, b)
        wa, wb = jnp.exp2(a - top), jnp.exp2(b - top)
        total = wa + wb
        inverse = 1.0 / total
        lanes = slice(g * HEAD_WIDTH, (g + 1) * HEAD_WIDTH)
        mixed = data[0][:, lanes] * (wa * inverse) + data[1][:, lanes] * (wb * inverse)
        out_ref[..., lanes] = mixed.reshape(*shape, HEAD_WIDTH).astype(out_ref.dtype)
        ends.append(top + jnp.log2(total))
    if out_ref.dtype == jnp.float32:
        lane = lax.broadcasted_iota(jnp.int32, (mixed.shape[0], STAT), 1)
        stat = jnp.zeros(lane.shape, jnp.float32)
        for g in range(QUERY_PER_KEY):
            stat = jnp.where(lane == g, ends[g], stat)
    else:
        stat = stat_lanes(ends)
    out_ref[..., FEAT:] = stat.reshape(*shape, STAT).astype(out_ref.dtype)


def pair_kernel(a_ref, out_ref):
    data = [a_ref[c, :, :FEAT] for c in range(2)]
    lse = [[a_ref[c, :, FEAT + g : FEAT + g + 1] for g in range(QUERY_PER_KEY)] for c in range(2)]
    combine_two(data, lse, out_ref)


def last_kernel(a_ref, out_ref):
    for g in range(QUERY_PER_KEY):
        at = FEAT + 3 * g
        lse = [a_ref[:, :, at + k : at + k + 1].astype(jnp.float32) for k in range(3)]
        lse = lse[0] + (lse[1] + lse[2])
        weight = jnp.exp2(lse - jnp.max(lse, axis=0, keepdims=True))
        total = jnp.sum(weight, axis=0)
        lanes = slice(g * HEAD_WIDTH, (g + 1) * HEAD_WIDTH)
        mixed = jnp.sum(a_ref[:, :, lanes].astype(jnp.float32) * weight, axis=0) / total
        for h in range(KEY_HEADS):
            head = h * FEAT + g * HEAD_WIDTH
            out_ref[:, head : head + HEAD_WIDTH] = mixed[h : h + 1].astype(jnp.bfloat16)


def call(kernel, shape, dtype, name, *args, scratch=()):
    return pl.pallas_call(
        kernel,
        out_shape=jax.ShapeDtypeStruct(shape, dtype),
        in_specs=[pl.BlockSpec(memory_space=pltpu.VMEM)] * len(args),
        out_specs=pl.BlockSpec(memory_space=pltpu.VMEM),
        scratch_shapes=list(scratch),
        compiler_params=pltpu.CompilerParams(vmem_limit_bytes=40 * 1024 * 1024),
        name=name,
    )(*args)


def per_device(queries, keys, values, block_ids):
    count_x = lax.axis_size("sx")
    count_y = lax.axis_size("sy")
    count_z = count_x // 2
    tokens = keys.shape[0]
    cores = [[2 * z, 2 * z + 1] for z in range(count_z)]
    along_z = [[2 * z + c for z in range(count_z)] for c in range(2)]
    partners = [
        (x * count_y + y, x * count_y + (y ^ PARTNER[x % 2])) for x in range(count_x) for y in range(count_y)
    ]

    def exchange(x, axis, groups=None):
        return lax.all_to_all(x, axis, split_axis=0, concat_axis=0, tiled=True, axis_index_groups=groups)

    own = jnp.broadcast_to(queries.reshape(1, KEY_HEADS, FEAT), (count_z, KEY_HEADS, FEAT))
    rows = exchange(own, "sx", along_z)

    hbm = pl.BlockSpec(memory_space=pltpu.HBM)
    width = HALF * HEAD_WIDTH
    kv = pl.pallas_call(
        relay_kernel,
        out_shape=jax.ShapeDtypeStruct((2 * tokens, width), keys.dtype),
        in_specs=[hbm, hbm],
        out_specs=hbm,
        scratch_shapes=[
            pltpu.VMEM((2 * tokens, width), keys.dtype),
            pltpu.SemaphoreType.DMA((2, 4)),
            pltpu.SemaphoreType.DMA((2, 4)),
        ],
        compiler_params=pltpu.CompilerParams(vmem_limit_bytes=60 * 1024 * 1024),
        name="relay",
    )(keys, values)
    kv = lax.ppermute(kv, ("sx", "sy"), partners)

    pos = call(find_kernel, (8, count_x * KEY_HEADS), jnp.float32, "find", block_ids.T)
    rows = lax.all_gather(rows, "sx", axis=0, axis_index_groups=cores)
    rows = rows.reshape(count_x, KEY_HEADS, FEAT)
    asked = call(
        select_kernel,
        (count_y, SLOTS, HALF * FEAT),
        jnp.bfloat16,
        "select",
        pos,
        rows,
        scratch=[pltpu.VMEM((2, 2, SLOTS, HALF * FEAT), jnp.bfloat16)],
    )
    asked = exchange(asked, "sy")
    part = call(attend_kernel, (count_y, SLOTS, HALF * FEAT + STAT), jnp.bfloat16, "attend", asked, keys, values, kv)
    part = exchange(part, "sy")
    part = call(merge_kernel, (2, count_z * KEY_HEADS, FEAT + STAT), jnp.float32, "merge", pos, part)
    part = exchange(part, "sx", cores)
    part = call(pair_kernel, (count_z, KEY_HEADS, FEAT + STAT), jnp.bfloat16, "pair", part)
    part = exchange(part, "sx", along_z)
    return call(last_kernel, (1, KEY_HEADS * FEAT), jnp.bfloat16, "last", part)


def solution(mesh):
    return jax.shard_map(
        per_device,
        mesh=mesh,
        in_specs=(P(("sx", "sy"), None), P(("sx", "sy"), None), P(("sx", "sy"), None), P()),
        out_specs=P(("sx", "sy"), None),
        check_vma=False,
    )
```

time: 129 us -> 97.7 us (0.76)
  blocking collectives: 112 us -> 59 us
  starting transfers between devices: 5.32 us -> 18.6 us
  waiting for transfers between devices: 0.01 us -> 8.29 us
    all_gather x2 -> x1, blocking collectives: 57.1 us -> 1.98 us  [per_device(): rows = lax.all_gather(rows, 'sx', axis=0, axis_index_groups=cores)]
    all_to_all x1, starting transfers between devices: 5.32 us -> 15.2 us  [exchange(): lax.all_to_all(x, axis, split_axis=0, concat_axis=0, tiled=True, axis_ind...]
    all_to_all x1, waiting for transfers between devices: 0.01 us -> 8.29 us  [exchange(): lax.all_to_all(x, axis, split_axis=0, concat_axis=0, tiled=True, axis_ind...]
    ppermute x0 -> x1, starting transfers between devices: none -> 3.4 us  [per_device(): kv = lax.ppermute(kv, ('sx', 'sy'), partners)]
    all_to_all x3 -> x4, blocking collectives: 54.8 us -> 57 us  [exchange(): lax.all_to_all(x, axis, split_axis=0, concat_axis=0, tiled=True, axis_ind...]
    pallas_call x2 -> x1, Pallas kernels: 4.22 us -> 2.12 us  [per_device(): pl.pallas_call(relay_kernel, out_shape=jax.ShapeDtypeStruct((2 * tokens,...]
    pallas_call x4 -> x6, Pallas kernels: 5.8 us -> 7.64 us  [call(): pl.pallas_call(kernel, out_shape=jax.ShapeDtypeStruct(shape, dtype), in_s...]
  transfers between devices with their start and end apart: 1 -> 2, of which waited for: 0 -> 1; matrix products, arithmetic and copies ran while one was open for 0% -> 0% of each run, Pallas kernels for 1% -> 3%
where the time goes in v9:
time: 97.7 us; the launch traced here: 97.2 us
  blocking collectives  59 us (60%)
  starting transfers between devices  18.6 us (19%)
  Pallas kernels  9.76 us (10%)
  waiting for transfers between devices  8.29 us (8%)
    all_to_all x4, blocking collectives, exchange(): lax.all_to_all(x, axis, split_axis=0, concat_axis=0, tiled=True, axis_ind...  57 us
    all_to_all x1, starting transfers between devices, exchange(): lax.all_to_all(x, axis, split_axis=0, concat_axis=0, tiled=True, axis_ind...  15.2 us
    all_to_all x1, waiting for transfers between devices, exchange(): lax.all_to_all(x, axis, split_axis=0, concat_axis=0, tiled=True, axis_ind...  8.29 us
    pallas_call x6, Pallas kernels, call(): pl.pallas_call(kernel, out_shape=jax.ShapeDtypeStruct(shape, dtype), in_s...  7.64 us
    ppermute x1, starting transfers between devices, per_device(): kv = lax.ppermute(kv, ('sx', 'sy'), partners)  3.4 us
    pallas_call x1, Pallas kernels, per_device(): pl.pallas_call(relay_kernel, out_shape=jax.ShapeDtypeStruct((2 * tokens,...  2.12 us
    all_gather x1, blocking collectives, per_device(): rows = lax.all_gather(rows, 'sx', axis=0, axis_index_groups=cores)  1.98 us
  transfers between devices with their start and end apart: 2, of which 1 were waited for; matrix products, arithmetic and copies ran while one was open for 0% of the time, Pallas kernels for 3%

profile of v9, /device:TPU:32, one launch (start us, length us, event | category | flops | bytes accessed | tf_op | source)
XLA Modules:
  0.0 97.2 jit_solution(1528640487232005195)
XLA Ops:
  0.0 0.8 reduce
  0.8 0.7 broadcast_in_dim.8
  1.4 15.2 %all-to-all-start = ((bf16[16,8,512]{2,1,0:T(8,128)(2,1)}), bf16[16,8,512]{2,1,0:T(8,128)(2,1)S(1)}, u32[]{:S(2)}, u32[]{:S(2)}) async-start(bf16[16,8,512]{2,1,0:T(8,128)(2,1)} %broadcast_in_dim.8), calls=%async_computation | async-start | bytes 262144 | tf_op jit(solution)/shard_map/all_to_all | solution.py:269
  16.7 0.0 copy-start.2
  16.7 2.1 %relay.1 = bf16[1024,512]{1,0:T(8,128)(2,1)} custom-call(bf16[512,1024]{1,0:T(8,128)(2,1)} %k_ref.3, bf16[512,1024]{1,0:T(8,128)(2,1)} %v_ref.3), custom_call_target="tpu_custom_call" | custom-call | tf_op jit(solution)/shard_map/relay/pallas_call | solution.py:276
  18.8 3.4 %collective-permute-start = (bf16[1024,512]{1,0:T(8,128)(2,1)}, bf16[1024,512]{1,0:T(8,128)(2,1)S(1)}, u32[]{:S(2)}, u32[]{:S(2)}) collective-permute-start(bf16[1024,512]{1,0:T(8,128)(2,1)} %relay.1), channel_id=1, source_target_pairs={{0,1},{1,0},{2,3},{3,2},{4,5},{5,4},{6,7},{7,6},{8,9},{9,8},{10,11... | collective-permute-start | bytes 3145736 | tf_op jit(solution)/shard_map/ppermute | solution.py:289
  22.2 0.0 copy-done.2
  22.2 0.4 find.1.pos_ref
  22.6 0.0 copy-start
  22.6 0.0 copy-start.1
  22.6 8.3 %all-to-all-done = bf16[16,8,512]{2,1,0:T(8,128)(2,1)S(1)} async-done(((bf16[16,8,512]{2,1,0:T(8,128)(2,1)}), bf16[16,8,512]{2,1,0:T(8,128)(2,1)S(1)}, u32[]{:S(2)}, u32[]{:S(2)}) %all-to-all-start) | async-done | bytes 131104 | tf_op jit(solution)/shard_map/all_to_all | solution.py:269
  30.9 2.0 %all-gather.q_ref = bf16[32,8,512]{2,1,0:T(8,128)(2,1)S(1)} all-gather(bf16[16,8,512]{2,1,0:T(8,128)(2,1)S(1)} %all-to-all-done), channel_id=2, replica_groups={{0,16},{32,48},{64,80},{96,112},{128,144},{160,176},{192,208},{224,240}..., dimensions={0}, use_global_device_ids=true | all-gather | bytes 393216 | tf_op jit(solution)/shard_map/all_gather | solution.py:292
  32.9 0.2 select.1
  33.1 18.7 %all_to_all.25.x_ref = bf16[16,8,2048]{2,1,0:T(8,128)(2,1)S(1)} all-to-all(bf16[16,8,2048]{2,1,0:T(8,128)(2,1)S(1)} %select.1), channel_id=1, replica_groups=mesh['sx'=32,'sy'=16] {'sy'}, dimensions={0} | all-to-all | bytes 1048576 | tf_op jit(solution)/shard_map/all_to_all | solution.py:269
  51.8 0.0 collective-permute-done.kv_ref
  51.8 0.0 copy-done
  51.8 0.0 copy-done.1
  51.8 3.4 %attend.1 = bf16[16,8,2176]{2,1,0:T(8,128)(2,1)S(1)} custom-call(bf16[16,8,2048]{2,1,0:T(8,128)(2,1)S(1)} %all_to_all.25.x_ref, bf16[512,1024]{1,0:T(8,128)(2,1)S(1)} %copy-done, bf16[512,1024]{1,0:T(8,128)(2,1)S(1)} %copy-done.1, bf16[1024,512]{1,0:T(8,128)(2,1)S(1)} %collective-permute-done.kv_ref), custom_call_target="tpu_custom_call" | custom-call | tf_op jit(solution)/shard_map/attend/pallas_call | solution.py:246
  55.2 14.5 %all_to_all.26.y_ref = bf16[16,8,2176]{2,1,0:T(8,128)(2,1)S(1)} all-to-all(bf16[16,8,2176]{2,1,0:T(8,128)(2,1)S(1)} %attend.1), channel_id=1, replica_groups=mesh['sx'=32,'sy'=16] {'sy'}, dimensions={0} | all-to-all | bytes 1114112 | tf_op jit(solution)/shard_map/all_to_all | solution.py:269
  69.7 2.3 %merge.1 = f32[2,128,640]{2,1,0:T(8,128)S(1)} custom-call(f32[8,256]{1,0:T(8,128)S(1)} %find.1.pos_ref, bf16[16,8,2176]{2,1,0:T(8,128)(2,1)S(1)} %all_to_all.26.y_ref), custom_call_target="tpu_custom_call" | custom-call | tf_op jit(solution)/shard_map/merge/pallas_call | solution.py:246
  72.0 4.3 %all_to_all.27.a_ref = f32[2,128,640]{2,1,0:T(8,128)S(1)} all-to-all(f32[2,128,640]{2,1,0:T(8,128)S(1)} %merge.1), channel_id=1, replica_groups={{0,16},{32,48},{64,80},{96,112},{128,144},{160,176},{192,208},{224,240}..., dimensions={0} | all-to-all | bytes 1310720 | tf_op jit(solution)/shard_map/all_to_all | solution.py:269
  76.3 0.3 pair.1
  76.6 19.6 %all_to_all.28.a_ref = bf16[16,8,640]{2,1,0:T(8,128)(2,1)S(1)} all-to-all(bf16[16,8,640]{2,1,0:T(8,128)(2,1)S(1)} %pair.1), channel_id=1, replica_groups={{0,32,64,96,128,160,192,224,256,288,320,352,384,416,448,480},{16,48,80,..., dimensions={0} | all-to-all | bytes 327680 | tf_op jit(solution)/shard_map/all_to_all | solution.py:269
  96.3 0.9 last.1
  (1 shorter events, 0.0 us)
Async XLA Ops:
  1.4 29.4 %all-to-all-start = ((bf16[16,8,512]{2,1,0:T(8,128)(2,1)}), bf16[16,8,512]{2,1,0:T(8,128)(2,1)S(1)}, u32[]{:S(2)}, u32[]{:S(2)}) async-start(bf16[16,8,512]{2,1,0:T(8,128)(2,1)} %broadcast_in_dim.8), calls=%async_computation | async-start | bytes 262144 | tf_op jit(solution)/shard_map/all_to_all | solution.py:269
  16.7 5.5 %copy-start.2 = (s32[512,16]{0,1:T(8,128)S(1)}, s32[512,16]{0,1:T(8,128)}, u32[]{:S(2)}) copy-start(s32[512,16]{0,1:T(8,128)} %param.7) | copy-start | bytes 98308
  18.8 33.0 %collective-permute-start = (bf16[1024,512]{1,0:T(8,128)(2,1)}, bf16[1024,512]{1,0:T(8,128)(2,1)S(1)}, u32[]{:S(2)}, u32[]{:S(2)}) collective-permute-start(bf16[1024,512]{1,0:T(8,128)(2,1)} %relay.1), channel_id=1, source_target_pairs={{0,1},{1,0},{2,3},{3,2},{4,5},{5,4},{6,7},{7,6},{8,9},{9,8},{10,11... | collective-permute-start | bytes 3145736 | tf_op jit(solution)/shard_map/ppermute | solution.py:289
  22.6 29.2 %copy-start = (bf16[512,1024]{1,0:T(8,128)(2,1)S(1)}, bf16[512,1024]{1,0:T(8,128)(2,1)}, u32[]{:S(2)}) copy-start(bf16[512,1024]{1,0:T(8,128)(2,1)} %k_ref.3) | copy-start | bytes 3145732
  22.6 29.2 %copy-start.1 = (bf16[512,1024]{1,0:T(8,128)(2,1)S(1)}, bf16[512,1024]{1,0:T(8,128)(2,1)}, u32[]{:S(2)}) copy-start(bf16[512,1024]{1,0:T(8,128)(2,1)} %v_ref.3) | copy-start | bytes 3145732

commit v10 on v9

v10 whole, which is shorter than its diff:
```python
import functools

import jax
import jax.numpy as jnp
from jax import lax
from jax.experimental import pallas as pl
from jax.experimental.pallas import tpu as pltpu
from jax.sharding import PartitionSpec as P

QUERY_HEADS = 32
KEY_HEADS = 8
HEAD_WIDTH = 128
BLOCK = 4096
QUERY_PER_KEY = 4
LOG2E = 1.4426950408889634
NEVER = -1e30

FEAT = QUERY_PER_KEY * HEAD_WIDTH
SLOTS = 8
SLABS = 8
SHARE = KEY_HEADS // 4
PARTNERS = ((1, 4, 5), (3, 4, 7))
STAT = 128
ONE_LANE = 12


def share_of(s):
    return (s // 4) * 2 + s % 2


def pieces(x):
    hi = x.astype(jnp.bfloat16).astype(jnp.float32)
    rest = x - hi
    mid = rest.astype(jnp.bfloat16).astype(jnp.float32)
    return hi, mid, rest - mid


def stat_lanes(lse):
    lane = lax.broadcasted_iota(jnp.int32, (lse[0].shape[0], STAT), 1)
    stat = jnp.zeros(lane.shape, jnp.float32)
    for at, x in enumerate(lse):
        for k, piece in enumerate(pieces(x)):
            stat = jnp.where(lane == at * 3 + k, piece, stat)
    return stat


def find_kernel(ids_ref, pos_ref):
    count_x, count_y = lax.axis_size("sx"), lax.axis_size("sy")
    index_x, index_y = lax.axis_index("sx"), lax.axis_index("sy")
    lanes = 128
    r = lax.broadcasted_iota(jnp.int32, (count_x * count_y, lanes), 0)
    c = lax.broadcasted_iota(jnp.int32, (count_x * count_y, lanes), 1)
    row = (c % (count_x // 2)) * 2 + c // (count_x // 2)
    own = jnp.where((r == row * count_y + index_y) & (c < count_x), 1.0, 0.0).astype(jnp.bfloat16)
    ids = ids_ref[...].astype(jnp.float32).astype(jnp.bfloat16)
    column = jnp.dot(ids, own, preferred_element_type=jnp.float32)
    b = lax.broadcasted_iota(jnp.int32, (8, lanes), 0)
    c = lax.broadcasted_iota(jnp.int32, (8, lanes), 1)
    named = jnp.zeros((8, lanes), jnp.float32)
    for block in range(2):
        wanted = (index_x * 2 + block).astype(jnp.float32)
        hit = jnp.max(jnp.where(column == wanted, 1.0, 0.0), axis=0, keepdims=True)
        named = jnp.where((b == block) & (c < count_x), hit, named)
    r = lax.broadcasted_iota(jnp.int32, (lanes, lanes), 0)
    c = lax.broadcasted_iota(jnp.int32, (lanes, lanes), 1)
    before = jnp.where(r < c, 1.0, 0.0).astype(jnp.bfloat16)
    rank = jnp.dot(named.astype(jnp.bfloat16), before, preferred_element_type=jnp.float32)
    pos = jnp.where(named > 0.5, rank, -1.0).astype(jnp.bfloat16)
    shape = (lanes, pos_ref.shape[1])
    r = lax.broadcasted_iota(jnp.int32, shape, 0)
    c = lax.broadcasted_iota(jnp.int32, shape, 1)
    heads = jnp.where(r == c // KEY_HEADS, 1.0, 0.0).astype(jnp.bfloat16)
    pos_ref[...] = jnp.dot(pos, heads, preferred_element_type=jnp.float32)


def slot_onehot(pos):
    shape = (KEY_HEADS * SLOTS, pos.shape[1])
    r = lax.broadcasted_iota(jnp.int32, shape, 0)
    c = lax.broadcasted_iota(jnp.int32, shape, 1)
    hit = (pos == (r % SLOTS).astype(jnp.float32)) & (r // SLOTS == c % KEY_HEADS)
    return jnp.where(hit, 1.0, 0.0).astype(jnp.bfloat16)


def copies_kernel(q_ref, out_ref):
    q = q_ref[...].astype(jnp.float32)
    q = jnp.concatenate([q[:, h * FEAT : (h + 1) * FEAT] for h in range(KEY_HEADS)], axis=0).astype(jnp.bfloat16)
    for z in range(out_ref.shape[0]):
        out_ref[z] = q


def relay_kernel(k_ref, v_ref, *refs):
    count = len(PARTNERS[0])
    out_refs, (here, in_sems, out_sems) = refs[:count], refs[count:]
    core, s = lax.axis_index("sx") % 2, lax.axis_index("sy") % SLABS
    tokens, width = k_ref.shape[0], out_refs[0].shape[1]
    there = (k_ref, v_ref)
    arriving, leaving = {}, []
    for i in range(count):
        partner = jnp.bitwise_xor(s, jnp.where(core == 0, PARTNERS[0][i], PARTNERS[1][i]))
        lanes = pl.ds(pl.multiple_of(share_of(partner) * width, width), width)
        for j in range(2):
            to = here.at[i, pl.ds(j * tokens, tokens)]
            arriving[i, j] = pltpu.make_async_copy(there[j].at[:, lanes], to, in_sems.at[i, j])
            arriving[i, j].start()
    for i in range(count):
        for j in range(2):
            arriving[i, j].wait()
            part = pl.ds(j * tokens, tokens)
            leaving.append(pltpu.make_async_copy(here.at[i, part], out_refs[i].at[part], out_sems.at[i, j]))
            leaving[-1].start()
    for copy in leaving:
        copy.wait()


def select_kernel(pos_ref, q_ref, out_ref):
    q = q_ref[...].astype(jnp.float32).reshape(-1, FEAT).astype(jnp.bfloat16)
    for p in range(2):
        hot = slot_onehot(pos_ref[p : p + 1, :])
        picked = jnp.dot(hot, q, preferred_element_type=jnp.float32).astype(jnp.bfloat16)
        heads = [picked[h * SLOTS : (h + 1) * SLOTS] for h in range(KEY_HEADS)]
        for s in range(SLABS):
            for h in range(SHARE):
                out_ref[p * SLABS + s, :, h * FEAT : (h + 1) * FEAT] = heads[share_of(s) * SHARE + h]


def attend_kernel(x_ref, k_ref, v_ref, *refs):
    kv_refs, y_ref = refs[:-1], refs[-1]
    scale = HEAD_WIDTH ** (-0.5) * LOG2E
    mine = share_of(lax.axis_index("sy") % SLABS)
    columns, tokens = x_ref.shape[0], k_ref.shape[0]
    rows = columns * SLOTS
    ones = jnp.ones((tokens, HEAD_WIDTH), jnp.bfloat16)
    ends = []
    for h in range(SHARE):
        x = x_ref[:, :, h * FEAT : (h + 1) * FEAT].astype(jnp.float32).reshape(rows, FEAT).astype(jnp.bfloat16)
        q = [x[:, g * HEAD_WIDTH : (g + 1) * HEAD_WIDTH] for g in range(QUERY_PER_KEY)]
        q = jnp.concatenate(q, axis=0)
        there = pl.ds(pl.multiple_of((mine * SHARE + h) * HEAD_WIDTH, HEAD_WIDTH), HEAD_WIDTH)
        here = slice(h * HEAD_WIDTH, (h + 1) * HEAD_WIDTH)
        slabs = [(k_ref[:, there], v_ref[:, there])]
        slabs += [(kv_ref[:tokens, here], kv_ref[tokens:, here]) for kv_ref in kv_refs]
        tops, sums = [], []
        for k, v in slabs:
            v = jnp.concatenate([v, ones], axis=1)
            s = lax.dot_general(q, k, (((1,), (1,)), ((), ())), preferred_element_type=jnp.float32)
            m = jnp.max(s, axis=1, keepdims=True)
            w = jnp.exp2((s - m) * scale).astype(jnp.bfloat16)
            tops.append(m)
            sums.append(jnp.dot(w, v, preferred_element_type=jnp.float32))
        top = functools.reduce(jnp.maximum, tops)
        both = functools.reduce(jnp.add, [jnp.exp2((m - top) * scale) * o for m, o in zip(tops, sums)])
        total = both[:, HEAD_WIDTH:]
        out = both[:, :HEAD_WIDTH] / total
        lse = top * scale + jnp.log2(total[:, :1])
        for g in range(QUERY_PER_KEY):
            part = out[g * rows : (g + 1) * rows].reshape(columns, SLOTS, HEAD_WIDTH).astype(jnp.bfloat16)
            at = (h * QUERY_PER_KEY + g) * HEAD_WIDTH
            y_ref[:, :, at : at + HEAD_WIDTH] = part
            ends.append(lse[g * rows : (g + 1) * rows])
    stat = stat_lanes(ends).reshape(columns, SLOTS, STAT).astype(jnp.bfloat16)
    y_ref[:, :, SHARE * FEAT :] = stat


def merge_kernel(pos_ref, y_ref, mine_ref, theirs_ref):
    core = lax.axis_index("sx") % 2
    flip = (((0,), (0,)), ((), ()))
    lane = lax.broadcasted_iota(jnp.int32, (SLOTS, STAT), 1)
    data, lse = [], []
    for p in range(2):
        tall = []
        for share in range(4):
            froms = [p * SLABS + s for s in range(SLABS) if share_of(s) == share]
            ends = []
            for s in froms:
                stat = y_ref[s, :, SHARE * FEAT :].astype(jnp.float32)
                ends.append(stat + (pltpu.roll(stat, STAT - 1, 1) + pltpu.roll(stat, STAT - 2, 1)))
            top = functools.reduce(jnp.maximum, ends)
            weights = [jnp.exp2(x - top) for x in ends]
            total = functools.reduce(jnp.add, weights)
            inverse = 1.0 / total
            weights = [w * inverse for w in weights]
            block = top + jnp.log2(total)
            for h in range(SHARE):
                heads = []
                for g in range(QUERY_PER_KEY):
                    n = h * QUERY_PER_KEY + g
                    lanes = slice(n * HEAD_WIDTH, (n + 1) * HEAD_WIDTH)
                    terms = [w[:, 3 * n : 3 * n + 1] * y_ref[s, :, lanes].astype(jnp.float32) for w, s in zip(weights, froms)]
                    heads.append(functools.reduce(jnp.add, terms))
                shift = 3 * h * QUERY_PER_KEY
                stat = block if shift == 0 else pltpu.roll(block, STAT - shift, 1)
                stat = jnp.where(lane == ONE_LANE, 1.0, jnp.where(lane < ONE_LANE, stat, 0.0))
                tall.append(jnp.concatenate(heads + [stat], axis=1))
        tall = jnp.concatenate([x.astype(jnp.bfloat16) for x in pieces(jnp.concatenate(tall, axis=0))], axis=0)
        hot = jnp.concatenate([slot_onehot(pos_ref[p : p + 1, :])] * 3, axis=0)
        dense = lax.dot_general(hot, tall, flip, preferred_element_type=jnp.float32)
        named = dense[:, FEAT + ONE_LANE : FEAT + ONE_LANE + 1] > 0.5
        data.append(dense)
        lse.append(
            [jnp.where(named, dense[:, FEAT + 3 * g : FEAT + 3 * g + 1], NEVER) for g in range(QUERY_PER_KEY)]
        )
    rows = mine_ref.shape[0]
    for out_ref, is_first in ((mine_ref, core == 0), (theirs_ref, core == 1)):

        def side(x):
            return jnp.where(is_first, x[:rows], x[rows:])

        combine_two([side(x) for x in data], [[side(x) for x in y] for y in lse], out_ref)


def combine_two(data, lse, out_ref):
    shape = out_ref.shape[:-1]
    ends = []
    for g in range(QUERY_PER_KEY):
        a, b = lse[0][g], lse[1][g]
        top = jnp.maximum(a, b)
        wa, wb = jnp.exp2(a - top), jnp.exp2(b - top)
        total = wa + wb
        inverse = 1.0 / total
        lanes = slice(g * HEAD_WIDTH, (g + 1) * HEAD_WIDTH)
        mixed = data[0][:, lanes] * (wa * inverse) + data[1][:, lanes] * (wb * inverse)
        out_ref[..., lanes] = mixed.reshape(*shape, HEAD_WIDTH).astype(out_ref.dtype)
        ends.append(top + jnp.log2(total))
    if out_ref.dtype == jnp.float32:
        lane = lax.broadcasted_iota(jnp.int32, (mixed.shape[0], STAT), 1)
        stat = jnp.zeros(lane.shape, jnp.float32)
        for g in range(QUERY_PER_KEY):
            stat = jnp.where(lane == g, ends[g], stat)
    else:
        stat = stat_lanes(ends)
    out_ref[..., FEAT:] = stat.reshape(*shape, STAT).astype(out_ref.dtype)


def pair_kernel(mine_ref, pair_ref, out_ref):
    other = 1 - lax.axis_index("sx") % 2
    data = [mine_ref[:, :FEAT], pair_ref[other, :, :FEAT]]
    lse = [[x[:, g : g + 1] for g in range(QUERY_PER_KEY)] for x in (mine_ref[:, FEAT:], pair_ref[other, :, FEAT:])]
    combine_two(data, lse, out_ref)


def last_kernel(a_ref, out_ref):
    stat = a_ref[:, :, FEAT:].astype(jnp.float32)
    lse = stat + (pltpu.roll(stat, STAT - 1, 2) + pltpu.roll(stat, STAT - 2, 2))
    weight = jnp.exp2(lse - jnp.max(lse, axis=0, keepdims=True))
    weight = weight / jnp.sum(weight, axis=0, keepdims=True)
    for g in range(QUERY_PER_KEY):
        lanes = slice(g * HEAD_WIDTH, (g + 1) * HEAD_WIDTH)
        mixed = jnp.sum(a_ref[:, :, lanes].astype(jnp.float32) * weight[:, :, 3 * g : 3 * g + 1], axis=0)
        for h in range(KEY_HEADS):
            head = h * FEAT + g * HEAD_WIDTH
            out_ref[:, head : head + HEAD_WIDTH] = mixed[h : h + 1].astype(jnp.bfloat16)


def call(kernel, out, name, *args):
    return pl.pallas_call(
        kernel,
        out_shape=out,
        in_specs=[pl.BlockSpec(memory_space=pltpu.VMEM)] * len(args),
        out_specs=jax.tree.map(lambda _: pl.BlockSpec(memory_space=pltpu.VMEM), out),
        compiler_params=pltpu.CompilerParams(vmem_limit_bytes=40 * 1024 * 1024),
        name=name,
    )(*args)


def per_device(queries, keys, values, block_ids):
    count_x = lax.axis_size("sx")
    count_y = lax.axis_size("sy")
    count_z = count_x // 2
    tokens = keys.shape[0]
    cores = [[2 * z, 2 * z + 1] for z in range(count_z)]
    along_z = [[2 * z + c for z in range(count_z)] for c in range(2)]

    def exchange(x, axis, groups=None):
        return lax.all_to_all(x, axis, split_axis=0, concat_axis=0, tiled=True, axis_index_groups=groups)

    def swap(x, i):
        pairs = [(a * count_y + b, a * count_y + (b ^ PARTNERS[a % 2][i])) for a in range(count_x) for b in range(count_y)]
        return lax.ppermute(x, ("sx", "sy"), pairs)

    def half(*shape):
        return jax.ShapeDtypeStruct(shape, jnp.bfloat16)

    def full(*shape):
        return jax.ShapeDtypeStruct(shape, jnp.float32)

    own = call(copies_kernel, half(count_z, KEY_HEADS, FEAT), "copies", queries)
    rows = exchange(own, "sx", along_z)

    hbm = pl.BlockSpec(memory_space=pltpu.HBM)
    width = SHARE * HEAD_WIDTH
    count = len(PARTNERS[0])
    kv = pl.pallas_call(
        relay_kernel,
        out_shape=[half(2 * tokens, width)] * count,
        in_specs=[hbm, hbm],
        out_specs=[hbm] * count,
        scratch_shapes=[
            pltpu.VMEM((count, 2 * tokens, width), jnp.bfloat16),
            pltpu.SemaphoreType.DMA((count, 2)),
            pltpu.SemaphoreType.DMA((count, 2)),
        ],
        compiler_params=pltpu.CompilerParams(vmem_limit_bytes=60 * 1024 * 1024),
        name="relay",
    )(keys, values)
    kv = [swap(x, i) for i, x in enumerate(kv)]

    pos = call(find_kernel, full(8, count_x * KEY_HEADS), "find", block_ids.T)
    rows = lax.all_gather(rows, "sx", axis=0, axis_index_groups=cores)
    rows = rows.reshape(count_x, KEY_HEADS, FEAT)
    asked = call(select_kernel, half(count_y, SLOTS, SHARE * FEAT), "select", pos, rows)
    asked = exchange(asked, "sy")
    part = call(attend_kernel, half(count_y, SLOTS, SHARE * FEAT + STAT), "attend", asked, keys, values, *kv)
    part = exchange(part, "sy")
    side = full(count_z * KEY_HEADS, FEAT + STAT)
    mine, theirs = call(merge_kernel, [side, side], "merge", pos, part)
    pair = lax.all_gather(theirs, "sx", axis=0, axis_index_groups=cores)
    part = call(pair_kernel, half(count_z, KEY_HEADS, FEAT + STAT), "pair", mine, pair)
    part = exchange(part, "sx", along_z)
    return call(last_kernel, half(1, KEY_HEADS * FEAT), "last", part)


def solution(mesh):
    return jax.shard_map(
        per_device,
        mesh=mesh,
        in_specs=(P(("sx", "sy"), None), P(("sx", "sy"), None), P(("sx", "sy"), None), P()),
        out_specs=P(("sx", "sy"), None),
        check_vma=False,
    )
```

time: 97.7 us -> 104 us (1.064)
  blocking collectives: 59 us -> 42.6 us
  starting transfers between devices: 18.6 us -> 31.6 us
  waiting for transfers between devices: 8.29 us -> 16.5 us
  Pallas kernels: 9.76 us -> 11.6 us
    all_to_all x4 -> x2, blocking collectives: 57 us -> 38.4 us  [exchange(): lax.all_to_all(x, axis, split_axis=0, concat_axis=0, tiled=True, axis_ind...]
    ppermute x1 -> x3, waiting for transfers between devices: 0.01 us -> 11.7 us  [swap(): return lax.ppermute(x, ('sx', 'sy'), pairs)]
    all_to_all x1 -> x2, starting transfers between devices: 15.2 us -> 22.2 us  [exchange(): lax.all_to_all(x, axis, split_axis=0, concat_axis=0, tiled=True, axis_ind...]
    ppermute x1 -> x3, starting transfers between devices: 3.4 us -> 9.34 us  [swap(): return lax.ppermute(x, ('sx', 'sy'), pairs)]
    all_to_all x1 -> x2, waiting for transfers between devices: 8.29 us -> 4.89 us  [exchange(): lax.all_to_all(x, axis, split_axis=0, concat_axis=0, tiled=True, axis_ind...]
    all_gather x0 -> x1, blocking collectives: none -> 2.28 us  [per_device(): pair = lax.all_gather(theirs, 'sx', axis=0, axis_index_groups=cores)]
    pallas_call x7 -> x8, Pallas kernels: 9.76 us -> 11.6 us  [the longest x7 9.31 us: call(): pl.pallas_call(kernel, out_shape=out, in_specs=[pl.BlockSpec(memory_space...]
  transfers between devices with their start and end apart: 2 -> 5, of which waited for: 1 -> 3; matrix products, arithmetic and copies ran while one was open for 0% -> 0% of each run, Pallas kernels for 3% -> 4%
where the time goes in v10:
time: 104 us; the launch traced here: 103 us
  blocking collectives  42.6 us (41%)
  starting transfers between devices  31.6 us (30%)
  waiting for transfers between devices  16.5 us (16%)
  Pallas kernels  11.6 us (11%)
    all_to_all x2, blocking collectives, exchange(): lax.all_to_all(x, axis, split_axis=0, concat_axis=0, tiled=True, axis_ind...  38.4 us
    all_to_all x2, starting transfers between devices, exchange(): lax.all_to_all(x, axis, split_axis=0, concat_axis=0, tiled=True, axis_ind...  22.2 us
    ppermute x3, waiting for transfers between devices, swap(): return lax.ppermute(x, ('sx', 'sy'), pairs)  11.7 us
    ppermute x3, starting transfers between devices, swap(): return lax.ppermute(x, ('sx', 'sy'), pairs)  9.34 us
    pallas_call x7, Pallas kernels, call(): pl.pallas_call(kernel, out_shape=out, in_specs=[pl.BlockSpec(memory_space...  9.31 us
    all_to_all x2, waiting for transfers between devices, exchange(): lax.all_to_all(x, axis, split_axis=0, concat_axis=0, tiled=True, axis_ind...  4.89 us
    pallas_call x1, Pallas kernels, per_device(): pl.pallas_call(relay_kernel, out_shape=[half(2 * tokens, width)] * count,...  2.34 us
    all_gather x1, blocking collectives, per_device(): pair = lax.all_gather(theirs, 'sx', axis=0, axis_index_groups=cores)  2.28 us
  transfers between devices with their start and end apart: 5, of which 3 were waited for; matrix products, arithmetic and copies ran while one was open for 0% of the time, Pallas kernels for 4%

profile of v10, /device:TPU:32, one launch (start us, length us, event | category | flops | bytes accessed | tf_op | source)
XLA Modules:
  0.0 103.2 jit_solution(15260093303345625725)
XLA Ops:
  0.0 0.0 copy-start.3
  0.0 0.7 copy-done.3
  0.7 0.7 copies.1
  1.4 15.2 %all-to-all-start = ((bf16[16,8,512]{2,1,0:T(8,128)(2,1)}), bf16[16,8,512]{2,1,0:T(8,128)(2,1)S(1)}, u32[]{:S(2)}, u32[]{:S(2)}) async-start(bf16[16,8,512]{2,1,0:T(8,128)(2,1)} %copies.1), calls=%async_computation | async-start | bytes 262144 | tf_op jit(solution)/shard_map/all_to_all | solution.py:274
  16.6 0.0 copy-start.2
  16.6 0.0 copy-start.1
  16.6 2.3 %relay.1 = (bf16[1024,256]{1,0:T(8,128)(2,1)}, bf16[1024,256]{1,0:T(8,128)(2,1)}, bf16[1024,256]{1,0:T(8,128)(2,1)}) custom-call(bf16[512,1024]{1,0:T(8,128)(2,1)} %k_ref.3, bf16[512,1024]{1,0:T(8,128)(2,1)} %v_ref.3), custom_call_target="tpu_custom_call" | custom-call | tf_op jit(solution)/shard_map/relay/pallas_call | solution.py:292
  19.0 0.0 copy-start
  19.0 3.5 %collective-permute-start = (bf16[1024,256]{1,0:T(8,128)(2,1)}, bf16[1024,256]{1,0:T(8,128)(2,1)S(1)}, u32[]{:S(2)}, u32[]{:S(2)}) collective-permute-start(bf16[1024,256]{1,0:T(8,128)(2,1)} %get-tuple-element.10), channel_id=1, source_target_pairs={{0,1},{1,0},{2,3},{3,2},{4,5},{5,4},{6,7},{7,6},{8,9},{9,8},{10,11... | collective-permute-start | bytes 1572872 | tf_op jit(solution)/shard_map/ppermute | solution.py:278
  22.5 3.5 %collective-permute-start.1 = (bf16[1024,256]{1,0:T(8,128)(2,1)}, bf16[1024,256]{1,0:T(8,128)(2,1)S(1)}, u32[]{:S(2)}, u32[]{:S(2)}) collective-permute-start(bf16[1024,256]{1,0:T(8,128)(2,1)} %get-tuple-element.11), channel_id=1, source_target_pairs={{0,4},{1,5},{2,6},{3,7},{4,0},{5,1},{6,2},{7,3},{8,12},{9,13},{10,... | collective-permute-start | bytes 1572872 | tf_op jit(solution)/shard_map/ppermute | solution.py:278
  26.0 2.3 %collective-permute-start.2 = (bf16[1024,256]{1,0:T(8,128)(2,1)}, bf16[1024,256]{1,0:T(8,128)(2,1)}, u32[]{:S(2)}, u32[]{:S(2)}) collective-permute-start(bf16[1024,256]{1,0:T(8,128)(2,1)} %get-tuple-element.12), channel_id=1, source_target_pairs={{0,5},{1,4},{2,7},{3,6},{4,1},{5,0},{6,3},{7,2},{8,13},{9,12},{10,... | collective-permute-start | bytes 1572872 | tf_op jit(solution)/shard_map/ppermute | solution.py:278
  28.3 0.0 copy-done.2
  28.3 0.4 find.1.pos_ref
  28.7 2.1 %all-to-all-done = bf16[16,8,512]{2,1,0:T(8,128)(2,1)S(1)} async-done(((bf16[16,8,512]{2,1,0:T(8,128)(2,1)}), bf16[16,8,512]{2,1,0:T(8,128)(2,1)S(1)}, u32[]{:S(2)}, u32[]{:S(2)}) %all-to-all-start) | async-done | bytes 131104 | tf_op jit(solution)/shard_map/all_to_all | solution.py:274
  30.8 2.0 %all-gather.q_ref = bf16[32,8,512]{2,1,0:T(8,128)(2,1)S(1)} all-gather(bf16[16,8,512]{2,1,0:T(8,128)(2,1)S(1)} %all-to-all-done), channel_id=2, replica_groups={{0,16},{32,48},{64,80},{96,112},{128,144},{160,176},{192,208},{224,240}..., dimensions={0}, use_global_device_ids=true | all-gather | bytes 393216 | tf_op jit(solution)/shard_map/all_gather | solution.py:308
  32.8 0.9 select.1
  33.7 7.0 %all-to-all-start.1 = ((bf16[16,8,1024]{2,1,0:T(8,128)(2,1)}), bf16[16,8,1024]{2,1,0:T(8,128)(2,1)S(1)}, u32[]{:S(2)}, u32[]{:S(2)}) async-start(bf16[16,8,1024]{2,1,0:T(8,128)(2,1)} %select.1), calls=%async_computation.1 | async-start | bytes 524288 | tf_op jit(solution)/shard_map/all_to_all | solution.py:274
  40.7 0.0 collective-permute-done.refs_0_
  40.7 11.7 %collective-permute-done.1.refs_1_ = bf16[1024,256]{1,0:T(8,128)(2,1)S(1)} collective-permute-done((bf16[1024,256]{1,0:T(8,128)(2,1)}, bf16[1024,256]{1,0:T(8,128)(2,1)S(1)}, u32[]{:S(2)}, u32[]{:S(2)}) %collective-permute-start.1) | collective-permute-done | bytes 524320 | tf_op jit(solution)/shard_map/ppermute | solution.py:278
  52.4 0.0 collective-permute-done.2.refs_2_
  52.4 2.8 %all-to-all-done.1.x_ref = bf16[16,8,1024]{2,1,0:T(8,128)(2,1)S(1)} async-done(((bf16[16,8,1024]{2,1,0:T(8,128)(2,1)}), bf16[16,8,1024]{2,1,0:T(8,128)(2,1)S(1)}, u32[]{:S(2)}, u32[]{:S(2)}) %all-to-all-start.1) | async-done | bytes 262176 | tf_op jit(solution)/shard_map/all_to_all | solution.py:274
  55.2 0.0 copy-done.1
  55.2 0.0 copy-done
  55.2 4.2 %attend.1 = bf16[16,8,1152]{2,1,0:T(8,128)(2,1)S(1)} custom-call(bf16[16,8,1024]{2,1,0:T(8,128)(2,1)S(1)} %all-to-all-done.1.x_ref, bf16[512,1024]{1,0:T(8,128)(2,1)S(1)} %copy-done, bf16[512,1024]{1,0:T(8,128)(2,1)S(1)} %copy-done.1, bf16[1024,256]{1,0:T(8,128)(2,1)S(1)} %collective-permute-done.refs_0_, ...), custom_call_target="tpu_custom_call" | custom-call | tf_op jit(solution)/shard_map/attend/pallas_call | solution.py:255
  59.5 11.5 %all_to_all.20.y_ref = bf16[16,8,1152]{2,1,0:T(8,128)(2,1)S(1)} all-to-all(bf16[16,8,1152]{2,1,0:T(8,128)(2,1)S(1)} %attend.1), channel_id=1, replica_groups=mesh['sx'=32,'sy'=16] {'sy'}, dimensions={0} | all-to-all | bytes 589824 | tf_op jit(solution)/shard_map/all_to_all | solution.py:274
  70.9 1.9 %merge.1 = (f32[128,640]{1,0:T(8,128)S(1)}, f32[128,640]{1,0:T(8,128)S(1)}) custom-call(f32[8,256]{1,0:T(8,128)S(1)} %find.1.pos_ref, bf16[16,8,1152]{2,1,0:T(8,128)(2,1)S(1)} %all_to_all.20.y_ref), custom_call_target="tpu_custom_call" | custom-call | tf_op jit(solution)/shard_map/merge/pallas_call | solution.py:255
  72.8 2.3 %all-gather.1 = f32[256,640]{1,0:T(8,128)S(1)} all-gather(f32[128,640]{1,0:T(8,128)S(1)} %get-tuple-element.14), channel_id=3, replica_groups={{0,16},{32,48},{64,80},{96,112},{128,144},{160,176},{192,208},{224,240}..., dimensions={0}, use_global_device_ids=true | all-gather | bytes 983040 | tf_op jit(solution)/shard_map/all_gather | solution.py:316
  75.1 0.3 pair.1
  75.5 26.9 %all_to_all.21.a_ref = bf16[16,8,640]{2,1,0:T(8,128)(2,1)S(1)} all-to-all(bf16[16,8,640]{2,1,0:T(8,128)(2,1)S(1)} %pair.1), channel_id=1, replica_groups={{0,32,64,96,128,160,192,224,256,288,320,352,384,416,448,480},{16,48,80,..., dimensions={0} | all-to-all | bytes 327680 | tf_op jit(solution)/shard_map/all_to_all | solution.py:274
  102.4 0.9 last.1
Async XLA Ops:
  0.0 0.7 copy-start.3
  1.4 29.4 %all-to-all-start = ((bf16[16,8,512]{2,1,0:T(8,128)(2,1)}), bf16[16,8,512]{2,1,0:T(8,128)(2,1)S(1)}, u32[]{:S(2)}, u32[]{:S(2)}) async-start(bf16[16,8,512]{2,1,0:T(8,128)(2,1)} %copies.1), calls=%async_computation | async-start | bytes 262144 | tf_op jit(solution)/shard_map/all_to_all | solution.py:274
  16.6 11.8 %copy-start.2 = (s32[512,16]{0,1:T(8,128)S(1)}, s32[512,16]{0,1:T(8,128)}, u32[]{:S(2)}) copy-start(s32[512,16]{0,1:T(8,128)} %param.7) | copy-start | bytes 98308
  16.6 38.6 %copy-start.1 = (bf16[512,1024]{1,0:T(8,128)(2,1)S(1)}, bf16[512,1024]{1,0:T(8,128)(2,1)}, u32[]{:S(2)}) copy-start(bf16[512,1024]{1,0:T(8,128)(2,1)} %v_ref.3) | copy-start | bytes 3145732
  19.0 36.2 %copy-start = (bf16[512,1024]{1,0:T(8,128)(2,1)S(1)}, bf16[512,1024]{1,0:T(8,128)(2,1)}, u32[]{:S(2)}) copy-start(bf16[512,1024]{1,0:T(8,128)(2,1)} %k_ref.3) | copy-start | bytes 3145732
  19.0 21.8 %collective-permute-start = (bf16[1024,256]{1,0:T(8,128)(2,1)}, bf16[1024,256]{1,0:T(8,128)(2,1)S(1)}, u32[]{:S(2)}, u32[]{:S(2)}) collective-permute-start(bf16[1024,256]{1,0:T(8,128)(2,1)} %get-tuple-element.10), channel_id=1, source_target_pairs={{0,1},{1,0},{2,3},{3,2},{4,5},{5,4},{6,7},{7,6},{8,9},{9,8},{10,11... | collective-permute-start | bytes 1572872 | tf_op jit(solution)/shard_map/ppermute | solution.py:278
  22.5 29.9 %collective-permute-start.1 = (bf16[1024,256]{1,0:T(8,128)(2,1)}, bf16[1024,256]{1,0:T(8,128)(2,1)S(1)}, u32[]{:S(2)}, u32[]{:S(2)}) collective-permute-start(bf16[1024,256]{1,0:T(8,128)(2,1)} %get-tuple-element.11), channel_id=1, source_target_pairs={{0,4},{1,5},{2,6},{3,7},{4,0},{5,1},{6,2},{7,3},{8,12},{9,13},{10,... | collective-permute-start | bytes 1572872 | tf_op jit(solution)/shard_map/ppermute | solution.py:278
  26.0 26.4 %collective-permute-start.2 = (bf16[1024,256]{1,0:T(8,128)(2,1)}, bf16[1024,256]{1,0:T(8,128)(2,1)}, u32[]{:S(2)}, u32[]{:S(2)}) collective-permute-start(bf16[1024,256]{1,0:T(8,128)(2,1)} %get-tuple-element.12), channel_id=1, source_target_pairs={{0,5},{1,4},{2,7},{3,6},{4,1},{5,0},{6,3},{7,2},{8,13},{9,12},{10,... | collective-permute-start | bytes 1572872 | tf_op jit(solution)/shard_map/ppermute | solution.py:278
  33.7 21.5 %all-to-all-start.1 = ((bf16[16,8,1024]{2,1,0:T(8,128)(2,1)}), bf16[16,8,1024]{2,1,0:T(8,128)(2,1)S(1)}, u32[]{:S(2)}, u32[]{:S(2)}) async-start(bf16[16,8,1024]{2,1,0:T(8,128)(2,1)} %select.1), calls=%async_computation.1 | async-start | bytes 524288 | tf_op jit(solution)/shard_map/all_to_all | solution.py:274

commit v11 on v9

--- a/solution.py
+++ b/solution.py
@@ -24,6 +24,14 @@
 ONE_LANE = 12
 
 
+ASK_FIRST = 11
+ANSWER_FIRST = 8
+
+
+def z_order(count, first):
+    return [(i + first) % count for i in range(count)]
+
+
 def half_of(core, s):
     return jnp.where(core == 0, s % 2, s // 4)
 
@@ -44,14 +52,14 @@
     return stat
 
 
-def find_kernel(ids_ref, pos_ref):
+def find_kernel(ids_ref, ask_ref, answer_ref):
     count_x, count_y = lax.axis_size("sx"), lax.axis_size("sy")
     index_x, index_y = lax.axis_index("sx"), lax.axis_index("sy")
+    count_z = count_x // 2
     lanes = 128
     r = lax.broadcasted_iota(jnp.int32, (count_x * count_y, lanes), 0)
     c = lax.broadcasted_iota(jnp.int32, (count_x * count_y, lanes), 1)
-    row = (c % (count_x // 2)) * 2 + c // (count_x // 2)
-    own = jnp.where((r == row * count_y + index_y) & (c < count_x), 1.0, 0.0).astype(jnp.bfloat16)
+    own = jnp.where((r == c * count_y + index_y) & (c < count_x), 1.0, 0.0).astype(jnp.bfloat16)
     ids = ids_ref[...].astype(jnp.float32).astype(jnp.bfloat16)
     column = jnp.dot(ids, own, preferred_element_type=jnp.float32)
     b = lax.broadcasted_iota(jnp.int32, (8, lanes), 0)
@@ -66,19 +74,28 @@
     before = jnp.where(r < c, 1.0, 0.0).astype(jnp.bfloat16)
     rank = jnp.dot(named.astype(jnp.bfloat16), before, preferred_element_type=jnp.float32)
     pos = jnp.where(named > 0.5, rank, -1.0).astype(jnp.bfloat16)
-    shape = (lanes, pos_ref.shape[1])
-    r = lax.broadcasted_iota(jnp.int32, shape, 0)
-    c = lax.broadcasted_iota(jnp.int32, shape, 1)
-    heads = jnp.where(r == c // KEY_HEADS, 1.0, 0.0).astype(jnp.bfloat16)
-    pos_ref[...] = jnp.dot(pos, heads, preferred_element_type=jnp.float32)
-
-
-def slot_onehot(pos, dtype):
+    for out_ref, first in ((ask_ref, ASK_FIRST), (answer_ref, ANSWER_FIRST)):
+        shape = (lanes, out_ref.shape[1])
+        r = lax.broadcasted_iota(jnp.int32, shape, 0)
+        c = lax.broadcasted_iota(jnp.int32, shape, 1) // KEY_HEADS
+        row = ((c + first) % count_z) * 2 + c // count_z
+        spread = jnp.where(r == row, 1.0, 0.0).astype(jnp.bfloat16)
+        out_ref[...] = jnp.dot(pos, spread, preferred_element_type=jnp.float32)
+
+
+def slot_onehot(pos):
     shape = (KEY_HEADS * SLOTS, pos.shape[1])
     r = lax.broadcasted_iota(jnp.int32, shape, 0)
     c = lax.broadcasted_iota(jnp.int32, shape, 1)
     hit = (pos == (r % SLOTS).astype(jnp.float32)) & (r // SLOTS == c % KEY_HEADS)
-    return jnp.where(hit, 1.0, 0.0).astype(dtype)
+    return jnp.where(hit, 1.0, 0.0).astype(jnp.bfloat16)
+
+
+def copies_kernel(q_ref, out_ref):
+    q = q_ref[...].astype(jnp.float32)
+    q = jnp.concatenate([q[:, h * FEAT : (h + 1) * FEAT] for h in range(KEY_HEADS)], axis=0).astype(jnp.bfloat16)
+    for z in range(out_ref.shape[0]):
+        out_ref[z] = q
 
 
 def relay_kernel(k_ref, v_ref, out_ref, here, in_sems, out_sems):
@@ -108,7 +125,7 @@
     core = lax.axis_index("sx") % 2
     q = q_ref[...].astype(jnp.float32).reshape(-1, FEAT).astype(jnp.bfloat16)
     for p in range(2):
-        hot = slot_onehot(pos_ref[p : p + 1, :], jnp.bfloat16)
+        hot = slot_onehot(pos_ref[p : p + 1, :])
         picked = jnp.dot(hot, q, preferred_element_type=jnp.float32)
         for h in range(KEY_HEADS):
             lanes = slice((h % HALF) * FEAT, (h % HALF + 1) * FEAT)
@@ -153,9 +170,10 @@
     y_ref[:, :, HALF * FEAT :] = stat
 
 
-def merge_kernel(pos_ref, y_ref, out_ref):
+def merge_kernel(pos_ref, y_ref, mine_ref, theirs_ref):
     core = lax.axis_index("sx") % 2
     flip = (((0,), (0,)), ((), ()))
+    lane = lax.broadcasted_iota(jnp.int32, (SLOTS, STAT), 1)
     data, lse = [], []
     for p in range(2):
         tall = []
@@ -172,31 +190,31 @@
             weights = [w * inverse for w in weights]
             block = top + jnp.log2(total)
             for h in range(HALF):
-                pair = []
+                heads = []
                 for g in range(QUERY_PER_KEY):
                     n = h * QUERY_PER_KEY + g
                     lanes = slice(n * HEAD_WIDTH, (n + 1) * HEAD_WIDTH)
                     terms = [w[:, 3 * n : 3 * n + 1] * y_ref[s, :, lanes].astype(jnp.float32) for w, s in zip(weights, froms)]
-                    pair.append(functools.reduce(jnp.add, terms))
+                    heads.append(functools.reduce(jnp.add, terms))
                 shift = 3 * h * QUERY_PER_KEY
                 stat = block if shift == 0 else pltpu.roll(block, STAT - shift, 1)
-                lane = lax.broadcasted_iota(jnp.int32, stat.shape, 1)
                 stat = jnp.where(lane == ONE_LANE, 1.0, jnp.where(lane < ONE_LANE, stat, 0.0))
-                tall.append(jnp.concatenate(pair + [stat], axis=1))
-        hot = slot_onehot(pos_ref[p : p + 1, :], jnp.float32)
-        dense = lax.dot_general(
-            hot,
-            jnp.concatenate(tall, axis=0),
-            flip,
-            precision=lax.Precision.HIGHEST,
-            preferred_element_type=jnp.float32,
-        )
+                tall.append(jnp.concatenate(heads + [stat], axis=1))
+        tall = jnp.concatenate([x.astype(jnp.bfloat16) for x in pieces(jnp.concatenate(tall, axis=0))], axis=0)
+        hot = jnp.concatenate([slot_onehot(pos_ref[p : p + 1, :])] * 3, axis=0)
+        dense = lax.dot_general(hot, tall, flip, preferred_element_type=jnp.float32)
         named = dense[:, FEAT + ONE_LANE : FEAT + ONE_LANE + 1] > 0.5
         data.append(dense)
         lse.append(
             [jnp.where(named, dense[:, FEAT + 3 * g : FEAT + 3 * g + 1], NEVER) for g in range(QUERY_PER_KEY)]
         )
-    combine_two(data, lse, out_ref)
+    rows = mine_ref.shape[0]
+    for out_ref, is_first in ((mine_ref, core == 0), (theirs_ref, core == 1)):
+
+        def side(x):
+            return jnp.where(is_first, x[:rows], x[rows:])
+
+        combine_two([side(x) for x in data], [[side(x) for x in y] for y in lse], out_ref)
 
 
 def combine_two(data, lse, out_ref):
@@ -222,32 +240,32 @@
     out_ref[..., FEAT:] = stat.reshape(*shape, STAT).astype(out_ref.dtype)
 
 
-def pair_kernel(a_ref, out_ref):
-    data = [a_ref[c, :, :FEAT] for c in range(2)]
-    lse = [[a_ref[c, :, FEAT + g : FEAT + g + 1] for g in range(QUERY_PER_KEY)] for c in range(2)]
+def pair_kernel(mine_ref, pair_ref, out_ref):
+    other = 1 - lax.axis_index("sx") % 2
+    data = [mine_ref[:, :FEAT], pair_ref[other, :, :FEAT]]
+    lse = [[x[:, g : g + 1] for g in range(QUERY_PER_KEY)] for x in (mine_ref[:, FEAT:], pair_ref[other, :, FEAT:])]
     combine_two(data, lse, out_ref)
 
 
 def last_kernel(a_ref, out_ref):
+    stat = a_ref[:, :, FEAT:].astype(jnp.float32)
+    lse = stat + (pltpu.roll(stat, STAT - 1, 2) + pltpu.roll(stat, STAT - 2, 2))
+    weight = jnp.exp2(lse - jnp.max(lse, axis=0, keepdims=True))
+    weight = weight / jnp.sum(weight, axis=0, keepdims=True)
     for g in range(QUERY_PER_KEY):
-        at = FEAT + 3 * g
-        lse = [a_ref[:, :, at + k : at + k + 1].astype(jnp.float32) for k in range(3)]
-        lse = lse[0] + (lse[1] + lse[2])
-        weight = jnp.exp2(lse - jnp.max(lse, axis=0, keepdims=True))
-        total = jnp.sum(weight, axis=0)
         lanes = slice(g * HEAD_WIDTH, (g + 1) * HEAD_WIDTH)
-        mixed = jnp.sum(a_ref[:, :, lanes].astype(jnp.float32) * weight, axis=0) / total
+        mixed = jnp.sum(a_ref[:, :, lanes].astype(jnp.float32) * weight[:, :, 3 * g : 3 * g + 1], axis=0)
         for h in range(KEY_HEADS):
             head = h * FEAT + g * HEAD_WIDTH
             out_ref[:, head : head + HEAD_WIDTH] = mixed[h : h + 1].astype(jnp.bfloat16)
 
 
-def call(kernel, shape, dtype, name, *args, scratch=()):
+def call(kernel, out, name, *args, scratch=()):
     return pl.pallas_call(
         kernel,
-        out_shape=jax.ShapeDtypeStruct(shape, dtype),
+        out_shape=out,
         in_specs=[pl.BlockSpec(memory_space=pltpu.VMEM)] * len(args),
-        out_specs=pl.BlockSpec(memory_space=pltpu.VMEM),
+        out_specs=jax.tree.map(lambda _: pl.BlockSpec(memory_space=pltpu.VMEM), out),
         scratch_shapes=list(scratch),
         compiler_params=pltpu.CompilerParams(vmem_limit_bytes=40 * 1024 * 1024),
         name=name,
@@ -260,7 +278,9 @@
     count_z = count_x // 2
     tokens = keys.shape[0]
     cores = [[2 * z, 2 * z + 1] for z in range(count_z)]
-    along_z = [[2 * z + c for z in range(count_z)] for c in range(2)]
+    ask_groups, answer_groups = (
+        [[2 * z + c for z in z_order(count_z, first)] for c in range(2)] for first in (ASK_FIRST, ANSWER_FIRST)
+    )
     partners = [
         (x * count_y + y, x * count_y + (y ^ PARTNER[x % 2])) for x in range(count_x) for y in range(count_y)
     ]
@@ -268,18 +288,24 @@
     def exchange(x, axis, groups=None):
         return lax.all_to_all(x, axis, split_axis=0, concat_axis=0, tiled=True, axis_index_groups=groups)
 
-    own = jnp.broadcast_to(queries.reshape(1, KEY_HEADS, FEAT), (count_z, KEY_HEADS, FEAT))
-    rows = exchange(own, "sx", along_z)
+    def half(*shape):
+        return jax.ShapeDtypeStruct(shape, jnp.bfloat16)
+
+    def full(*shape):
+        return jax.ShapeDtypeStruct(shape, jnp.float32)
+
+    own = call(copies_kernel, half(count_z, KEY_HEADS, FEAT), "copies", queries)
+    rows = exchange(own, "sx", ask_groups)
 
     hbm = pl.BlockSpec(memory_space=pltpu.HBM)
     width = HALF * HEAD_WIDTH
     kv = pl.pallas_call(
         relay_kernel,
-        out_shape=jax.ShapeDtypeStruct((2 * tokens, width), keys.dtype),
+        out_shape=half(2 * tokens, width),
         in_specs=[hbm, hbm],
         out_specs=hbm,
         scratch_shapes=[
-            pltpu.VMEM((2 * tokens, width), keys.dtype),
+            pltpu.VMEM((2 * tokens, width), jnp.bfloat16),
             pltpu.SemaphoreType.DMA((2, 4)),
             pltpu.SemaphoreType.DMA((2, 4)),
         ],
@@ -288,26 +314,27 @@
     )(keys, values)
     kv = lax.ppermute(kv, ("sx", "sy"), partners)
 
-    pos = call(find_kernel, (8, count_x * KEY_HEADS), jnp.float32, "find", block_ids.T)
+    pos = full(8, count_x * KEY_HEADS)
+    ask_pos, answer_pos = call(find_kernel, [pos, pos], "find", block_ids.T)
     rows = lax.all_gather(rows, "sx", axis=0, axis_index_groups=cores)
     rows = rows.reshape(count_x, KEY_HEADS, FEAT)
     asked = call(
         select_kernel,
-        (count_y, SLOTS, HALF * FEAT),
-        jnp.bfloat16,
+        half(count_y, SLOTS, HALF * FEAT),
         "select",
-        pos,
+        ask_pos,
         rows,
         scratch=[pltpu.VMEM((2, 2, SLOTS, HALF * FEAT), jnp.bfloat16)],
     )
     asked = exchange(asked, "sy")
-    part = call(attend_kernel, (count_y, SLOTS, HALF * FEAT + STAT), jnp.bfloat16, "attend", asked, keys, values, kv)
+    part = call(attend_kernel, half(count_y, SLOTS, HALF * FEAT + STAT), "attend", asked, keys, values, kv)
     part = exchange(part, "sy")
-    part = call(merge_kernel, (2, count_z * KEY_HEADS, FEAT + STAT), jnp.float32, "merge", pos, part)
-    part = exchange(part, "sx", cores)
-    part = call(pair_kernel, (count_z, KEY_HEADS, FEAT + STAT), jnp.bfloat16, "pair", part)
-    part = exchange(part, "sx", along_z)
-    return call(last_kernel, (1, KEY_HEADS * FEAT), jnp.bfloat16, "last", part)
+    side = full(count_z * KEY_HEADS, FEAT + STAT)
+    mine, theirs = call(merge_kernel, [side, side], "merge", answer_pos, part)
+    pair = lax.all_gather(theirs, "sx", axis=0, axis_index_groups=cores)
+    part = call(pair_kernel, half(count_z, KEY_HEADS, FEAT + STAT), "pair", mine, pair)
+    part = exchange(part, "sx", answer_groups)
+    return call(last_kernel, half(1, KEY_HEADS * FEAT), "last", part)
 
 
 def solution(mesh):

time: 97.7 us -> 92.1 us (0.943)
  the two profiles are of different devices: /device:TPU:32 before, /device:TPU:1 now
where the time goes in v11:
time: 92.1 us; the launch traced here: 91.7 us
  blocking collectives  58.3 us (63%)
  starting transfers between devices  19.6 us (21%)
  Pallas kernels  10.2 us (11%)
  waiting for transfers between devices  2.81 us (3%)
    all_to_all x3, blocking collectives, exchange(): lax.all_to_all(x, axis, split_axis=0, concat_axis=0, tiled=True, axis_ind...  50.9 us
    all_to_all x1, starting transfers between devices, exchange(): lax.all_to_all(x, axis, split_axis=0, concat_axis=0, tiled=True, axis_ind...  16.4 us
    pallas_call x7, Pallas kernels, call(): pl.pallas_call(kernel, out_shape=out, in_specs=[pl.BlockSpec(memory_space...  8.09 us
    all_gather x1, blocking collectives, per_device(): pair = lax.all_gather(theirs, 'sx', axis=0, axis_index_groups=cores)  3.93 us
    all_gather x1, blocking collectives, per_device(): rows = lax.all_gather(rows, 'sx', axis=0, axis_index_groups=cores)  3.41 us
    ppermute x1, starting transfers between devices, per_device(): kv = lax.ppermute(kv, ('sx', 'sy'), partners)  3.2 us
    all_to_all x1, waiting for transfers between devices, exchange(): lax.all_to_all(x, axis, split_axis=0, concat_axis=0, tiled=True, axis_ind...  2.81 us
    pallas_call x1, Pallas kernels, per_device(): pl.pallas_call(relay_kernel, out_shape=half(2 * tokens, width), in_specs=...  2.13 us
  transfers between devices with their start and end apart: 2, of which 1 were waited for; matrix products, arithmetic and copies ran while one was open for 0% of the time, Pallas kernels for 3%

profile of v11, /device:TPU:1, one launch (start us, length us, event | category | flops | bytes accessed | tf_op | source)
XLA Modules:
  0.0 91.7 jit_solution(675388286870892957)
XLA Ops:
  0.0 0.0 copy-start.3
  0.0 0.7 copy-done.3
  0.7 0.7 copies.1
  1.4 16.4 %all-to-all-start = ((bf16[16,8,512]{2,1,0:T(8,128)(2,1)}), bf16[16,8,512]{2,1,0:T(8,128)(2,1)S(1)}, u32[]{:S(2)}, u32[]{:S(2)}) async-start(bf16[16,8,512]{2,1,0:T(8,128)(2,1)} %copies.1), calls=%async_computation | async-start | bytes 262144 | tf_op jit(solution)/shard_map/all_to_all | solution.py:289
  17.8 0.0 copy-start.2
  17.8 2.1 %relay.1 = bf16[1024,512]{1,0:T(8,128)(2,1)} custom-call(bf16[512,1024]{1,0:T(8,128)(2,1)} %k_ref.3, bf16[512,1024]{1,0:T(8,128)(2,1)} %v_ref.3), custom_call_target="tpu_custom_call" | custom-call | tf_op jit(solution)/shard_map/relay/pallas_call | solution.py:302
  20.0 3.2 %collective-permute-start = (bf16[1024,512]{1,0:T(8,128)(2,1)}, bf16[1024,512]{1,0:T(8,128)(2,1)S(1)}, u32[]{:S(2)}, u32[]{:S(2)}) collective-permute-start(bf16[1024,512]{1,0:T(8,128)(2,1)} %relay.1), channel_id=1, source_target_pairs={{0,1},{1,0},{2,3},{3,2},{4,5},{5,4},{6,7},{7,6},{8,9},{9,8},{10,11... | collective-permute-start | bytes 3145736 | tf_op jit(solution)/shard_map/ppermute | solution.py:315
  23.2 0.0 copy-done.2
  23.2 0.4 find.1
  23.6 0.0 copy-start
  23.6 0.0 copy-start.1
  23.6 2.8 %all-to-all-done = bf16[16,8,512]{2,1,0:T(8,128)(2,1)S(1)} async-done(((bf16[16,8,512]{2,1,0:T(8,128)(2,1)}), bf16[16,8,512]{2,1,0:T(8,128)(2,1)S(1)}, u32[]{:S(2)}, u32[]{:S(2)}) %all-to-all-start) | async-done | bytes 131104 | tf_op jit(solution)/shard_map/all_to_all | solution.py:289
  26.4 3.4 %all-gather.q_ref = bf16[32,8,512]{2,1,0:T(8,128)(2,1)S(1)} all-gather(bf16[16,8,512]{2,1,0:T(8,128)(2,1)S(1)} %all-to-all-done), channel_id=2, replica_groups={{0,16},{32,48},{64,80},{96,112},{128,144},{160,176},{192,208},{224,240}..., dimensions={0}, use_global_device_ids=true | all-gather | bytes 393216 | tf_op jit(solution)/shard_map/all_gather | solution.py:319
  29.8 0.2 select.1
  30.0 17.3 %all_to_all.20.x_ref = bf16[16,8,2048]{2,1,0:T(8,128)(2,1)S(1)} all-to-all(bf16[16,8,2048]{2,1,0:T(8,128)(2,1)S(1)} %select.1), channel_id=1, replica_groups=mesh['sx'=32,'sy'=16] {'sy'}, dimensions={0} | all-to-all | bytes 1048576 | tf_op jit(solution)/shard_map/all_to_all | solution.py:289
  47.3 0.0 collective-permute-done.kv_ref
  47.3 0.0 copy-done
  47.3 0.0 copy-done.1
  47.3 3.4 %attend.1 = bf16[16,8,2176]{2,1,0:T(8,128)(2,1)S(1)} custom-call(bf16[16,8,2048]{2,1,0:T(8,128)(2,1)S(1)} %all_to_all.20.x_ref, bf16[512,1024]{1,0:T(8,128)(2,1)S(1)} %copy-done, bf16[512,1024]{1,0:T(8,128)(2,1)S(1)} %copy-done.1, bf16[1024,512]{1,0:T(8,128)(2,1)S(1)} %collective-permute-done.kv_ref), custom_call_target="tpu_custom_call" | custom-call | tf_op jit(solution)/shard_map/attend/pallas_call | solution.py:264
  50.8 14.2 %all_to_all.21.y_ref = bf16[16,8,2176]{2,1,0:T(8,128)(2,1)S(1)} all-to-all(bf16[16,8,2176]{2,1,0:T(8,128)(2,1)S(1)} %attend.1), channel_id=1, replica_groups=mesh['sx'=32,'sy'=16] {'sy'}, dimensions={0} | all-to-all | bytes 1114112 | tf_op jit(solution)/shard_map/all_to_all | solution.py:289
  65.0 2.2 %merge.1 = (f32[128,640]{1,0:T(8,128)S(1)}, f32[128,640]{1,0:T(8,128)S(1)}) custom-call(f32[8,256]{1,0:T(8,128)S(1)} %get-tuple-element.9.pos_ref, bf16[16,8,2176]{2,1,0:T(8,128)(2,1)S(1)} %all_to_all.21.y_ref), custom_call_target="tpu_custom_call" | custom-call | tf_op jit(solution)/shard_map/merge/pallas_call | solution.py:264
  67.1 3.9 %all-gather.1 = f32[256,640]{1,0:T(8,128)S(1)} all-gather(f32[128,640]{1,0:T(8,128)S(1)} %get-tuple-element.12), channel_id=3, replica_groups={{0,16},{32,48},{64,80},{96,112},{128,144},{160,176},{192,208},{224,240}..., dimensions={0}, use_global_device_ids=true | all-gather | bytes 983040 | tf_op jit(solution)/shard_map/all_gather | solution.py:334
  71.0 0.3 pair.1
  71.4 19.4 %all_to_all.22.a_ref = bf16[16,8,640]{2,1,0:T(8,128)(2,1)S(1)} all-to-all(bf16[16,8,640]{2,1,0:T(8,128)(2,1)S(1)} %pair.1), channel_id=1, replica_groups={{256,288,320,352,384,416,448,480,0,32,64,96,128,160,192,224},{272,304,3..., dimensions={0} | all-to-all | bytes 327680 | tf_op jit(solution)/shard_map/all_to_all | solution.py:289
  90.8 0.9 last.1
Async XLA Ops:
  0.0 0.7 copy-start.3
  1.4 25.0 %all-to-all-start = ((bf16[16,8,512]{2,1,0:T(8,128)(2,1)}), bf16[16,8,512]{2,1,0:T(8,128)(2,1)S(1)}, u32[]{:S(2)}, u32[]{:S(2)}) async-start(bf16[16,8,512]{2,1,0:T(8,128)(2,1)} %copies.1), calls=%async_computation | async-start | bytes 262144 | tf_op jit(solution)/shard_map/all_to_all | solution.py:289
  17.8 5.4 %copy-start.2 = (s32[512,16]{0,1:T(8,128)S(1)}, s32[512,16]{0,1:T(8,128)}, u32[]{:S(2)}) copy-start(s32[512,16]{0,1:T(8,128)} %param.7) | copy-start | bytes 98308
  20.0 27.3 %collective-permute-start = (bf16[1024,512]{1,0:T(8,128)(2,1)}, bf16[1024,512]{1,0:T(8,128)(2,1)S(1)}, u32[]{:S(2)}, u32[]{:S(2)}) collective-permute-start(bf16[1024,512]{1,0:T(8,128)(2,1)} %relay.1), channel_id=1, source_target_pairs={{0,1},{1,0},{2,3},{3,2},{4,5},{5,4},{6,7},{7,6},{8,9},{9,8},{10,11... | collective-permute-start | bytes 3145736 | tf_op jit(solution)/shard_map/ppermute | solution.py:315
  23.6 23.7 %copy-start = (bf16[512,1024]{1,0:T(8,128)(2,1)S(1)}, bf16[512,1024]{1,0:T(8,128)(2,1)}, u32[]{:S(2)}) copy-start(bf16[512,1024]{1,0:T(8,128)(2,1)} %k_ref.3) | copy-start | bytes 3145732
  23.6 23.7 %copy-start.1 = (bf16[512,1024]{1,0:T(8,128)(2,1)S(1)}, bf16[512,1024]{1,0:T(8,128)(2,1)}, u32[]{:S(2)}) copy-start(bf16[512,1024]{1,0:T(8,128)(2,1)} %v_ref.3) | copy-start | bytes 3145732

commit v12 on v11

--- a/solution.py
+++ b/solution.py
@@ -28,8 +28,15 @@
 ANSWER_FIRST = 8
 
 
-def z_order(count, first):
+COLUMN_FIRST = 10
+
+
+def listed_from(first, count):
     return [(i + first) % count for i in range(count)]
+
+
+def column_at(i):
+    return (i - COLUMN_FIRST) % (2 * SLABS)
 
 
 def half_of(core, s):
@@ -131,7 +138,7 @@
             lanes = slice((h % HALF) * FEAT, (h % HALF + 1) * FEAT)
             halves[p, h // HALF, :, lanes] = picked[h * SLOTS : (h + 1) * SLOTS].astype(jnp.bfloat16)
         for s in range(SLABS):
-            out_ref[p * SLABS + s] = halves[p, half_of(core, s)]
+            out_ref[column_at(p * SLABS + s)] = halves[p, half_of(core, s)]
 
 
 def attend_kernel(x_ref, k_ref, v_ref, kv_ref, y_ref):
@@ -178,7 +185,10 @@
     for p in range(2):
         tall = []
         for half in range(2):
-            froms = [p * SLABS + jnp.where(core == 0, 2 * t + half, HALF * half + t) for t in range(4)]
+            froms = [
+                jnp.where(core == 0, column_at(p * SLABS + 2 * t + half), column_at(p * SLABS + HALF * half + t))
+                for t in range(4)
+            ]
             ends = []
             for s in froms:
                 stat = y_ref[s, :, HALF * FEAT :].astype(jnp.float32)
@@ -279,8 +289,9 @@
     tokens = keys.shape[0]
     cores = [[2 * z, 2 * z + 1] for z in range(count_z)]
     ask_groups, answer_groups = (
-        [[2 * z + c for z in z_order(count_z, first)] for c in range(2)] for first in (ASK_FIRST, ANSWER_FIRST)
+        [[2 * z + c for z in listed_from(first, count_z)] for c in range(2)] for first in (ASK_FIRST, ANSWER_FIRST)
     )
+    columns = [listed_from(COLUMN_FIRST, count_y)]
     partners = [
         (x * count_y + y, x * count_y + (y ^ PARTNER[x % 2])) for x in range(count_x) for y in range(count_y)
     ]
@@ -326,9 +337,9 @@
         rows,
         scratch=[pltpu.VMEM((2, 2, SLOTS, HALF * FEAT), jnp.bfloat16)],
     )
-    asked = exchange(asked, "sy")
+    asked = exchange(asked, "sy", columns)
     part = call(attend_kernel, half(count_y, SLOTS, HALF * FEAT + STAT), "attend", asked, keys, values, kv)
-    part = exchange(part, "sy")
+    part = exchange(part, "sy", columns)
     side = full(count_z * KEY_HEADS, FEAT + STAT)
     mine, theirs = call(merge_kernel, [side, side], "merge", answer_pos, part)
     pair = lax.all_gather(theirs, "sx", axis=0, axis_index_groups=cores)

time: 92.1 us -> 89.3 us (0.970)
  blocking collectives: 58.3 us -> 55.4 us
    all_to_all x3, blocking collectives: 50.9 us -> 46.1 us  [exchange(): lax.all_to_all(x, axis, split_axis=0, concat_axis=0, tiled=True, axis_ind...]
    all_gather x1, blocking collectives: 3.93 us -> 5.91 us  [per_device(): pair = lax.all_gather(theirs, 'sx', axis=0, axis_index_groups=cores)]
where the time goes in v12:
time: 89.3 us; the launch traced here: 88.9 us
  blocking collectives  55.4 us (62%)
  starting transfers between devices  19.6 us (22%)
  Pallas kernels  10.2 us (11%)
  waiting for transfers between devices  2.81 us (3%)
    all_to_all x3, blocking collectives, exchange(): lax.all_to_all(x, axis, split_axis=0, concat_axis=0, tiled=True, axis_ind...  46.1 us
    all_to_all x1, starting transfers between devices, exchange(): lax.all_to_all(x, axis, split_axis=0, concat_axis=0, tiled=True, axis_ind...  16.4 us
    pallas_call x7, Pallas kernels, call(): pl.pallas_call(kernel, out_shape=out, in_specs=[pl.BlockSpec(memory_space...  8.08 us
    all_gather x1, blocking collectives, per_device(): pair = lax.all_gather(theirs, 'sx', axis=0, axis_index_groups=cores)  5.91 us
    all_gather x1, blocking collectives, per_device(): rows = lax.all_gather(rows, 'sx', axis=0, axis_index_groups=cores)  3.41 us
    ppermute x1, starting transfers between devices, per_device(): kv = lax.ppermute(kv, ('sx', 'sy'), partners)  3.2 us
    all_to_all x1, waiting for transfers between devices, exchange(): lax.all_to_all(x, axis, split_axis=0, concat_axis=0, tiled=True, axis_ind...  2.81 us
    pallas_call x1, Pallas kernels, per_device(): pl.pallas_call(relay_kernel, out_shape=half(2 * tokens, width), in_specs=...  2.13 us
  transfers between devices with their start and end apart: 2, of which 1 were waited for; matrix products, arithmetic and copies ran while one was open for 0% of the time, Pallas kernels for 3%

profile of v12, /device:TPU:1, one launch (start us, length us, event | category | flops | bytes accessed | tf_op | source)
XLA Modules:
  0.0 88.9 jit_solution(10264898089547960796)
XLA Ops:
  0.0 0.0 copy-start.3
  0.0 0.7 copy-done.3
  0.7 0.7 copies.1
  1.4 16.4 %all-to-all-start = ((bf16[16,8,512]{2,1,0:T(8,128)(2,1)}), bf16[16,8,512]{2,1,0:T(8,128)(2,1)S(1)}, u32[]{:S(2)}, u32[]{:S(2)}) async-start(bf16[16,8,512]{2,1,0:T(8,128)(2,1)} %copies.1), calls=%async_computation | async-start | bytes 262144 | tf_op jit(solution)/shard_map/all_to_all | solution.py:300
  17.8 0.0 copy-start.2
  17.8 2.1 %relay.1 = bf16[1024,512]{1,0:T(8,128)(2,1)} custom-call(bf16[512,1024]{1,0:T(8,128)(2,1)} %k_ref.3, bf16[512,1024]{1,0:T(8,128)(2,1)} %v_ref.3), custom_call_target="tpu_custom_call" | custom-call | tf_op jit(solution)/shard_map/relay/pallas_call | solution.py:313
  20.0 3.2 %collective-permute-start = (bf16[1024,512]{1,0:T(8,128)(2,1)}, bf16[1024,512]{1,0:T(8,128)(2,1)S(1)}, u32[]{:S(2)}, u32[]{:S(2)}) collective-permute-start(bf16[1024,512]{1,0:T(8,128)(2,1)} %relay.1), channel_id=1, source_target_pairs={{0,1},{1,0},{2,3},{3,2},{4,5},{5,4},{6,7},{7,6},{8,9},{9,8},{10,11... | collective-permute-start | bytes 3145736 | tf_op jit(solution)/shard_map/ppermute | solution.py:326
  23.2 0.0 copy-done.2
  23.2 0.4 find.1
  23.6 0.0 copy-start
  23.6 0.0 copy-start.1
  23.6 2.8 %all-to-all-done = bf16[16,8,512]{2,1,0:T(8,128)(2,1)S(1)} async-done(((bf16[16,8,512]{2,1,0:T(8,128)(2,1)}), bf16[16,8,512]{2,1,0:T(8,128)(2,1)S(1)}, u32[]{:S(2)}, u32[]{:S(2)}) %all-to-all-start) | async-done | bytes 131104 | tf_op jit(solution)/shard_map/all_to_all | solution.py:300
  26.4 3.4 %all-gather.q_ref = bf16[32,8,512]{2,1,0:T(8,128)(2,1)S(1)} all-gather(bf16[16,8,512]{2,1,0:T(8,128)(2,1)S(1)} %all-to-all-done), channel_id=2, replica_groups={{0,16},{32,48},{64,80},{96,112},{128,144},{160,176},{192,208},{224,240}..., dimensions={0}, use_global_device_ids=true | all-gather | bytes 393216 | tf_op jit(solution)/shard_map/all_gather | solution.py:330
  29.8 0.2 select.1
  30.0 15.5 %all_to_all.20.x_ref = bf16[16,8,2048]{2,1,0:T(8,128)(2,1)S(1)} all-to-all(bf16[16,8,2048]{2,1,0:T(8,128)(2,1)S(1)} %select.1), channel_id=1, replica_groups={{10,11,12,13,14,15,0,1,2,3,4,5,6,7,8,9},{26,27,28,29,30,31,16,17,18,19,..., dimensions={0} | all-to-all | bytes 1048576 | tf_op jit(solution)/shard_map/all_to_all | solution.py:300
  45.5 0.0 collective-permute-done.kv_ref
  45.5 0.0 copy-done
  45.5 0.0 copy-done.1
  45.5 3.4 %attend.1 = bf16[16,8,2176]{2,1,0:T(8,128)(2,1)S(1)} custom-call(bf16[16,8,2048]{2,1,0:T(8,128)(2,1)S(1)} %all_to_all.20.x_ref, bf16[512,1024]{1,0:T(8,128)(2,1)S(1)} %copy-done, bf16[512,1024]{1,0:T(8,128)(2,1)S(1)} %copy-done.1, bf16[1024,512]{1,0:T(8,128)(2,1)S(1)} %collective-permute-done.kv_ref), custom_call_target="tpu_custom_call" | custom-call | tf_op jit(solution)/shard_map/attend/pallas_call | solution.py:274
  49.0 11.2 %all_to_all.21.y_ref = bf16[16,8,2176]{2,1,0:T(8,128)(2,1)S(1)} all-to-all(bf16[16,8,2176]{2,1,0:T(8,128)(2,1)S(1)} %attend.1), channel_id=1, replica_groups={{10,11,12,13,14,15,0,1,2,3,4,5,6,7,8,9},{26,27,28,29,30,31,16,17,18,19,..., dimensions={0} | all-to-all | bytes 1114112 | tf_op jit(solution)/shard_map/all_to_all | solution.py:300
  60.1 2.1 %merge.1 = (f32[128,640]{1,0:T(8,128)S(1)}, f32[128,640]{1,0:T(8,128)S(1)}) custom-call(f32[8,256]{1,0:T(8,128)S(1)} %get-tuple-element.9.pos_ref, bf16[16,8,2176]{2,1,0:T(8,128)(2,1)S(1)} %all_to_all.21.y_ref), custom_call_target="tpu_custom_call" | custom-call | tf_op jit(solution)/shard_map/merge/pallas_call | solution.py:274
  62.3 5.9 %all-gather.1 = f32[256,640]{1,0:T(8,128)S(1)} all-gather(f32[128,640]{1,0:T(8,128)S(1)} %get-tuple-element.12), channel_id=3, replica_groups={{0,16},{32,48},{64,80},{96,112},{128,144},{160,176},{192,208},{224,240}..., dimensions={0}, use_global_device_ids=true | all-gather | bytes 983040 | tf_op jit(solution)/shard_map/all_gather | solution.py:345
  68.2 0.3 pair.1
  68.6 19.4 %all_to_all.22.a_ref = bf16[16,8,640]{2,1,0:T(8,128)(2,1)S(1)} all-to-all(bf16[16,8,640]{2,1,0:T(8,128)(2,1)S(1)} %pair.1), channel_id=1, replica_groups={{256,288,320,352,384,416,448,480,0,32,64,96,128,160,192,224},{272,304,3..., dimensions={0} | all-to-all | bytes 327680 | tf_op jit(solution)/shard_map/all_to_all | solution.py:300
  88.0 0.9 last.1
Async XLA Ops:
  0.0 0.7 copy-start.3
  1.4 25.0 %all-to-all-start = ((bf16[16,8,512]{2,1,0:T(8,128)(2,1)}), bf16[16,8,512]{2,1,0:T(8,128)(2,1)S(1)}, u32[]{:S(2)}, u32[]{:S(2)}) async-start(bf16[16,8,512]{2,1,0:T(8,128)(2,1)} %copies.1), calls=%async_computation | async-start | bytes 262144 | tf_op jit(solution)/shard_map/all_to_all | solution.py:300
  17.8 5.4 %copy-start.2 = (s32[512,16]{0,1:T(8,128)S(1)}, s32[512,16]{0,1:T(8,128)}, u32[]{:S(2)}) copy-start(s32[512,16]{0,1:T(8,128)} %param.7) | copy-start | bytes 98308
  20.0 25.6 %collective-permute-start = (bf16[1024,512]{1,0:T(8,128)(2,1)}, bf16[1024,512]{1,0:T(8,128)(2,1)S(1)}, u32[]{:S(2)}, u32[]{:S(2)}) collective-permute-start(bf16[1024,512]{1,0:T(8,128)(2,1)} %relay.1), channel_id=1, source_target_pairs={{0,1},{1,0},{2,3},{3,2},{4,5},{5,4},{6,7},{7,6},{8,9},{9,8},{10,11... | collective-permute-start | bytes 3145736 | tf_op jit(solution)/shard_map/ppermute | solution.py:326
  23.6 22.0 %copy-start = (bf16[512,1024]{1,0:T(8,128)(2,1)S(1)}, bf16[512,1024]{1,0:T(8,128)(2,1)}, u32[]{:S(2)}) copy-start(bf16[512,1024]{1,0:T(8,128)(2,1)} %k_ref.3) | copy-start | bytes 3145732
  23.6 22.0 %copy-start.1 = (bf16[512,1024]{1,0:T(8,128)(2,1)S(1)}, bf16[512,1024]{1,0:T(8,128)(2,1)}, u32[]{:S(2)}) copy-start(bf16[512,1024]{1,0:T(8,128)(2,1)} %v_ref.3) | copy-start | bytes 3145732

commit v13 on v12

--- a/solution.py
+++ b/solution.py
@@ -22,6 +22,7 @@
 PARTNER = (1, 4)
 STAT = 128
 ONE_LANE = 12
+PART_ROWS = QUERY_HEADS + 2
 
 
 ASK_FIRST = 11
@@ -50,13 +51,14 @@
     return hi, mid, rest - mid
 
 
-def stat_lanes(lse):
-    lane = lax.broadcasted_iota(jnp.int32, (lse[0].shape[0], STAT), 1)
-    stat = jnp.zeros(lane.shape, jnp.float32)
-    for at, x in enumerate(lse):
-        for k, piece in enumerate(pieces(x)):
-            stat = jnp.where(lane == at * 3 + k, piece, stat)
-    return stat
+def spread_pieces(lse):
+    lane = lax.broadcasted_iota(jnp.int32, lse.shape, 1)
+    hi, mid, lo = pieces(lse)
+    return jnp.where(lane % 3 == 0, hi, jnp.where(lane % 3 == 1, pltpu.roll(mid, 1, 1), pltpu.roll(lo, 2, 1)))
+
+
+def sum_pieces(stat):
+    return stat + (pltpu.roll(stat, STAT - 1, 1) + pltpu.roll(stat, STAT - 2, 1))
 
 
 def find_kernel(ids_ref, ask_ref, answer_ref):
@@ -167,14 +169,19 @@
         both = functools.reduce(jnp.add, [jnp.exp2((m - top) * scale) * o for m, o in zip(tops, sums)])
         total = both[:, HEAD_WIDTH:]
         out = both[:, :HEAD_WIDTH] / total
-        lse = top * scale + jnp.log2(total[:, :1])
+        lse = top * scale + jnp.log2(total)
         for g in range(QUERY_PER_KEY):
             part = out[g * rows : (g + 1) * rows].reshape(columns, SLOTS, HEAD_WIDTH).astype(jnp.bfloat16)
             at = (h * QUERY_PER_KEY + g) * HEAD_WIDTH
             y_ref[:, :, at : at + HEAD_WIDTH] = part
             ends.append(lse[g * rows : (g + 1) * rows])
-    stat = stat_lanes(ends).reshape(columns, SLOTS, STAT).astype(jnp.bfloat16)
-    y_ref[:, :, HALF * FEAT :] = stat
+    lane = lax.broadcasted_iota(jnp.int32, (rows, STAT), 1)
+    stat = jnp.zeros((rows, STAT), jnp.float32)
+    for n, x in enumerate(ends):
+        stat = jnp.where(lane // 3 == n, x, stat)
+    hi, mid, lo = pieces(stat)
+    stat = jnp.where(lane % 3 == 0, hi, jnp.where(lane % 3 == 1, mid, lo))
+    y_ref[:, :, HALF * FEAT :] = stat.reshape(columns, SLOTS, STAT).astype(jnp.bfloat16)
 
 
 def merge_kernel(pos_ref, y_ref, mine_ref, theirs_ref):
@@ -191,8 +198,7 @@
             ]
             ends = []
             for s in froms:
-                stat = y_ref[s, :, HALF * FEAT :].astype(jnp.float32)
-                ends.append(stat + (pltpu.roll(stat, STAT - 1, 1) + pltpu.roll(stat, STAT - 2, 1)))
+                ends.append(sum_pieces(y_ref[s, :, HALF * FEAT :].astype(jnp.float32)))
             top = functools.reduce(jnp.maximum, ends)
             weights = [jnp.exp2(x - top) for x in ends]
             total = functools.reduce(jnp.add, weights)
@@ -213,61 +219,57 @@
         tall = jnp.concatenate([x.astype(jnp.bfloat16) for x in pieces(jnp.concatenate(tall, axis=0))], axis=0)
         hot = jnp.concatenate([slot_onehot(pos_ref[p : p + 1, :])] * 3, axis=0)
         dense = lax.dot_general(hot, tall, flip, preferred_element_type=jnp.float32)
-        named = dense[:, FEAT + ONE_LANE : FEAT + ONE_LANE + 1] > 0.5
+        stat = dense[:, FEAT:]
         data.append(dense)
-        lse.append(
-            [jnp.where(named, dense[:, FEAT + 3 * g : FEAT + 3 * g + 1], NEVER) for g in range(QUERY_PER_KEY)]
-        )
+        lse.append(jnp.where(stat[:, ONE_LANE : ONE_LANE + 1] > 0.5, stat, NEVER))
+    mixed = jnp.concatenate(combine_two(data, lse), axis=1)
     rows = mine_ref.shape[0]
-    for out_ref, is_first in ((mine_ref, core == 0), (theirs_ref, core == 1)):
-
-        def side(x):
-            return jnp.where(is_first, x[:rows], x[rows:])
-
-        combine_two([side(x) for x in data], [[side(x) for x in y] for y in lse], out_ref)
-
-
-def combine_two(data, lse, out_ref):
-    shape = out_ref.shape[:-1]
-    ends = []
+    mine_ref[...] = jnp.where(core == 0, mixed[:rows], mixed[rows:])
+    theirs_ref[...] = jnp.where(core == 0, mixed[rows:], mixed[:rows])
+
+
+def combine_two(data, lse):
+    top = jnp.maximum(lse[0], lse[1])
+    weights = [jnp.exp2(x - top) for x in lse]
+    total = weights[0] + weights[1]
+    inverse = 1.0 / total
+    weights = [w * inverse for w in weights]
+    mixed = []
     for g in range(QUERY_PER_KEY):
-        a, b = lse[0][g], lse[1][g]
-        top = jnp.maximum(a, b)
-        wa, wb = jnp.exp2(a - top), jnp.exp2(b - top)
-        total = wa + wb
-        inverse = 1.0 / total
         lanes = slice(g * HEAD_WIDTH, (g + 1) * HEAD_WIDTH)
-        mixed = data[0][:, lanes] * (wa * inverse) + data[1][:, lanes] * (wb * inverse)
-        out_ref[..., lanes] = mixed.reshape(*shape, HEAD_WIDTH).astype(out_ref.dtype)
-        ends.append(top + jnp.log2(total))
-    if out_ref.dtype == jnp.float32:
-        lane = lax.broadcasted_iota(jnp.int32, (mixed.shape[0], STAT), 1)
-        stat = jnp.zeros(lane.shape, jnp.float32)
+        terms = [x[:, lanes] * w[:, 3 * g : 3 * g + 1] for x, w in zip(data, weights)]
+        mixed.append(terms[0] + terms[1])
+    return mixed + [top + jnp.log2(total)]
+
+
+def pair_kernel(mine_ref, pair_ref, out_ref, wide, stats):
+    other = 1 - lax.axis_index("sx") % 2
+    refs = (mine_ref, pair_ref.at[other])
+    mixed = combine_two([x[:, :FEAT] for x in refs], [x[:, FEAT:] for x in refs])
+    count = out_ref.shape[0] // PART_ROWS
+    for z in range(count):
         for g in range(QUERY_PER_KEY):
-            stat = jnp.where(lane == g, ends[g], stat)
-    else:
-        stat = stat_lanes(ends)
-    out_ref[..., FEAT:] = stat.reshape(*shape, STAT).astype(out_ref.dtype)
-
-
-def pair_kernel(mine_ref, pair_ref, out_ref):
-    other = 1 - lax.axis_index("sx") % 2
-    data = [mine_ref[:, :FEAT], pair_ref[other, :, :FEAT]]
-    lse = [[x[:, g : g + 1] for g in range(QUERY_PER_KEY)] for x in (mine_ref[:, FEAT:], pair_ref[other, :, FEAT:])]
-    combine_two(data, lse, out_ref)
-
-
-def last_kernel(a_ref, out_ref):
-    stat = a_ref[:, :, FEAT:].astype(jnp.float32)
-    lse = stat + (pltpu.roll(stat, STAT - 1, 2) + pltpu.roll(stat, STAT - 2, 2))
+            part = mixed[g][z * KEY_HEADS : (z + 1) * KEY_HEADS]
+            wide[pl.ds(z * PART_ROWS + g, KEY_HEADS, stride=QUERY_PER_KEY), :] = part
+    lane = lax.broadcasted_iota(jnp.int32, stats.shape, 1)
+    stats[...] = jnp.where(lane < ONE_LANE, spread_pieces(mixed[-1]), 0.0)
+    terms = [stats[pl.ds(h, count, stride=KEY_HEADS), :] for h in range(KEY_HEADS)]
+    terms = [x if h == 0 else pltpu.roll(x, ONE_LANE * h, 1) for h, x in enumerate(terms)]
+    wide[pl.ds(QUERY_HEADS, count, stride=PART_ROWS), :] = functools.reduce(jnp.add, terms)
+    wide[pl.ds(QUERY_HEADS + 1, count, stride=PART_ROWS), :] = jnp.zeros((count, STAT), jnp.float32)
+    out_ref[...] = wide[...].astype(jnp.bfloat16)
+
+
+def last_kernel(a_ref, out_ref, wide):
+    count = a_ref.shape[0] // PART_ROWS
+    wide[...] = a_ref[...].astype(jnp.float32)
+    lse = sum_pieces(wide[pl.ds(QUERY_HEADS, count, stride=PART_ROWS), :])
     weight = jnp.exp2(lse - jnp.max(lse, axis=0, keepdims=True))
     weight = weight / jnp.sum(weight, axis=0, keepdims=True)
-    for g in range(QUERY_PER_KEY):
-        lanes = slice(g * HEAD_WIDTH, (g + 1) * HEAD_WIDTH)
-        mixed = jnp.sum(a_ref[:, :, lanes].astype(jnp.float32) * weight[:, :, 3 * g : 3 * g + 1], axis=0)
-        for h in range(KEY_HEADS):
-            head = h * FEAT + g * HEAD_WIDTH
-            out_ref[:, head : head + HEAD_WIDTH] = mixed[h : h + 1].astype(jnp.bfloat16)
+    for n in range(QUERY_HEADS):
+        part = wide[pl.ds(n, count, stride=PART_ROWS), :] * weight[:, 3 * n : 3 * n + 1]
+        part = jnp.sum(part, axis=0, keepdims=True)
+        out_ref[:, n * HEAD_WIDTH : (n + 1) * HEAD_WIDTH] = part.astype(jnp.bfloat16)
 
 
 def call(kernel, out, name, *args, scratch=()):
@@ -343,9 +345,11 @@
     side = full(count_z * KEY_HEADS, FEAT + STAT)
     mine, theirs = call(merge_kernel, [side, side], "merge", answer_pos, part)
     pair = lax.all_gather(theirs, "sx", axis=0, axis_index_groups=cores)
-    part = call(pair_kernel, half(count_z, KEY_HEADS, FEAT + STAT), "pair", mine, pair)
-    part = exchange(part, "sx", answer_groups)
-    return call(last_kernel, half(1, KEY_HEADS * FEAT), "last", part)
+    wide = pltpu.VMEM((count_z * PART_ROWS, HEAD_WIDTH), jnp.float32)
+    stats = pltpu.VMEM((count_z * KEY_HEADS, STAT), jnp.float32)
+    part = call(pair_kernel, half(*wide.shape), "pair", mine, pair, scratch=[wide, stats])
+    part = exchange(part.reshape(count_z, PART_ROWS // 2, 2, HEAD_WIDTH), "sx", answer_groups)
+    return call(last_kernel, half(1, KEY_HEADS * FEAT), "last", part.reshape(wide.shape), scratch=[wide])
 
 
 def solution(mesh):

time: 89.3 us -> 87.8 us (0.983)
  blocking collectives: 55.4 us -> 54.4 us
    all_to_all x3, blocking collectives: 46.1 us -> 45.1 us  [exchange(): lax.all_to_all(x, axis, split_axis=0, concat_axis=0, tiled=True, axis_ind...]
where the time goes in v13:
time: 87.8 us; the launch traced here: 87.4 us
  blocking collectives  54.4 us (62%)
  starting transfers between devices  19.6 us (22%)
  Pallas kernels  9.75 us (11%)
  waiting for transfers between devices  2.81 us (3%)
    all_to_all x3, blocking collectives, exchange(): lax.all_to_all(x, axis, split_axis=0, concat_axis=0, tiled=True, axis_ind...  45.1 us
    all_to_all x1, starting transfers between devices, exchange(): lax.all_to_all(x, axis, split_axis=0, concat_axis=0, tiled=True, axis_ind...  16.4 us
    pallas_call x7, Pallas kernels, call(): pl.pallas_call(kernel, out_shape=out, in_specs=[pl.BlockSpec(memory_space...  7.61 us
    all_gather x1, blocking collectives, per_device(): pair = lax.all_gather(theirs, 'sx', axis=0, axis_index_groups=cores)  5.91 us
    all_gather x1, blocking collectives, per_device(): rows = lax.all_gather(rows, 'sx', axis=0, axis_index_groups=cores)  3.41 us
    ppermute x1, starting transfers between devices, per_device(): kv = lax.ppermute(kv, ('sx', 'sy'), partners)  3.2 us
    all_to_all x1, waiting for transfers between devices, exchange(): lax.all_to_all(x, axis, split_axis=0, concat_axis=0, tiled=True, axis_ind...  2.81 us
    pallas_call x1, Pallas kernels, per_device(): pl.pallas_call(relay_kernel, out_shape=half(2 * tokens, width), in_specs=...  2.13 us
  transfers between devices with their start and end apart: 2, of which 1 were waited for; matrix products, arithmetic and copies ran while one was open for 0% of the time, Pallas kernels for 3%

profile of v13, /device:TPU:1, one launch (start us, length us, event | category | flops | bytes accessed | tf_op | source)
XLA Modules:
  0.0 87.4 jit_solution(3258263892182240825)
XLA Ops:
  0.0 0.0 copy-start.3
  0.0 0.7 copy-done.3
  0.7 0.7 copies.1
  1.4 16.4 %all-to-all-start = ((bf16[16,8,512]{2,1,0:T(8,128)(2,1)}), bf16[16,8,512]{2,1,0:T(8,128)(2,1)S(1)}, u32[]{:S(2)}, u32[]{:S(2)}) async-start(bf16[16,8,512]{2,1,0:T(8,128)(2,1)} %copies.1), calls=%async_computation | async-start | bytes 262144 | tf_op jit(solution)/shard_map/all_to_all | solution.py:302
  17.8 0.0 copy-start.2
  17.8 2.1 %relay.1 = bf16[1024,512]{1,0:T(8,128)(2,1)} custom-call(bf16[512,1024]{1,0:T(8,128)(2,1)} %k_ref.3, bf16[512,1024]{1,0:T(8,128)(2,1)} %v_ref.3), custom_call_target="tpu_custom_call" | custom-call | tf_op jit(solution)/shard_map/relay/pallas_call | solution.py:315
  20.0 3.2 %collective-permute-start = (bf16[1024,512]{1,0:T(8,128)(2,1)}, bf16[1024,512]{1,0:T(8,128)(2,1)S(1)}, u32[]{:S(2)}, u32[]{:S(2)}) collective-permute-start(bf16[1024,512]{1,0:T(8,128)(2,1)} %relay.1), channel_id=1, source_target_pairs={{0,1},{1,0},{2,3},{3,2},{4,5},{5,4},{6,7},{7,6},{8,9},{9,8},{10,11... | collective-permute-start | bytes 3145736 | tf_op jit(solution)/shard_map/ppermute | solution.py:328
  23.2 0.0 copy-done.2
  23.2 0.4 find.1
  23.6 0.0 copy-start
  23.6 0.0 copy-start.1
  23.6 2.8 %all-to-all-done = bf16[16,8,512]{2,1,0:T(8,128)(2,1)S(1)} async-done(((bf16[16,8,512]{2,1,0:T(8,128)(2,1)}), bf16[16,8,512]{2,1,0:T(8,128)(2,1)S(1)}, u32[]{:S(2)}, u32[]{:S(2)}) %all-to-all-start) | async-done | bytes 131104 | tf_op jit(solution)/shard_map/all_to_all | solution.py:302
  26.4 3.4 %all-gather.q_ref = bf16[32,8,512]{2,1,0:T(8,128)(2,1)S(1)} all-gather(bf16[16,8,512]{2,1,0:T(8,128)(2,1)S(1)} %all-to-all-done), channel_id=2, replica_groups={{0,16},{32,48},{64,80},{96,112},{128,144},{160,176},{192,208},{224,240}..., dimensions={0}, use_global_device_ids=true | all-gather | bytes 393216 | tf_op jit(solution)/shard_map/all_gather | solution.py:332
  29.8 0.2 select.1
  30.0 15.5 %all_to_all.20.x_ref = bf16[16,8,2048]{2,1,0:T(8,128)(2,1)S(1)} all-to-all(bf16[16,8,2048]{2,1,0:T(8,128)(2,1)S(1)} %select.1), channel_id=1, replica_groups={{10,11,12,13,14,15,0,1,2,3,4,5,6,7,8,9},{26,27,28,29,30,31,16,17,18,19,..., dimensions={0} | all-to-all | bytes 1048576 | tf_op jit(solution)/shard_map/all_to_all | solution.py:302
  45.5 0.0 collective-permute-done.kv_ref
  45.5 0.0 copy-done
  45.5 0.0 copy-done.1
  45.5 3.2 %attend.1 = bf16[16,8,2176]{2,1,0:T(8,128)(2,1)S(1)} custom-call(bf16[16,8,2048]{2,1,0:T(8,128)(2,1)S(1)} %all_to_all.20.x_ref, bf16[512,1024]{1,0:T(8,128)(2,1)S(1)} %copy-done, bf16[512,1024]{1,0:T(8,128)(2,1)S(1)} %copy-done.1, bf16[1024,512]{1,0:T(8,128)(2,1)S(1)} %collective-permute-done.kv_ref), custom_call_target="tpu_custom_call" | custom-call | tf_op jit(solution)/shard_map/attend/pallas_call | solution.py:276
  48.7 11.2 %all_to_all.21.y_ref = bf16[16,8,2176]{2,1,0:T(8,128)(2,1)S(1)} all-to-all(bf16[16,8,2176]{2,1,0:T(8,128)(2,1)S(1)} %attend.1), channel_id=1, replica_groups={{10,11,12,13,14,15,0,1,2,3,4,5,6,7,8,9},{26,27,28,29,30,31,16,17,18,19,..., dimensions={0} | all-to-all | bytes 1114112 | tf_op jit(solution)/shard_map/all_to_all | solution.py:302
  59.9 1.9 %merge.1 = (f32[128,640]{1,0:T(8,128)S(1)}, f32[128,640]{1,0:T(8,128)S(1)}) custom-call(f32[8,256]{1,0:T(8,128)S(1)} %get-tuple-element.9.pos_ref, bf16[16,8,2176]{2,1,0:T(8,128)(2,1)S(1)} %all_to_all.21.y_ref), custom_call_target="tpu_custom_call" | custom-call | tf_op jit(solution)/shard_map/merge/pallas_call | solution.py:276
  61.8 5.9 %all-gather.1 = f32[256,640]{1,0:T(8,128)S(1)} all-gather(f32[128,640]{1,0:T(8,128)S(1)} %get-tuple-element.12), channel_id=3, replica_groups={{0,16},{32,48},{64,80},{96,112},{128,144},{160,176},{192,208},{224,240}..., dimensions={0}, use_global_device_ids=true | all-gather | bytes 983040 | tf_op jit(solution)/shard_map/all_gather | solution.py:347
  67.7 0.4 pair.1
  68.1 18.4 %all_to_all.22 = bf16[16,17,2,128]{3,2,1,0:T(2,128)(2,1)S(1)} all-to-all(bf16[16,17,2,128]{3,2,1,0:T(2,128)(2,1)S(1)} %bitcast.5), channel_id=1, replica_groups={{256,288,320,352,384,416,448,480,0,32,64,96,128,160,192,224},{272,304,3..., dimensions={0} | all-to-all | bytes 278528 | tf_op jit(solution)/shard_map/all_to_all | solution.py:302
  86.5 0.9 %last.1 = bf16[1,4096]{1,0:T(2,128)(2,1)} custom-call(bf16[544,128]{1,0:T(8,128)(2,1)S(1)} %bitcast.6), custom_call_target="tpu_custom_call" | custom-call | tf_op jit(solution)/shard_map/last/pallas_call | solution.py:276
Async XLA Ops:
  0.0 0.7 copy-start.3
  1.4 25.0 %all-to-all-start = ((bf16[16,8,512]{2,1,0:T(8,128)(2,1)}), bf16[16,8,512]{2,1,0:T(8,128)(2,1)S(1)}, u32[]{:S(2)}, u32[]{:S(2)}) async-start(bf16[16,8,512]{2,1,0:T(8,128)(2,1)} %copies.1), calls=%async_computation | async-start | bytes 262144 | tf_op jit(solution)/shard_map/all_to_all | solution.py:302
  17.8 5.4 %copy-start.2 = (s32[512,16]{0,1:T(8,128)S(1)}, s32[512,16]{0,1:T(8,128)}, u32[]{:S(2)}) copy-start(s32[512,16]{0,1:T(8,128)} %param.7) | copy-start | bytes 98308
  20.0 25.6 %collective-permute-start = (bf16[1024,512]{1,0:T(8,128)(2,1)}, bf16[1024,512]{1,0:T(8,128)(2,1)S(1)}, u32[]{:S(2)}, u32[]{:S(2)}) collective-permute-start(bf16[1024,512]{1,0:T(8,128)(2,1)} %relay.1), channel_id=1, source_target_pairs={{0,1},{1,0},{2,3},{3,2},{4,5},{5,4},{6,7},{7,6},{8,9},{9,8},{10,11... | collective-permute-start | bytes 3145736 | tf_op jit(solution)/shard_map/ppermute | solution.py:328
  23.6 22.0 %copy-start = (bf16[512,1024]{1,0:T(8,128)(2,1)S(1)}, bf16[512,1024]{1,0:T(8,128)(2,1)}, u32[]{:S(2)}) copy-start(bf16[512,1024]{1,0:T(8,128)(2,1)} %k_ref.3) | copy-start | bytes 3145732
  23.6 22.0 %copy-start.1 = (bf16[512,1024]{1,0:T(8,128)(2,1)S(1)}, bf16[512,1024]{1,0:T(8,128)(2,1)}, u32[]{:S(2)}) copy-start(bf16[512,1024]{1,0:T(8,128)(2,1)} %v_ref.3) | copy-start | bytes 3145732

commit v14 on v13

--- a/solution.py
+++ b/solution.py
@@ -83,13 +83,19 @@
     before = jnp.where(r < c, 1.0, 0.0).astype(jnp.bfloat16)
     rank = jnp.dot(named.astype(jnp.bfloat16), before, preferred_element_type=jnp.float32)
     pos = jnp.where(named > 0.5, rank, -1.0).astype(jnp.bfloat16)
-    for out_ref, first in ((ask_ref, ASK_FIRST), (answer_ref, ANSWER_FIRST)):
-        shape = (lanes, out_ref.shape[1])
-        r = lax.broadcasted_iota(jnp.int32, shape, 0)
-        c = lax.broadcasted_iota(jnp.int32, shape, 1) // KEY_HEADS
-        row = ((c + first) % count_z) * 2 + c // count_z
-        spread = jnp.where(r == row, 1.0, 0.0).astype(jnp.bfloat16)
-        out_ref[...] = jnp.dot(pos, spread, preferred_element_type=jnp.float32)
+    shape = (lanes, ask_ref.shape[1])
+    r = lax.broadcasted_iota(jnp.int32, shape, 0)
+    c = lax.broadcasted_iota(jnp.int32, shape, 1) // KEY_HEADS
+    row = ((c + ASK_FIRST) % count_z) * 2 + c // count_z
+    spread = jnp.where(r == row, 1.0, 0.0).astype(jnp.bfloat16)
+    ask_ref[...] = jnp.dot(pos, spread, preferred_element_type=jnp.float32)
+    shape = (answer_ref.shape[0], lanes)
+    r = lax.broadcasted_iota(jnp.int32, shape, 0) // KEY_HEADS
+    c = lax.broadcasted_iota(jnp.int32, shape, 1)
+    row = ((r + ANSWER_FIRST) % count_z) * 2 + r // count_z
+    spread = jnp.where(c == row, 1.0, 0.0).astype(jnp.bfloat16)
+    across = (((1,), (1,)), ((), ()))
+    answer_ref[...] = lax.dot_general(spread, pos, across, preferred_element_type=jnp.float32)
 
 
 def slot_onehot(pos):
@@ -186,7 +192,6 @@
 
 def merge_kernel(pos_ref, y_ref, mine_ref, theirs_ref):
     core = lax.axis_index("sx") % 2
-    flip = (((0,), (0,)), ((), ()))
     lane = lax.broadcasted_iota(jnp.int32, (SLOTS, STAT), 1)
     data, lse = [], []
     for p in range(2):
@@ -217,8 +222,12 @@
                 stat = jnp.where(lane == ONE_LANE, 1.0, jnp.where(lane < ONE_LANE, stat, 0.0))
                 tall.append(jnp.concatenate(heads + [stat], axis=1))
         tall = jnp.concatenate([x.astype(jnp.bfloat16) for x in pieces(jnp.concatenate(tall, axis=0))], axis=0)
-        hot = jnp.concatenate([slot_onehot(pos_ref[p : p + 1, :])] * 3, axis=0)
-        dense = lax.dot_general(hot, tall, flip, preferred_element_type=jnp.float32)
+        shape = (pos_ref.shape[0], 3 * KEY_HEADS * SLOTS)
+        r = lax.broadcasted_iota(jnp.int32, shape, 0)
+        c = lax.broadcasted_iota(jnp.int32, shape, 1)
+        hit = (pos_ref[:, p : p + 1] == (c % SLOTS).astype(jnp.float32)) & (c // SLOTS % KEY_HEADS == r % KEY_HEADS)
+        hot = jnp.where(hit, 1.0, 0.0).astype(jnp.bfloat16)
+        dense = jnp.dot(hot, tall, preferred_element_type=jnp.float32)
         stat = dense[:, FEAT:]
         data.append(dense)
         lse.append(jnp.where(stat[:, ONE_LANE : ONE_LANE + 1] > 0.5, stat, NEVER))
@@ -251,25 +260,27 @@
         for g in range(QUERY_PER_KEY):
             part = mixed[g][z * KEY_HEADS : (z + 1) * KEY_HEADS]
             wide[pl.ds(z * PART_ROWS + g, KEY_HEADS, stride=QUERY_PER_KEY), :] = part
-    lane = lax.broadcasted_iota(jnp.int32, stats.shape, 1)
-    stats[...] = jnp.where(lane < ONE_LANE, spread_pieces(mixed[-1]), 0.0)
+    stat = spread_pieces(mixed[-1])
+    lane = lax.broadcasted_iota(jnp.int32, stat.shape, 1)
+    stats[: stat.shape[0]] = jnp.where(lane < ONE_LANE, stat, 0.0)
     terms = [stats[pl.ds(h, count, stride=KEY_HEADS), :] for h in range(KEY_HEADS)]
     terms = [x if h == 0 else pltpu.roll(x, ONE_LANE * h, 1) for h, x in enumerate(terms)]
     wide[pl.ds(QUERY_HEADS, count, stride=PART_ROWS), :] = functools.reduce(jnp.add, terms)
     wide[pl.ds(QUERY_HEADS + 1, count, stride=PART_ROWS), :] = jnp.zeros((count, STAT), jnp.float32)
-    out_ref[...] = wide[...].astype(jnp.bfloat16)
+    out_ref[...] = wide[: out_ref.shape[0]].astype(jnp.bfloat16)
 
 
 def last_kernel(a_ref, out_ref, wide):
     count = a_ref.shape[0] // PART_ROWS
-    wide[...] = a_ref[...].astype(jnp.float32)
+    wide[: a_ref.shape[0]] = a_ref[...].astype(jnp.float32)
     lse = sum_pieces(wide[pl.ds(QUERY_HEADS, count, stride=PART_ROWS), :])
     weight = jnp.exp2(lse - jnp.max(lse, axis=0, keepdims=True))
     weight = weight / jnp.sum(weight, axis=0, keepdims=True)
+    parts = []
     for n in range(QUERY_HEADS):
         part = wide[pl.ds(n, count, stride=PART_ROWS), :] * weight[:, 3 * n : 3 * n + 1]
-        part = jnp.sum(part, axis=0, keepdims=True)
-        out_ref[:, n * HEAD_WIDTH : (n + 1) * HEAD_WIDTH] = part.astype(jnp.bfloat16)
+        parts.append(jnp.sum(part, axis=0, keepdims=True))
+    out_ref[...] = jnp.concatenate(parts, axis=1).astype(jnp.bfloat16)
 
 
 def call(kernel, out, name, *args, scratch=()):
@@ -327,8 +338,8 @@
     )(keys, values)
     kv = lax.ppermute(kv, ("sx", "sy"), partners)
 
-    pos = full(8, count_x * KEY_HEADS)
-    ask_pos, answer_pos = call(find_kernel, [pos, pos], "find", block_ids.T)
+    rows_heads = count_x * KEY_HEADS
+    ask_pos, answer_pos = call(find_kernel, [full(8, rows_heads), full(rows_heads, 8)], "find", block_ids.T)
     rows = lax.all_gather(rows, "sx", axis=0, axis_index_groups=cores)
     rows = rows.reshape(count_x, KEY_HEADS, FEAT)
     asked = call(
@@ -345,11 +356,12 @@
     side = full(count_z * KEY_HEADS, FEAT + STAT)
     mine, theirs = call(merge_kernel, [side, side], "merge", answer_pos, part)
     pair = lax.all_gather(theirs, "sx", axis=0, axis_index_groups=cores)
-    wide = pltpu.VMEM((count_z * PART_ROWS, HEAD_WIDTH), jnp.float32)
-    stats = pltpu.VMEM((count_z * KEY_HEADS, STAT), jnp.float32)
-    part = call(pair_kernel, half(*wide.shape), "pair", mine, pair, scratch=[wide, stats])
+    flat = (count_z * PART_ROWS, HEAD_WIDTH)
+    wide = pltpu.VMEM(((count_z + 2) * PART_ROWS, HEAD_WIDTH), jnp.float32)
+    stats = pltpu.VMEM(((count_z + 1) * KEY_HEADS, STAT), jnp.float32)
+    part = call(pair_kernel, half(*flat), "pair", mine, pair, scratch=[wide, stats])
     part = exchange(part.reshape(count_z, PART_ROWS // 2, 2, HEAD_WIDTH), "sx", answer_groups)
-    return call(last_kernel, half(1, KEY_HEADS * FEAT), "last", part.reshape(wide.shape), scratch=[wide])
+    return call(last_kernel, half(1, KEY_HEADS * FEAT), "last", part.reshape(flat), scratch=[wide])
 
 
 def solution(mesh):

time: 87.8 us -> 87.8 us (level)
  no operation moved by 1% of the time
where the time goes in v14:
time: 87.8 us; the launch traced here: 87.3 us
  blocking collectives  54.4 us (62%)
  starting transfers between devices  19.6 us (22%)
  Pallas kernels  9.71 us (11%)
  waiting for transfers between devices  2.73 us (3%)
    all_to_all x3, blocking collectives, exchange(): lax.all_to_all(x, axis, split_axis=0, concat_axis=0, tiled=True, axis_ind...  45.1 us
    all_to_all x1, starting transfers between devices, exchange(): lax.all_to_all(x, axis, split_axis=0, concat_axis=0, tiled=True, axis_ind...  16.4 us
    pallas_call x7, Pallas kernels, call(): pl.pallas_call(kernel, out_shape=out, in_specs=[pl.BlockSpec(memory_space...  7.58 us
    all_gather x1, blocking collectives, per_device(): pair = lax.all_gather(theirs, 'sx', axis=0, axis_index_groups=cores)  5.91 us
    all_gather x1, blocking collectives, per_device(): rows = lax.all_gather(rows, 'sx', axis=0, axis_index_groups=cores)  3.41 us
    ppermute x1, starting transfers between devices, per_device(): kv = lax.ppermute(kv, ('sx', 'sy'), partners)  3.2 us
    all_to_all x1, waiting for transfers between devices, exchange(): lax.all_to_all(x, axis, split_axis=0, concat_axis=0, tiled=True, axis_ind...  2.73 us
    pallas_call x1, Pallas kernels, per_device(): pl.pallas_call(relay_kernel, out_shape=half(2 * tokens, width), in_specs=...  2.13 us
  transfers between devices with their start and end apart: 2, of which 1 were waited for; matrix products, arithmetic and copies ran while one was open for 0% of the time, Pallas kernels for 3%

profile of v14, /device:TPU:1, one launch (start us, length us, event | category | flops | bytes accessed | tf_op | source)
XLA Modules:
  0.0 87.3 jit_solution(12495707539086118262)
XLA Ops:
  0.0 0.0 copy-start.3
  0.0 0.7 copy-done.3
  0.7 0.7 copies.1
  1.4 16.4 %all-to-all-start = ((bf16[16,8,512]{2,1,0:T(8,128)(2,1)}), bf16[16,8,512]{2,1,0:T(8,128)(2,1)S(1)}, u32[]{:S(2)}, u32[]{:S(2)}) async-start(bf16[16,8,512]{2,1,0:T(8,128)(2,1)} %copies.1), calls=%async_computation | async-start | bytes 262144 | tf_op jit(solution)/shard_map/all_to_all | solution.py:313
  17.8 0.0 copy-start.2
  17.8 2.1 %relay.1 = bf16[1024,512]{1,0:T(8,128)(2,1)} custom-call(bf16[512,1024]{1,0:T(8,128)(2,1)} %k_ref.3, bf16[512,1024]{1,0:T(8,128)(2,1)} %v_ref.3), custom_call_target="tpu_custom_call" | custom-call | tf_op jit(solution)/shard_map/relay/pallas_call | solution.py:326
  20.0 3.2 %collective-permute-start = (bf16[1024,512]{1,0:T(8,128)(2,1)}, bf16[1024,512]{1,0:T(8,128)(2,1)S(1)}, u32[]{:S(2)}, u32[]{:S(2)}) collective-permute-start(bf16[1024,512]{1,0:T(8,128)(2,1)} %relay.1), channel_id=1, source_target_pairs={{0,1},{1,0},{2,3},{3,2},{4,5},{5,4},{6,7},{7,6},{8,9},{9,8},{10,11... | collective-permute-start | bytes 3145736 | tf_op jit(solution)/shard_map/ppermute | solution.py:339
  23.2 0.0 copy-done.2
  23.2 0.4 find.1
  23.6 0.0 copy-start
  23.6 0.0 copy-start.1
  23.6 2.7 %all-to-all-done = bf16[16,8,512]{2,1,0:T(8,128)(2,1)S(1)} async-done(((bf16[16,8,512]{2,1,0:T(8,128)(2,1)}), bf16[16,8,512]{2,1,0:T(8,128)(2,1)S(1)}, u32[]{:S(2)}, u32[]{:S(2)}) %all-to-all-start) | async-done | bytes 131104 | tf_op jit(solution)/shard_map/all_to_all | solution.py:313
  26.4 3.4 %all-gather.q_ref = bf16[32,8,512]{2,1,0:T(8,128)(2,1)S(1)} all-gather(bf16[16,8,512]{2,1,0:T(8,128)(2,1)S(1)} %all-to-all-done), channel_id=2, replica_groups={{0,16},{32,48},{64,80},{96,112},{128,144},{160,176},{192,208},{224,240}..., dimensions={0}, use_global_device_ids=true | all-gather | bytes 393216 | tf_op jit(solution)/shard_map/all_gather | solution.py:343
  29.8 0.2 select.1
  30.0 15.5 %all_to_all.20.x_ref = bf16[16,8,2048]{2,1,0:T(8,128)(2,1)S(1)} all-to-all(bf16[16,8,2048]{2,1,0:T(8,128)(2,1)S(1)} %select.1), channel_id=1, replica_groups={{10,11,12,13,14,15,0,1,2,3,4,5,6,7,8,9},{26,27,28,29,30,31,16,17,18,19,..., dimensions={0} | all-to-all | bytes 1048576 | tf_op jit(solution)/shard_map/all_to_all | solution.py:313
  45.5 0.0 collective-permute-done.kv_ref
  45.5 0.0 copy-done
  45.5 0.0 copy-done.1
  45.5 3.1 %attend.1 = bf16[16,8,2176]{2,1,0:T(8,128)(2,1)S(1)} custom-call(bf16[16,8,2048]{2,1,0:T(8,128)(2,1)S(1)} %all_to_all.20.x_ref, bf16[512,1024]{1,0:T(8,128)(2,1)S(1)} %copy-done, bf16[512,1024]{1,0:T(8,128)(2,1)S(1)} %copy-done.1, bf16[1024,512]{1,0:T(8,128)(2,1)S(1)} %collective-permute-done.kv_ref), custom_call_target="tpu_custom_call" | custom-call | tf_op jit(solution)/shard_map/attend/pallas_call | solution.py:287
  48.7 11.2 %all_to_all.21.y_ref = bf16[16,8,2176]{2,1,0:T(8,128)(2,1)S(1)} all-to-all(bf16[16,8,2176]{2,1,0:T(8,128)(2,1)S(1)} %attend.1), channel_id=1, replica_groups={{10,11,12,13,14,15,0,1,2,3,4,5,6,7,8,9},{26,27,28,29,30,31,16,17,18,19,..., dimensions={0} | all-to-all | bytes 1114112 | tf_op jit(solution)/shard_map/all_to_all | solution.py:313
  59.8 1.8 %merge.1 = (f32[128,640]{1,0:T(8,128)S(1)}, f32[128,640]{1,0:T(8,128)S(1)}) custom-call(f32[256,8]{1,0:T(8,128)S(1)} %get-tuple-element.9.pos_ref, bf16[16,8,2176]{2,1,0:T(8,128)(2,1)S(1)} %all_to_all.21.y_ref), custom_call_target="tpu_custom_call" | custom-call | tf_op jit(solution)/shard_map/merge/pallas_call | solution.py:287
  61.7 5.9 %all-gather.1 = f32[256,640]{1,0:T(8,128)S(1)} all-gather(f32[128,640]{1,0:T(8,128)S(1)} %get-tuple-element.12), channel_id=3, replica_groups={{0,16},{32,48},{64,80},{96,112},{128,144},{160,176},{192,208},{224,240}..., dimensions={0}, use_global_device_ids=true | all-gather | bytes 983040 | tf_op jit(solution)/shard_map/all_gather | solution.py:358
  67.6 0.4 pair.1
  68.0 18.4 %all_to_all.22 = bf16[16,17,2,128]{3,2,1,0:T(2,128)(2,1)S(1)} all-to-all(bf16[16,17,2,128]{3,2,1,0:T(2,128)(2,1)S(1)} %bitcast.5), channel_id=1, replica_groups={{256,288,320,352,384,416,448,480,0,32,64,96,128,160,192,224},{272,304,3..., dimensions={0} | all-to-all | bytes 278528 | tf_op jit(solution)/shard_map/all_to_all | solution.py:313
  86.4 0.9 %last.1 = bf16[1,4096]{1,0:T(2,128)(2,1)} custom-call(bf16[544,128]{1,0:T(8,128)(2,1)S(1)} %bitcast.6), custom_call_target="tpu_custom_call" | custom-call | tf_op jit(solution)/shard_map/last/pallas_call | solution.py:287
Async XLA Ops:
  0.0 0.7 copy-start.3
  1.4 25.0 %all-to-all-start = ((bf16[16,8,512]{2,1,0:T(8,128)(2,1)}), bf16[16,8,512]{2,1,0:T(8,128)(2,1)S(1)}, u32[]{:S(2)}, u32[]{:S(2)}) async-start(bf16[16,8,512]{2,1,0:T(8,128)(2,1)} %copies.1), calls=%async_computation | async-start | bytes 262144 | tf_op jit(solution)/shard_map/all_to_all | solution.py:313
  17.8 5.4 %copy-start.2 = (s32[512,16]{0,1:T(8,128)S(1)}, s32[512,16]{0,1:T(8,128)}, u32[]{:S(2)}) copy-start(s32[512,16]{0,1:T(8,128)} %param.7) | copy-start | bytes 98308
  20.0 25.6 %collective-permute-start = (bf16[1024,512]{1,0:T(8,128)(2,1)}, bf16[1024,512]{1,0:T(8,128)(2,1)S(1)}, u32[]{:S(2)}, u32[]{:S(2)}) collective-permute-start(bf16[1024,512]{1,0:T(8,128)(2,1)} %relay.1), channel_id=1, source_target_pairs={{0,1},{1,0},{2,3},{3,2},{4,5},{5,4},{6,7},{7,6},{8,9},{9,8},{10,11... | collective-permute-start | bytes 3145736 | tf_op jit(solution)/shard_map/ppermute | solution.py:339
  23.6 21.9 %copy-start = (bf16[512,1024]{1,0:T(8,128)(2,1)S(1)}, bf16[512,1024]{1,0:T(8,128)(2,1)}, u32[]{:S(2)}) copy-start(bf16[512,1024]{1,0:T(8,128)(2,1)} %k_ref.3) | copy-start | bytes 3145732
  23.6 21.9 %copy-start.1 = (bf16[512,1024]{1,0:T(8,128)(2,1)S(1)}, bf16[512,1024]{1,0:T(8,128)(2,1)}, u32[]{:S(2)}) copy-start(bf16[512,1024]{1,0:T(8,128)(2,1)} %v_ref.3) | copy-start | bytes 3145732
